TPU v7x, 256 devices: a whole 4x4x8 slice. The times are simulated.
256 devices in a mesh: seq: 32 (over x, y, core), exp: 8 (over z).
Axes of the slice: x: 4, y: 4, z: 8, core: 2. Of those that a mesh axis runs over, the one named last changes fastest.
Arguments:
- residual_in: bfloat16 [4096, 4096], P('seq', 'exp'), may hold values from -12 to 12
- queries: bfloat16 [4096, 2048], P('seq', 'exp'), may hold values from -5.5 to 5.5
- key_heads: bfloat16 [4096, 1024], P('seq', 'exp'), may hold values from -5.5 to 5.5
- value_heads: bfloat16 [4096, 1024], P('seq', 'exp'), may hold values from -6 to 6
- out_proj: bfloat16 [2048, 4096], P('exp'), may hold values from -0.25 to 0.25
- norm_gain: float32 [4096], replicated, may hold values from 0.25 to 1.75
- expert_ids: int32 [4096, 8], P('seq'), may hold values from 0 to 63, all different within a row; in each aligned block of 128 rows (0 to 127, 128 to 255, ...) at most 32 rows name the same one
- route_weights: bfloat16 [4096, 8], P('seq'), may hold values from 0.049804688 to 0.29882812
- changed: int32 [4096], P('seq'), may hold values 0 or 1
- cached_moe: bfloat16 [4096, 4096], P('seq', 'exp'), may hold values from -3 to 3
- gate_proj: bfloat16 [256, 4096, 384], P(('exp', 'seq')), may hold values from -0.09375 to 0.09375
- up_proj: bfloat16 [256, 4096, 384], P(('exp', 'seq')), may hold values from -0.09375 to 0.09375
- down_proj: bfloat16 [256, 384, 4096], P(('exp', 'seq')), may hold values from -0.15625 to 0.15625
Outputs:
- layer_out: bfloat16 [4096, 4096], P('seq', 'exp')
Inputs may be any that keep to these rules, and one draw needn't show every extreme that they name: `expert_ids`: each row names 8 different experts. Among the 128 rows of one index of seq no expert is named by more than 32 rows, a bound that some block reaches.
All inputs are finite; a program needn't handle non-finite values. No bound on the sum of `changed` on one device may be relied on, other than what follows from the above.
Results may differ from a plain program's by a relative error of at most 0.014.
Values may be sent and summed in bfloat16 or wider, within the bound.
No kernel may reach another device: no remote copies, remote signals or barrier semaphores. Data moves between devices by JAX's collectives and lax.ppermute only.
A program may use at most 128 MiB of HBM per device.

v0:
```python
import jax
import jax.numpy as jnp
from jax import lax
from jax.sharding import PartitionSpec as P

HD = 128
TOP = 8
EXP_GROUP = 8


def expert_partial(arrived, gate_proj, up_proj, down_proj):
    model_width = arrived.shape[-1]
    flat_rows = arrived.reshape(-1, model_width)
    gate_out = jnp.dot(flat_rows, gate_proj[0], preferred_element_type=jnp.float32)
    up_out = jnp.dot(flat_rows, up_proj[0], preferred_element_type=jnp.float32)
    hidden = (jax.nn.silu(gate_out) * up_out).astype(jnp.bfloat16)
    partial_out = jnp.dot(hidden, down_proj[0], preferred_element_type=jnp.float32).astype(
        jnp.bfloat16
    )
    return partial_out.reshape(arrived.shape)


def shards(
    residual_in,
    queries,
    key_heads,
    value_heads,
    out_proj,
    norm_gain,
    expert_ids,
    route_weights,
    changed,
    cached_moe,
    gate_proj,
    up_proj,
    down_proj,
):
    seq_count = lax.axis_size("seq")
    exp_count = lax.axis_size("exp")
    group_index = lax.axis_index("exp")
    local_tokens = queries.shape[0]
    kv_local = key_heads.shape[1] // HD
    group_size = queries.shape[1] // HD // kv_local
    all_keys, all_values = (
        lax.all_gather(key_heads, "seq", axis=0, tiled=True),
        lax.all_gather(value_heads, "seq", axis=0, tiled=True),
    )
    query_split = queries.reshape(local_tokens, kv_local, group_size, HD)
    key_split = all_keys.reshape(-1, kv_local, HD)
    value_split = all_values.reshape(-1, kv_local, HD)
    scores = jnp.einsum(
        "tkgd,skd->kgts", query_split, key_split, preferred_element_type=jnp.float32
    ) * HD ** (-0.5)
    attn_probs = jax.nn.softmax(scores, axis=-1).astype(jnp.bfloat16)
    attended = jnp.einsum(
        "kgts,skd->tkgd", attn_probs, value_split, preferred_element_type=jnp.float32
    ).astype(jnp.bfloat16)
    attended = attended.reshape(local_tokens, -1)
    partial_attn = jnp.dot(attended, out_proj, preferred_element_type=jnp.float32)
    attn_share = lax.psum_scatter(
        partial_attn.astype(jnp.bfloat16), "exp", scatter_dimension=1, tiled=True
    ).astype(jnp.float32)
    mixed_local = (residual_in.astype(jnp.float32) + attn_share).astype(jnp.bfloat16)
    mixed_full = lax.all_gather(mixed_local, "exp", axis=1, tiled=True)
    mixed_float = mixed_full.astype(jnp.float32)
    mean_square = jnp.mean(mixed_float * mixed_float, axis=-1, keepdims=True)
    normed = (mixed_float * lax.rsqrt(mean_square + 1e-06) * norm_gain).astype(jnp.bfloat16)
    capacity = 2 * local_tokens * TOP // (EXP_GROUP * exp_count)
    splits = seq_count // EXP_GROUP
    local_experts = jnp.arange(EXP_GROUP, dtype=jnp.int32) + group_index * EXP_GROUP
    matches = expert_ids[:, :, None] == local_experts[None, None, :]
    member = jnp.any(matches, axis=1)
    token_weight = jnp.sum(
        jnp.where(matches, route_weights[:, :, None], jnp.zeros((), jnp.bfloat16)), axis=1
    )
    rank = jnp.cumsum(member.astype(jnp.int32), axis=0) - 1
    live_rows = member & (changed[:, None] == 1)
    slot_range = jnp.arange(capacity, dtype=jnp.int32)
    select_hit = live_rows.T[:, None, :] & (rank.T[:, None, :] == slot_range[None, :, None])
    selector = select_hit.astype(jnp.bfloat16)
    outgoing = jnp.einsum(
        "jct,td->jcd", selector, normed, preferred_element_type=jnp.float32
    ).astype(jnp.bfloat16)
    spread = jnp.repeat(outgoing, splits, axis=0)
    partial_out = expert_partial(
        lax.all_to_all(spread, "seq", split_axis=0, concat_axis=0, tiled=True),
        gate_proj,
        up_proj,
        down_proj,
    )
    returned = lax.all_to_all(partial_out, "seq", split_axis=0, concat_axis=0, tiled=True)
    expert_out = jnp.sum(
        returned.reshape(EXP_GROUP, splits, capacity, -1), axis=1, dtype=jnp.float32
    ).astype(jnp.bfloat16)
    weighted_select = selector * token_weight.T[:, None, :]
    combined = jnp.einsum(
        "jct,jcd->td", weighted_select, expert_out, preferred_element_type=jnp.float32
    )
    moe_share = lax.psum_scatter(
        combined.astype(jnp.bfloat16), "exp", scatter_dimension=1, tiled=True
    ).astype(jnp.float32)
    moe_value = jnp.where(changed[:, None] == 1, moe_share, cached_moe.astype(jnp.float32))
    return (mixed_local.astype(jnp.float32) + moe_value).astype(jnp.bfloat16)


def solution(mesh):
    in_specs = (
        P("seq", "exp"),
        P("seq", "exp"),
        P("seq", "exp"),
        P("seq", "exp"),
        P("exp", None),
        P(),
        P("seq", None),
        P("seq", None),
        P("seq"),
        P("seq", "exp"),
        P(("exp", "seq"), None, None),
        P(("exp", "seq"), None, None),
        P(("exp", "seq"), None, None),
    )
    out_specs = P("seq", "exp")
    return jax.shard_map(shards, mesh=mesh, in_specs=in_specs, out_specs=out_specs, check_vma=False)
```

profile of v0, /device:TPU:6, one launch (start us, length us, event | category | flops | bytes accessed | tf_op | source)
XLA Modules:
  0.0 496.2 jit_solution(6352796981562242021)
XLA Ops:
  6.5 0.7 all-gather.4.cloned.1.call-update
  7.3 1.6 copy.22
  9.0 51.3 %all-gather.4.cloned.1.call-done = bf16[4096,128]{1,0:T(8,128)(2,1)} async-done(((bf16[128,128]{1,0:T(8,128)(2,1)}), bf16[4096,128]{1,0:T(8,128)(2,1)}) %all-gather.4.cloned.1.call-update) | async-done | bytes 1048592 | tf_op jit(solution)/shard_map/all_gather | solution.py:45
  60.3 2.1 fusion.38
  62.4 1.9 copy-done.1
  64.9 45.3 %all-gather.6.cloned.1.call-done = bf16[4096,128]{0,1:T(8,128)(2,1)} async-done(((bf16[128,128]{0,1:T(8,128)(2,1)}), bf16[4096,128]{0,1:T(8,128)(2,1)}) %all-gather.6.cloned.1.call-update) | async-done | bytes 1048592 | tf_op jit(solution)/shard_map/all_gather | solution.py:46
  110.2 3.5 fusion.15
  113.7 1.4 convolution_convert_fusion.2
  115.2 38.5 %reduce-scatter.3.cloned.1.call-done = bf16[128,512]{1,0:T(8,128)(2,1)} async-done(((bf16[128,4096]{1,0:T(8,128)(2,1)}), bf16[128,512]{1,0:T(8,128)(2,1)}) %reduce-scatter.3.cloned.1.call-update) | async-done | bytes 131088 | tf_op jit(solution)/shard_map/reduce_scatter | solution.py:60
  153.7 1.6 add_convert_fusion.1
  155.8 37.2 %all-gather.8.cloned.1.call-done = bf16[128,4096]{1,0:T(8,128)(2,1)} async-done(((bf16[128,512]{1,0:T(8,128)(2,1)}), bf16[128,4096]{1,0:T(8,128)(2,1)}) %all-gather.8.cloned.1.call-update) | async-done | bytes 1048592 | tf_op jit(solution)/shard_map/all_gather | solution.py:64
  193.0 1.5 fusion.8
  194.5 2.0 convolution_convert_fusion.1
  196.6 1.0 broadcast_in_dim.22
  197.6 101.4 %all_to_all.10 = bf16[32,32,4096]{2,1,0:T(8,128)(2,1)S(1)} all-to-all(bf16[32,32,4096]{2,1,0:T(8,128)(2,1)S(1)} %bitcast.67), channel_id=1, replica_groups=mesh['seq'=32,'exp'=8] {'seq'}, dimensions={0} | all-to-all | bytes 16777216 | tf_op jit(solution)/shard_map/all_to_all | solution.py:86
  299.1 4.5 fusion.6
  303.6 4.6 multiply_convert_fusion
  308.2 6.7 %convolution_convert_fusion = bf16[1024,4096]{1,0:T(8,128)(2,1)} fusion(bf16[1024,384]{1,0:T(8,128)(2,1)S(1)} %multiply_convert_fusion, bf16[1,384,4096]{2,1,0:T(8,128)(2,1)S(1)} %copy-done), kind=kOutput, calls=%fused_computation.1 | convolution fusion | flops 3225419776 | bytes 12320768 | tf_op jit(solution)/shard_map/dot_general | solution.py:17
  314.9 6.6 %all-to-all-start.1 = ((bf16[32,32,4096]{2,1,0:T(8,128)(2,1)}), bf16[32,32,4096]{2,1,0:T(8,128)(2,1)}, u32[]{:S(2)}, u32[]{:S(2)}) async-start(bf16[32,32,4096]{2,1,0:T(8,128)(2,1)} %bitcast.68), calls=%async_computation.2 | async-start | bytes 16777216 | tf_op jit(solution)/shard_map/all_to_all | solution.py:91
  321.6 103.5 %all-to-all-done.1 = bf16[32,32,4096]{2,1,0:T(8,128)(2,1)} async-done(((bf16[32,32,4096]{2,1,0:T(8,128)(2,1)}), bf16[32,32,4096]{2,1,0:T(8,128)(2,1)}, u32[]{:S(2)}, u32[]{:S(2)}) %all-to-all-start.1) | async-done | bytes 8388640 | tf_op jit(solution)/shard_map/all_to_all | solution.py:91
  425.1 5.1 %bitcast_reduce_fusion = bf16[8,32,4096]{2,1,0:T(8,128)(2,1)S(1)} fusion(bf16[32,32,4096]{2,1,0:T(8,128)(2,1)} %all-to-all-done.1), kind=kLoop, calls=%fused_computation | loop fusion | flops 3145728 | bytes 10485760 | tf_op jit(solution)/shard_map/reduce_sum | solution.py:92
  430.3 1.5 fusion.1
  431.7 56.2 %reduce-scatter.5.cloned.1.call-done = bf16[128,512]{1,0:T(8,128)(2,1)} async-done(((bf16[128,4096]{1,0:T(8,128)(2,1)}), bf16[128,512]{1,0:T(8,128)(2,1)}) %reduce-scatter.5.cloned.1.call-update) | async-done | bytes 131088 | tf_op jit(solution)/shard_map/reduce_scatter | solution.py:99
  488.0 1.7 add_convert_fusion
  (43 shorter events, 1.4 us)
Async XLA Ops:
  6.5 301.6 %copy-start = (bf16[1,384,4096]{2,1,0:T(8,128)(2,1)S(1)}, bf16[1,384,4096]{2,1,0:T(8,128)(2,1)}, u32[]{:S(2)}) copy-start(bf16[1,384,4096]{2,1,0:T(8,128)(2,1)} %param.25) | copy-start | bytes 9437188
  6.5 53.8 %all-gather.4.cloned.1.call-start = ((), (), s32[]{:S(2)}) async-start(), calls=%async_computation.4 | async-start | bytes 1081344 | tf_op jit(solution)/shard_map/all_gather | solution.py:45
  7.3 102.9 %all-gather.6.cloned.1.call-start = ((), (), s32[]{:S(2)}) async-start(), calls=%async_computation.5 | async-start | bytes 1081344 | tf_op jit(solution)/shard_map/all_gather | solution.py:46
  9.0 144.8 %reduce-scatter.3.cloned.1.call-start = ((), (), s32[]{:S(2)}) async-start(), calls=%async_computation.6 | async-start | bytes 1179648 | tf_op jit(solution)/shard_map/reduce_scatter | solution.py:60
  62.4 1.9 copy-start.1
  110.2 3.5 copy-start.2
  113.7 40.1 %copy-start.4 = (bf16[128,512]{1,0:T(8,128)(2,1)S(1)}, bf16[128,512]{1,0:T(8,128)(2,1)}, u32[]{:S(2)}) copy-start(bf16[128,512]{1,0:T(8,128)(2,1)} %param.13) | copy-start | bytes 393220
  113.7 41.7 %copy-start.7 = (s32[128,8]{0,1:T(8,128)S(1)}, s32[128,8]{0,1:T(8,128)}, u32[]{:S(2)}) copy-start(s32[128,8]{0,1:T(8,128)} %param.19) | copy-start | bytes 12292
  113.7 41.8 %copy-start.11 = (s32[128]{0:T(128)S(1)}, s32[128]{0:T(128)}, u32[]{:S(2)}) copy-start(s32[128]{0:T(128)} %param.21) | copy-start | bytes 1540
  113.7 80.8 %copy-start.6 = (f32[4096]{0:T(1024)S(1)}, f32[4096]{0:T(1024)}, u32[]{:S(2)}) copy-start(f32[4096]{0:T(1024)} %param.18) | copy-start | bytes 49156
  115.2 77.8 %all-gather.8.cloned.1.call-start = ((), (), s32[]{:S(2)}) async-start(), calls=%async_computation.7 | async-start | bytes 1179648 | tf_op jit(solution)/shard_map/all_gather | solution.py:64
  197.6 101.4 %copy-start.9 = (bf16[1,4096,384]{2,1,0:T(8,128)(2,1)S(1)}, bf16[1,4096,384]{2,1,0:T(8,128)(2,1)}, u32[]{:S(2)}) copy-start(bf16[1,4096,384]{2,1,0:T(8,128)(2,1)} %param.23) | copy-start | bytes 9437188
  299.1 4.5 copy-start.10
  314.9 6.6 %copy-start.8 = (bf16[128,8]{0,1:T(8,128)(2,1)S(1)}, bf16[128,8]{0,1:T(8,128)(2,1)}, u32[]{:S(2)}) copy-start(bf16[128,8]{0,1:T(8,128)(2,1)} %param.20) | copy-start | bytes 6148
  314.9 110.2 %all-to-all-start.1 = ((bf16[32,32,4096]{2,1,0:T(8,128)(2,1)}), bf16[32,32,4096]{2,1,0:T(8,128)(2,1)}, u32[]{:S(2)}, u32[]{:S(2)}) async-start(bf16[32,32,4096]{2,1,0:T(8,128)(2,1)} %bitcast.68), calls=%async_computation.2 | async-start | bytes 16777216 | tf_op jit(solution)/shard_map/all_to_all | solution.py:91
  321.5 166.5 %reduce-scatter.5.cloned.1.call-start = ((), (), s32[]{:S(2)}) async-start(), calls=%async_computation.8 | async-start | bytes 1179648 | tf_op jit(solution)/shard_map/reduce_scatter | solution.py:99
  430.2 57.7 %copy-start.3 = (bf16[128,512]{1,0:T(8,128)(2,1)S(1)}, bf16[128,512]{1,0:T(8,128)(2,1)}, u32[]{:S(2)}) copy-start(bf16[128,512]{1,0:T(8,128)(2,1)} %add_convert_fusion.1) | copy-start | bytes 393220
  430.3 57.7 %copy-start.5 = (bf16[128,512]{1,0:T(8,128)(2,1)S(1)}, bf16[128,512]{1,0:T(8,128)(2,1)}, u32[]{:S(2)}) copy-start(bf16[128,512]{1,0:T(8,128)(2,1)} %param.22) | copy-start | bytes 393220
Sparse Core Ops, SparseCore 0:
  9.9 50.3 all-gather.3
  62.8 47.3 all-gather.5
  115.3 38.3 reduce-scatter.2
  155.5 37.4 all-gather.7
  431.9 56.0 reduce-scatter.4
where the time goes:
time: 497 us; the launch traced here: 496 us
  waiting for transfers between devices  333 us (67%)
  blocking collectives  101 us (20%)
  matrix products  26.3 us (5%)
  between operations  13.3 us (3%)
  other arithmetic  10.8 us (2%)
  starting transfers between devices  6.72 us (1%)
    all_to_all x1, waiting for transfers between devices, shards(): lax.all_to_all(partial_out, 'seq', split_axis=0, concat_axis=0, tiled=True)  104 us
    all_to_all x1, blocking collectives, shards(): lax.all_to_all(spread, 'seq', split_axis=0, concat_axis=0, tiled=True)  101 us
    reduce_scatter x1, waiting for transfers between devices, shards(): lax.psum_scatter(combined.astype(jnp.bfloat16), 'exp', scatter_dimension=...  56.2 us
    all_gather x1, waiting for transfers between devices, shards(): lax.all_gather(key_heads, 'seq', axis=0, tiled=True)  51.3 us
    all_gather x1, waiting for transfers between devices, shards(): lax.all_gather(value_heads, 'seq', axis=0, tiled=True)  45.3 us
    reduce_scatter x1, waiting for transfers between devices, shards(): lax.psum_scatter(partial_attn.astype(jnp.bfloat16), 'exp', scatter_dimens...  38.5 us
    all_gather x1, waiting for transfers between devices, shards(): mixed_full = lax.all_gather(mixed_local, 'exp', axis=1, tiled=True)  37.2 us
  transfers between devices with their start and end apart: 6, of which 6 were waited for; matrix products, arithmetic and copies ran while one was open for 1% of the time, Pallas kernels for 0%

commit v1 on v0

v1 whole, which is shorter than its diff:
```python
import jax
import jax.numpy as jnp
from jax import lax
from jax.sharding import Mesh, PartitionSpec as P

HD = 128
TOP = 8
EXP_GROUP = 8
BF = jnp.bfloat16
F32 = jnp.float32


def swap_cores(array):
    return lax.ppermute(array, "c", [(0, 1), (1, 0)])


def gather_by_exchange(array, axes, count):
    spread = jnp.broadcast_to(array[None], (count,) + array.shape)
    return lax.all_to_all(spread, axes, split_axis=0, concat_axis=0, tiled=True)


def attention(queries, all_kv, kv_local):
    tokens = queries.shape[0]
    group_size = queries.shape[1] // HD // kv_local
    width = kv_local * HD
    query_split = queries.reshape(tokens, kv_local, group_size, HD)
    key_split = all_kv[:, :width].reshape(-1, kv_local, HD)
    value_split = all_kv[:, width:].reshape(-1, kv_local, HD)
    scores = jnp.einsum(
        "tkgd,skd->kgts", query_split, key_split, preferred_element_type=F32
    ) * HD ** (-0.5)
    attn_probs = jax.nn.softmax(scores, axis=-1).astype(BF)
    attended = jnp.einsum(
        "kgts,skd->tkgd", attn_probs, value_split, preferred_element_type=F32
    ).astype(BF)
    return attended.reshape(tokens, -1)


def shards(
    residual_in,
    queries,
    key_heads,
    value_heads,
    out_proj,
    norm_gain,
    expert_ids,
    route_weights,
    changed,
    cached_moe,
    gate_proj,
    up_proj,
    down_proj,
):
    plane = lax.axis_size("x") * lax.axis_size("y")
    depth = lax.axis_size("z")
    group_index = lax.axis_index("z")
    core = lax.axis_index("c")
    tokens = queries.shape[0]
    slice_width = residual_in.shape[1]

    own_kv = gather_by_exchange(
        jnp.concatenate([key_heads, value_heads], axis=1), ("x", "y"), plane
    )
    all_kv = jnp.concatenate([own_kv, swap_cores(own_kv)], axis=0)
    all_kv = all_kv.reshape(-1, all_kv.shape[-1])

    half_rows = out_proj.shape[0] // 2
    out_half = lax.dynamic_slice_in_dim(out_proj, core * half_rows, half_rows, 0)
    out_own = lax.all_to_all(
        out_half.reshape(half_rows, depth, slice_width).transpose(1, 0, 2),
        "z", split_axis=0, concat_axis=0, tiled=True,
    )
    out_cols = jnp.concatenate([out_own, swap_cores(out_own)], axis=1)
    out_cols = out_cols.reshape(-1, slice_width)

    gate_other, up_other, down_other = (
        swap_cores(gate_proj[0]),
        swap_cores(up_proj[0]),
        swap_cores(down_proj[0]),
    )

    attended = attention(queries, all_kv, key_heads.shape[1] // HD)
    first, second = attended[:, :half_rows], attended[:, half_rows:]
    attended = jnp.where(
        core == 0,
        attended,
        jnp.concatenate([second, first], axis=1),
    )
    attended_all = gather_by_exchange(attended, "z", depth)
    attended_all = attended_all.transpose(1, 0, 2).reshape(tokens, -1)
    attn_share = jnp.dot(attended_all, out_cols, preferred_element_type=F32)
    mixed_local = (residual_in.astype(F32) + attn_share).astype(BF)

    mixed_full = gather_by_exchange(mixed_local, "z", depth)
    mixed_full = mixed_full.transpose(1, 0, 2).reshape(tokens, -1)
    mixed_float = mixed_full.astype(F32)
    mean_square = jnp.mean(mixed_float * mixed_float, axis=-1, keepdims=True)
    normed = (mixed_float * lax.rsqrt(mean_square + 1e-06) * norm_gain).astype(BF)

    capacity = 2 * tokens * TOP // (EXP_GROUP * depth)
    copies = plane // EXP_GROUP
    local_experts = jnp.arange(EXP_GROUP, dtype=jnp.int32) + group_index * EXP_GROUP
    matches = expert_ids[:, :, None] == local_experts[None, None, :]
    member = jnp.any(matches, axis=1)
    token_weight = jnp.sum(
        jnp.where(matches, route_weights[:, :, None], jnp.zeros((), BF)), axis=1
    )
    rank = jnp.cumsum(member.astype(jnp.int32), axis=0) - 1
    live_rows = member & (changed[:, None] == 1)
    slot_range = jnp.arange(capacity, dtype=jnp.int32)
    select_hit = live_rows.T[:, None, :] & (rank.T[:, None, :] == slot_range[None, :, None])
    selector = select_hit.astype(BF)
    weighted_select = selector * token_weight.T[:, None, :]
    selector = jnp.repeat(selector, copies, axis=0)
    weighted_select = jnp.repeat(weighted_select, copies, axis=0)

    outgoing = jnp.einsum(
        "jct,td->jcd", selector, normed, preferred_element_type=F32
    ).astype(BF)
    arrived = lax.all_to_all(outgoing, ("x", "y"), split_axis=0, concat_axis=0, tiled=True)
    rows = arrived.reshape(-1, arrived.shape[-1])

    def hidden_of(gate, up):
        gate_out = jnp.dot(rows, gate, preferred_element_type=F32)
        up_out = jnp.dot(rows, up, preferred_element_type=F32)
        return (jax.nn.silu(gate_out) * up_out).astype(BF)

    hidden_own = hidden_of(gate_proj[0], up_proj[0])
    hidden_other = hidden_of(gate_other, up_other)
    partial_out = (
        jnp.dot(hidden_own, down_proj[0], preferred_element_type=F32)
        + jnp.dot(hidden_other, down_other, preferred_element_type=F32)
    ).astype(BF)
    returned = lax.all_to_all(
        partial_out.reshape(arrived.shape), ("x", "y"), split_axis=0, concat_axis=0, tiled=True
    )
    combined = jnp.einsum(
        "jct,jcd->td", weighted_select, returned, preferred_element_type=F32
    ).astype(BF)
    shares = lax.all_to_all(
        combined.reshape(tokens, depth, slice_width).transpose(1, 0, 2),
        "z", split_axis=0, concat_axis=0, tiled=True,
    )
    moe_share = jnp.sum(shares.astype(F32), axis=0)
    moe_value = jnp.where(changed[:, None] == 1, moe_share, cached_moe.astype(F32))
    return (mixed_local.astype(F32) + moe_value).astype(BF)


def solution(mesh):
    cores = 2
    side = int(round((mesh.shape["seq"] // cores) ** 0.5))
    split_mesh = Mesh(
        mesh.devices.reshape(side, side, cores, mesh.shape["exp"]), ("x", "y", "c", "z")
    )
    seq = ("x", "y", "c")
    in_specs = (
        P(seq, "z"),
        P(seq, "z"),
        P(seq, "z"),
        P(seq, "z"),
        P("z", None),
        P(),
        P(seq, None),
        P(seq, None),
        P(seq),
        P(seq, "z"),
        P(("z",) + seq, None, None),
        P(("z",) + seq, None, None),
        P(("z",) + seq, None, None),
    )
    return jax.shard_map(
        shards, mesh=split_mesh, in_specs=in_specs, out_specs=P(seq, "z"), check_vma=False
    )
```

time: 497 us -> 329 us (0.66)
  waiting for transfers between devices: 333 us -> 202 us
  blocking collectives: 101 us -> 28.3 us
  starting transfers between devices: 6.72 us -> 38.6 us
  matrix products: 26.3 us -> 44.1 us
  between operations: 13.3 us -> 0.31 us
    all_gather x3 -> x0, waiting for transfers between devices: 134 us -> none  [the longest x1 51.3 us: shards(): lax.all_gather(key_heads, 'seq', axis=0, tiled=True)]
    all_to_all x1 -> x6, waiting for transfers between devices: 104 us -> 202 us  [the longest x1 61 us: shards(): lax.all_to_all(outgoing, ('x', 'y'), split_axis=0, concat_axis=0, tiled=T...]
    reduce_scatter x2 -> x0, waiting for transfers between devices: 94.7 us -> none  [the longest x1 56.2 us: shards(): lax.psum_scatter(combined.astype(jnp.bfloat16), 'exp', scatter_dimension=...]
    all_to_all x1, blocking collectives: 101 us -> 28.3 us  [shards(): lax.all_to_all(combined.reshape(tokens, depth, slice_width).transpose(1,...]
    all_to_all x1 -> x6, starting transfers between devices: 6.56 us -> 38 us  [the longest x3 14.5 us: gather_by_exchange(): return lax.all_to_all(spread, axes, split_axis=0, concat_axis=0, tiled=True)]
    dot_general x8 -> x9, matrix products: 26.3 us -> 44.1 us  [the longest x1 12.9 us: shards(): jnp.dot(hidden_other, down_other, preferred_element_type=F32)]
  transfers between devices with their start and end apart: 6 -> 11, of which waited for: 6 -> 6; matrix products, arithmetic and copies ran while one was open for 1% -> 9% of each run, Pallas kernels for 0% -> 0%
where the time goes in v1:
time: 329 us; the launch traced here: 326 us
  waiting for transfers between devices  202 us (61%)
  matrix products  44.1 us (13%)
  starting transfers between devices  38.6 us (12%)
  blocking collectives  28.3 us (9%)
  local copies, waits for them, and re-layouts  6.16 us (2%)
  other arithmetic  5.88 us (2%)
    all_to_all x1, waiting for transfers between devices, shards(): lax.all_to_all(outgoing, ('x', 'y'), split_axis=0, concat_axis=0, tiled=T...  61 us
    all_to_all x3, waiting for transfers between devices, gather_by_exchange(): return lax.all_to_all(spread, axes, split_axis=0, concat_axis=0, tiled=True)  60.3 us
    all_to_all x1, waiting for transfers between devices, shards(): lax.all_to_all(partial_out.reshape(arrived.shape), ('x', 'y'), split_axis...  54.2 us
    all_to_all x1, blocking collectives, shards(): lax.all_to_all(combined.reshape(tokens, depth, slice_width).transpose(1,...  28.3 us
    all_to_all x1, waiting for transfers between devices, shards(): lax.all_to_all(out_half.reshape(half_rows, depth, slice_width).transpose(...  27 us
    all_to_all x3, starting transfers between devices, gather_by_exchange(): return lax.all_to_all(spread, axes, split_axis=0, concat_axis=0, tiled=True)  14.5 us
    dot_general x1, matrix products, shards(): jnp.dot(hidden_other, down_other, preferred_element_type=F32)  12.9 us
    dot_general x1, matrix products, shards(): jnp.dot(hidden_own, down_proj[0], preferred_element_type=F32)  11.8 us
  transfers between devices with their start and end apart: 11, of which 6 were waited for; matrix products, arithmetic and copies ran while one was open for 9% of the time, Pallas kernels for 0%

profile of v1, /device:TPU:6, one launch (start us, length us, event | category | flops | bytes accessed | tf_op | source)
XLA Modules:
  0.0 325.9 jit_solution(16736752038880987012)
XLA Ops:
  0.0 0.9 pad_maximum_fusion.1
  0.9 1.1 broadcast_in_dim.27
  2.0 7.4 %all-to-all-start = ((bf16[16,128,256]{2,1,0:T(8,128)(2,1)}), bf16[16,128,256]{2,1,0:T(8,128)(2,1)}, u32[]{:S(2)}, u32[]{:S(2)}) async-start(bf16[16,128,256]{2,1,0:T(8,128)(2,1)} %broadcast_in_dim.27), calls=%async_computation | async-start | bytes 2097152 | tf_op jit(solution)/shard_map/all_to_all | solution.py:19
  10.2 1.3 copy.61
  11.5 13.2 %all-to-all-done = bf16[16,128,256]{2,1,0:T(8,128)(2,1)} async-done(((bf16[16,128,256]{2,1,0:T(8,128)(2,1)}), bf16[16,128,256]{2,1,0:T(8,128)(2,1)}, u32[]{:S(2)}, u32[]{:S(2)}) %all-to-all-start) | async-done | bytes 1048608 | tf_op jit(solution)/shard_map/all_to_all | solution.py:19
  24.8 8.6 %all-to-all-start.2 = ((bf16[8,128,512]{2,1,0:T(8,128)(2,1)}), bf16[8,128,512]{2,1,0:T(8,128)(2,1)S(1)}, u32[]{:S(2)}, u32[]{:S(2)}) async-start(bf16[8,128,512]{2,1,0:T(8,128)(2,1)} %bitcast.14), calls=%async_computation.2 | async-start | bytes 2097152 | tf_op jit(solution)/shard_map/all_to_all | solution.py:69
  33.4 27.0 %all-to-all-done.2 = bf16[8,128,512]{2,1,0:T(8,128)(2,1)S(1)} async-done(((bf16[8,128,512]{2,1,0:T(8,128)(2,1)}), bf16[8,128,512]{2,1,0:T(8,128)(2,1)S(1)}, u32[]{:S(2)}, u32[]{:S(2)}) %all-to-all-start.2) | async-done | bytes 1048608 | tf_op jit(solution)/shard_map/all_to_all | solution.py:69
  60.4 1.7 pad_maximum_fusion
  65.5 3.5 %all-to-all-start.1 = ((bf16[8,128,256]{2,1,0:T(8,128)(2,1)}), bf16[8,128,256]{2,1,0:T(8,128)(2,1)S(1)}, u32[]{:S(2)}, u32[]{:S(2)}) async-start(bf16[8,128,256]{2,1,0:T(8,128)(2,1)} %broadcast_in_dim.28), calls=%async_computation.1 | async-start | bytes 1048576 | tf_op jit(solution)/shard_map/all_to_all | solution.py:19
  69.1 18.4 %all-to-all-done.1 = bf16[8,128,256]{2,1,0:T(8,128)(2,1)S(1)} async-done(((bf16[8,128,256]{2,1,0:T(8,128)(2,1)}), bf16[8,128,256]{2,1,0:T(8,128)(2,1)S(1)}, u32[]{:S(2)}, u32[]{:S(2)}) %all-to-all-start.1) | async-done | bytes 524320 | tf_op jit(solution)/shard_map/all_to_all | solution.py:19
  87.9 1.1 broadcast_in_dim.34
  89.0 3.6 %all-to-all-start.3 = ((bf16[8,128,512]{2,1,0:T(8,128)(2,1)}), bf16[8,128,512]{2,1,0:T(8,128)(2,1)S(1)}, u32[]{:S(2)}, u32[]{:S(2)}) async-start(bf16[8,128,512]{2,1,0:T(8,128)(2,1)} %broadcast_in_dim.34), calls=%async_computation.3 | async-start | bytes 2097152 | tf_op jit(solution)/shard_map/all_to_all | solution.py:19
  93.1 28.7 %all-to-all-done.3 = bf16[8,128,512]{2,1,0:T(8,128)(2,1)S(1)} async-done(((bf16[8,128,512]{2,1,0:T(8,128)(2,1)}), bf16[8,128,512]{2,1,0:T(8,128)(2,1)S(1)}, u32[]{:S(2)}, u32[]{:S(2)}) %all-to-all-start.3) | async-done | bytes 1048608 | tf_op jit(solution)/shard_map/all_to_all | solution.py:19
  123.8 3.2 convolution_convert_fusion
  127.0 6.2 %all-to-all-start.4 = ((bf16[16,32,4096]{2,1,0:T(8,128)(2,1)}), bf16[16,32,4096]{2,1,0:T(8,128)(2,1)}, u32[]{:S(2)}, u32[]{:S(2)}) async-start(bf16[16,32,4096]{2,1,0:T(8,128)(2,1)} %convolution_convert_fusion), calls=%async_computation.4 | async-start | bytes 8388608 | tf_op jit(solution)/shard_map/all_to_all | solution.py:120
  133.8 61.0 %all-to-all-done.4 = bf16[16,32,4096]{2,1,0:T(8,128)(2,1)} async-done(((bf16[16,32,4096]{2,1,0:T(8,128)(2,1)}), bf16[16,32,4096]{2,1,0:T(8,128)(2,1)}, u32[]{:S(2)}, u32[]{:S(2)}) %all-to-all-start.4) | async-done | bytes 4194336 | tf_op jit(solution)/shard_map/all_to_all | solution.py:120
  194.7 5.5 %fusion.44 = f32[512,384]{1,0:T(8,128)S(1)} fusion(bf16[512,4096]{1,0:T(8,128)(2,1)} %bitcast.24, bf16[1,4096,384]{2,1,0:T(8,128)(2,1)} %param.23), kind=kOutput, calls=%fused_computation.62 | convolution fusion | flops 1610612736 | bytes 8126464 | tf_op jit(solution)/shard_map/dot_general | solution.py:124
  200.2 5.5 %fusion.52 = f32[512,384]{1,0:T(8,128)S(1)} fusion(bf16[512,4096]{1,0:T(8,128)(2,1)} %bitcast.24, bf16[4096,384]{1,0:T(8,128)(2,1)} %collective-permute-done.2), kind=kOutput, calls=%fused_computation.69 | convolution fusion | flops 1610612736 | bytes 8126464 | tf_op jit(solution)/shard_map/dot_general | solution.py:124
  205.7 11.8 %fusion.13 = f32[512,4096]{1,0:T(8,128)} fusion(bf16[512,4096]{1,0:T(8,128)(2,1)} %bitcast.24, f32[512,384]{1,0:T(8,128)S(1)} %fusion.44, bf16[1,384,4096]{2,1,0:T(8,128)(2,1)} %param.25, bf16[1,4096,384]{2,1,0:T(8,128)(2,1)} %param.24), kind=kOutput, calls=%fused_computation.24 | convolution fusion | flops 3222405120 | bytes 19660800 | tf_op jit(solution)/shard_map/dot_general | solution.py:131
  217.5 12.9 %add_convert_fusion = bf16[512,4096]{1,0:T(8,128)(2,1)} fusion(f32[512,4096]{1,0:T(8,128)} %fusion.13, bf16[384,4096]{1,0:T(8,128)(2,1)} %collective-permute-done.4, f32[512,384]{1,0:T(8,128)S(1)} %fusion.52, bf16[512,4096]{1,0:T(8,128)(2,1)} %bitcast.24, bf16[4096,384]{1,0:T(8,128)(2,1)} %collective-permute-done.3), kind=kOutput, calls=%fused_computation | convolution fusion | flops 3226599424 | bytes 23855104 | tf_op jit(solution)/shard_map/dot_general | solution.py:132
  230.4 8.7 %all-to-all-start.5 = ((bf16[16,32,4096]{2,1,0:T(8,128)(2,1)}), bf16[16,32,4096]{2,1,0:T(8,128)(2,1)}, u32[]{:S(2)}, u32[]{:S(2)}) async-start(bf16[16,32,4096]{2,1,0:T(8,128)(2,1)} %bitcast.92), calls=%async_computation.5 | async-start | bytes 8388608 | tf_op jit(solution)/shard_map/all_to_all | solution.py:134
  239.3 54.2 %all-to-all-done.5 = bf16[16,32,4096]{2,1,0:T(8,128)(2,1)} async-done(((bf16[16,32,4096]{2,1,0:T(8,128)(2,1)}), bf16[16,32,4096]{2,1,0:T(8,128)(2,1)}, u32[]{:S(2)}, u32[]{:S(2)}) %all-to-all-start.5) | async-done | bytes 4194336 | tf_op jit(solution)/shard_map/all_to_all | solution.py:134
  293.5 3.1 fusion.1
  296.7 28.3 %all_to_all.35 = bf16[8,128,512]{2,1,0:T(8,128)(2,1)S(1)} all-to-all(bf16[8,128,512]{2,1,0:T(8,128)(2,1)S(1)} %bitcast.94), channel_id=1, replica_groups=mesh['x'=4,'y'=4,'c'=2,'z'=8] {'z'}, dimensions={0} | all-to-all | bytes 2097152 | tf_op jit(solution)/shard_map/all_to_all | solution.py:140
  (59 shorter events, 8.8 us)
Async XLA Ops:
  0.0 9.4 %copy-start = (bf16[256,4096]{1,0:T(8,128)(2,1)S(1)}, bf16[256,4096]{1,0:T(8,128)(2,1)}, u32[]{:S(2)}) copy-start(bf16[256,4096]{1,0:T(8,128)(2,1)} %param.17) | copy-start | bytes 6291460
  2.0 22.8 %all-to-all-start = ((bf16[16,128,256]{2,1,0:T(8,128)(2,1)}), bf16[16,128,256]{2,1,0:T(8,128)(2,1)}, u32[]{:S(2)}, u32[]{:S(2)}) async-start(bf16[16,128,256]{2,1,0:T(8,128)(2,1)} %broadcast_in_dim.27), calls=%async_computation | async-start | bytes 2097152 | tf_op jit(solution)/shard_map/all_to_all | solution.py:19
  24.8 37.4 %copy-start.3 = (bf16[128,256]{1,0:T(8,128)(2,1)S(1)}, bf16[128,256]{1,0:T(8,128)(2,1)}, u32[]{:S(2)}) copy-start(bf16[128,256]{1,0:T(8,128)(2,1)} %param.14) | copy-start | bytes 196612
  24.8 35.6 %all-to-all-start.2 = ((bf16[8,128,512]{2,1,0:T(8,128)(2,1)}), bf16[8,128,512]{2,1,0:T(8,128)(2,1)S(1)}, u32[]{:S(2)}, u32[]{:S(2)}) async-start(bf16[8,128,512]{2,1,0:T(8,128)(2,1)} %bitcast.14), calls=%async_computation.2 | async-start | bytes 2097152 | tf_op jit(solution)/shard_map/all_to_all | solution.py:69
  33.4 27.1 %collective-permute-start = (bf16[16,128,256]{2,1,0:T(8,128)(2,1)}, bf16[16,128,256]{2,1,0:T(8,128)(2,1)}, u32[]{:S(2)}, u32[]{:S(2)}) collective-permute-start(bf16[16,128,256]{2,1,0:T(8,128)(2,1)} %all-to-all-done), channel_id=1, source_target_pairs={{0,8},{8,0},{1,9},{9,1},{2,10},{10,2},{3,11},{11,3},{4,12},{12,4},... | collective-permute-start | bytes 3145736 | tf_op jit(solution)/shard_map/ppermute | solution.py:14
  60.4 8.7 %collective-permute-start.1 = (bf16[8,128,512]{2,1,0:T(8,128)(2,1)S(1)}, bf16[8,128,512]{2,1,0:T(8,128)(2,1)S(1)}, u32[]{:S(2)}, u32[]{:S(2)}) collective-permute-start(bf16[8,128,512]{2,1,0:T(8,128)(2,1)S(1)} %all-to-all-done.2), channel_id=1, source_target_pairs={{0,8},{8,0},{1,9},{9,1},{2,10},{10,2},{3,11},{11,3},{4,12},{12,4},... | collective-permute-start | bytes 3145736 | tf_op jit(solution)/shard_map/ppermute | solution.py:14
  63.6 23.9 %copy-start.7 = (bf16[128,512]{1,0:T(8,128)(2,1)S(1)}, bf16[128,512]{1,0:T(8,128)(2,1)}, u32[]{:S(2)}) copy-start(bf16[128,512]{1,0:T(8,128)(2,1)} %param.13) | copy-start | bytes 393220
  65.5 21.9 %all-to-all-start.1 = ((bf16[8,128,256]{2,1,0:T(8,128)(2,1)}), bf16[8,128,256]{2,1,0:T(8,128)(2,1)S(1)}, u32[]{:S(2)}, u32[]{:S(2)}) async-start(bf16[8,128,256]{2,1,0:T(8,128)(2,1)} %broadcast_in_dim.28), calls=%async_computation.1 | async-start | bytes 1048576 | tf_op jit(solution)/shard_map/all_to_all | solution.py:19
  69.0 23.5 %copy-start.4 = (f32[4096]{0:T(1024)S(1)}, f32[4096]{0:T(1024)}, u32[]{:S(2)}) copy-start(f32[4096]{0:T(1024)} %param.18) | copy-start | bytes 49156
  69.1 23.5 %copy-start.5 = (s32[128,8]{0,1:T(8,128)S(1)}, s32[128,8]{0,1:T(8,128)}, u32[]{:S(2)}) copy-start(s32[128,8]{0,1:T(8,128)} %param.19) | copy-start | bytes 12292
  69.1 23.6 %copy-start.8 = (s32[128]{0:T(128)S(1)}, s32[128]{0:T(128)}, u32[]{:S(2)}) copy-start(s32[128]{0:T(128)} %param.21) | copy-start | bytes 1540
  89.0 32.8 %all-to-all-start.3 = ((bf16[8,128,512]{2,1,0:T(8,128)(2,1)}), bf16[8,128,512]{2,1,0:T(8,128)(2,1)S(1)}, u32[]{:S(2)}, u32[]{:S(2)}) async-start(bf16[8,128,512]{2,1,0:T(8,128)(2,1)} %broadcast_in_dim.34), calls=%async_computation.3 | async-start | bytes 2097152 | tf_op jit(solution)/shard_map/all_to_all | solution.py:19
  127.0 67.8 %all-to-all-start.4 = ((bf16[16,32,4096]{2,1,0:T(8,128)(2,1)}), bf16[16,32,4096]{2,1,0:T(8,128)(2,1)}, u32[]{:S(2)}, u32[]{:S(2)}) async-start(bf16[16,32,4096]{2,1,0:T(8,128)(2,1)} %convolution_convert_fusion), calls=%async_computation.4 | async-start | bytes 8388608 | tf_op jit(solution)/shard_map/all_to_all | solution.py:120
  133.1 67.1 %collective-permute-start.2 = (bf16[4096,384]{1,0:T(8,128)(2,1)}, bf16[4096,384]{1,0:T(8,128)(2,1)}, u32[]{:S(2)}, u32[]{:S(2)}) collective-permute-start(bf16[4096,384]{1,0:T(8,128)(2,1)} %bitcast.101), channel_id=1, source_target_pairs={{0,8},{8,0},{1,9},{9,1},{2,10},{10,2},{3,11},{11,3},{4,12},{12,4},... | collective-permute-start | bytes 9437192 | tf_op jit(solution)/shard_map/ppermute | solution.py:14
  133.2 84.4 %collective-permute-start.3 = (bf16[4096,384]{1,0:T(8,128)(2,1)}, bf16[4096,384]{1,0:T(8,128)(2,1)}, u32[]{:S(2)}, u32[]{:S(2)}) collective-permute-start(bf16[4096,384]{1,0:T(8,128)(2,1)} %bitcast.102), channel_id=1, source_target_pairs={{0,8},{8,0},{1,9},{9,1},{2,10},{10,2},{3,11},{11,3},{4,12},{12,4},... | collective-permute-start | bytes 9437192 | tf_op jit(solution)/shard_map/ppermute | solution.py:14
  133.7 83.9 %collective-permute-start.4 = (bf16[384,4096]{1,0:T(8,128)(2,1)}, bf16[384,4096]{1,0:T(8,128)(2,1)}, u32[]{:S(2)}, u32[]{:S(2)}) collective-permute-start(bf16[384,4096]{1,0:T(8,128)(2,1)} %bitcast.103), channel_id=1, source_target_pairs={{0,8},{8,0},{1,9},{9,1},{2,10},{10,2},{3,11},{11,3},{4,12},{12,4},... | collective-permute-start | bytes 9437192 | tf_op jit(solution)/shard_map/ppermute | solution.py:14
  230.4 8.7 %copy-start.6 = (bf16[128,8]{0,1:T(8,128)(2,1)S(1)}, bf16[128,8]{0,1:T(8,128)(2,1)}, u32[]{:S(2)}) copy-start(bf16[128,8]{0,1:T(8,128)(2,1)} %param.20) | copy-start | bytes 6148
  230.4 63.0 %all-to-all-start.5 = ((bf16[16,32,4096]{2,1,0:T(8,128)(2,1)}), bf16[16,32,4096]{2,1,0:T(8,128)(2,1)}, u32[]{:S(2)}, u32[]{:S(2)}) async-start(bf16[16,32,4096]{2,1,0:T(8,128)(2,1)} %bitcast.92), calls=%async_computation.5 | async-start | bytes 8388608 | tf_op jit(solution)/shard_map/all_to_all | solution.py:134
  293.4 32.4 %copy-start.1 = (bf16[256,4096]{1,0:T(8,128)(2,1)S(1)}, bf16[256,4096]{1,0:T(8,128)(2,1)}, u32[]{:S(2)}) copy-start(bf16[256,4096]{1,0:T(8,128)(2,1)} %param.17) | copy-start | bytes 6291460
  296.5 28.5 %copy-start.2 = (bf16[128,512]{1,0:T(8,128)(2,1)S(1)}, bf16[128,512]{1,0:T(8,128)(2,1)}, u32[]{:S(2)}) copy-start(bf16[128,512]{1,0:T(8,128)(2,1)} %param.22) | copy-start | bytes 393220

commit v2 on v1

--- a/solution.py
+++ b/solution.py
@@ -1,6 +1,8 @@
 import jax
 import jax.numpy as jnp
 from jax import lax
+from jax.experimental import pallas as pl
+from jax.experimental.pallas import tpu as pltpu
 from jax.sharding import Mesh, PartitionSpec as P
 
 HD = 128
@@ -8,6 +10,8 @@
 EXP_GROUP = 8
 BF = jnp.bfloat16
 F32 = jnp.float32
+STEPS = 4
+PIECES = 4
 
 
 def swap_cores(array):
@@ -17,6 +21,54 @@
 def gather_by_exchange(array, axes, count):
     spread = jnp.broadcast_to(array[None], (count,) + array.shape)
     return lax.all_to_all(spread, axes, split_axis=0, concat_axis=0, tiled=True)
+
+
+def expert_kernel(
+    rows, gate_a, up_a, down_a, gate_b, up_b, down_b, out, totals, hidden
+):
+    part = gate_a.shape[1]
+    deep = gate_a.shape[0] // STEPS
+    width = down_a.shape[1] // PIECES
+    for which, (gate, up) in enumerate(((gate_a, up_a), (gate_b, up_b))):
+        for step in range(STEPS):
+            here = pl.ds(step * deep, deep)
+            weights = jnp.concatenate([gate[here], up[here]], axis=1)
+            product = jnp.dot(rows[:, here], weights, preferred_element_type=F32)
+            if step:
+                product += totals[...]
+            if step < STEPS - 1:
+                totals[...] = product
+        gate_out, up_out = product[:, :part], product[:, part:]
+        hidden[:, pl.ds(which * part, part)] = (jax.nn.silu(gate_out) * up_out).astype(BF)
+    for piece in range(PIECES):
+        columns = pl.ds(piece * width, width)
+        down = jnp.concatenate([down_a[:, columns], down_b[:, columns]], axis=0)
+        out[:, columns] = jnp.dot(hidden[...], down, preferred_element_type=F32).astype(BF)
+
+
+def expert_partial(rows, gate_a, up_a, down_a, gate_b, up_b, down_b):
+    count, depth = rows.shape
+    part = gate_a.shape[1]
+    return pl.pallas_call(
+        expert_kernel,
+        out_shape=jax.ShapeDtypeStruct((count, depth), BF),
+        in_specs=[pl.BlockSpec(memory_space=pltpu.VMEM)] * 7,
+        out_specs=pl.BlockSpec(memory_space=pltpu.VMEM),
+        scratch_shapes=[
+            pltpu.VMEM((count, 2 * part), F32),
+            pltpu.VMEM((count, 2 * part), BF),
+        ],
+        compiler_params=pltpu.CompilerParams(vmem_limit_bytes=16 * 2**20),
+        cost_estimate=pl.CostEstimate(
+            flops=12 * count * depth * part,
+            bytes_accessed=12 * depth * part + 4 * count * depth,
+            transcendentals=2 * count * part,
+        ),
+        name="expert_partial",
+    )(*[
+        pltpu.with_memory_space_constraint(operand, pltpu.VMEM)
+        for operand in (rows, gate_a, up_a, down_a, gate_b, up_b, down_b)
+    ])
 
 
 def attention(queries, all_kv, kv_local):
@@ -66,10 +118,16 @@
 
     half_rows = out_proj.shape[0] // 2
     out_half = lax.dynamic_slice_in_dim(out_proj, core * half_rows, half_rows, 0)
-    out_own = lax.all_to_all(
-        out_half.reshape(half_rows, depth, slice_width).transpose(1, 0, 2),
-        "z", split_axis=0, concat_axis=0, tiled=True,
-    )
+    out_own = []
+    for step in range(depth):
+        target = lax.rem(group_index + depth - step, depth)
+        piece = lax.dynamic_slice_in_dim(out_half, target * slice_width, slice_width, 1)
+        if step:
+            piece = lax.ppermute(
+                piece, "z", [(i, (i + depth - step) % depth) for i in range(depth)]
+            )
+        out_own.append(piece)
+    out_own = jnp.stack(out_own)
     out_cols = jnp.concatenate([out_own, swap_cores(out_own)], axis=1)
     out_cols = out_cols.reshape(-1, slice_width)
 
@@ -87,6 +145,9 @@
         jnp.concatenate([second, first], axis=1),
     )
     attended_all = gather_by_exchange(attended, "z", depth)
+    attended_all = lax.dynamic_slice_in_dim(
+        jnp.concatenate([attended_all, attended_all], axis=0), group_index, depth, 0
+    )
     attended_all = attended_all.transpose(1, 0, 2).reshape(tokens, -1)
     attn_share = jnp.dot(attended_all, out_cols, preferred_element_type=F32)
     mixed_local = (residual_in.astype(F32) + attn_share).astype(BF)
@@ -120,17 +181,9 @@
     arrived = lax.all_to_all(outgoing, ("x", "y"), split_axis=0, concat_axis=0, tiled=True)
     rows = arrived.reshape(-1, arrived.shape[-1])
 
-    def hidden_of(gate, up):
-        gate_out = jnp.dot(rows, gate, preferred_element_type=F32)
-        up_out = jnp.dot(rows, up, preferred_element_type=F32)
-        return (jax.nn.silu(gate_out) * up_out).astype(BF)
-
-    hidden_own = hidden_of(gate_proj[0], up_proj[0])
-    hidden_other = hidden_of(gate_other, up_other)
-    partial_out = (
-        jnp.dot(hidden_own, down_proj[0], preferred_element_type=F32)
-        + jnp.dot(hidden_other, down_other, preferred_element_type=F32)
-    ).astype(BF)
+    partial_out = expert_partial(
+        rows, gate_proj[0], up_proj[0], down_proj[0], gate_other, up_other, down_other
+    )
     returned = lax.all_to_all(
         partial_out.reshape(arrived.shape), ("x", "y"), split_axis=0, concat_axis=0, tiled=True
     )

time: 329 us -> 308 us (0.936)
  waiting for transfers between devices: 202 us -> 166 us
  matrix products: 44.1 us -> 9.68 us
  local copies, waits for them, and re-layouts: 6.16 us -> 32.1 us
  Pallas kernels: 0 us -> 16.1 us
  starting transfers between devices: 38.6 us -> 48.7 us
    dot_general x4 -> x0, matrix products: 35.6 us -> none  [the longest x1 12.9 us: shards(): jnp.dot(hidden_other, down_other, preferred_element_type=F32)]
    all_to_all x1 -> x0, waiting for transfers between devices: 27 us -> none  [shards(): lax.all_to_all(out_half.reshape(half_rows, depth, slice_width).transpose(...]
    unnamed x19 -> x49, local copies, waits for them, and re-layouts: 0.71 us -> 25.9 us
    all_to_all x3, waiting for transfers between devices: 60.3 us -> 43.1 us  [gather_by_exchange(): return lax.all_to_all(spread, axes, split_axis=0, concat_axis=0, tiled=True)]
    pallas_call x0 -> x1, Pallas kernels: none -> 16.1 us  [expert_partial(): pl.pallas_call(expert_kernel, out_shape=jax.ShapeDtypeStruct((count, dept...]
    ppermute x0 -> x7, starting transfers between devices: none -> 15.5 us  [shards(): lax.ppermute(piece, 'z', [(i, (i + depth - step) % depth) for i in range(...]
    all_to_all x1, waiting for transfers between devices: 61 us -> 47.5 us  [shards(): lax.all_to_all(outgoing, ('x', 'y'), split_axis=0, concat_axis=0, tiled=T...]
    ppermute x5, waiting for transfers between devices: 0.01 us -> 12.5 us  [swap_cores(): return lax.ppermute(array, 'c', [(0, 1), (1, 0)])]
  transfers between devices with their start and end apart: 11 -> 17, of which waited for: 6 -> 11; matrix products, arithmetic and copies ran while one was open for 9% -> 4% of each run, Pallas kernels for 0% -> 0%
where the time goes in v2:
time: 308 us; the launch traced here: 303 us
  waiting for transfers between devices  166 us (54%)
  starting transfers between devices  48.7 us (16%)
  local copies, waits for them, and re-layouts  32.1 us (10%)
  blocking collectives  26.3 us (9%)
  Pallas kernels  16.1 us (5%)
  matrix products  9.68 us (3%)
  other arithmetic  4.33 us (1%)
    all_to_all x1, waiting for transfers between devices, shards(): lax.all_to_all(partial_out.reshape(arrived.shape), ('x', 'y'), split_axis...  51 us
    all_to_all x1, waiting for transfers between devices, shards(): lax.all_to_all(outgoing, ('x', 'y'), split_axis=0, concat_axis=0, tiled=T...  47.5 us
    all_to_all x3, waiting for transfers between devices, gather_by_exchange(): return lax.all_to_all(spread, axes, split_axis=0, concat_axis=0, tiled=True)  43.1 us
    all_to_all x1, blocking collectives, shards(): lax.all_to_all(combined.reshape(tokens, depth, slice_width).transpose(1,...  26.3 us
    unnamed x49, local copies, waits for them, and re-layouts  25.9 us
    all_to_all x3, starting transfers between devices, gather_by_exchange(): return lax.all_to_all(spread, axes, split_axis=0, concat_axis=0, tiled=True)  16.4 us
    pallas_call x1, Pallas kernels, expert_partial(): pl.pallas_call(expert_kernel, out_shape=jax.ShapeDtypeStruct((count, dept...  16.1 us
    ppermute x7, starting transfers between devices, shards(): lax.ppermute(piece, 'z', [(i, (i + depth - step) % depth) for i in range(...  15.5 us
  transfers between devices with their start and end apart: 17, of which 11 were waited for; matrix products, arithmetic and copies ran while one was open for 4% of the time, Pallas kernels for 0%

profile of v2, /device:TPU:6, one launch (start us, length us, event | category | flops | bytes accessed | tf_op | source)
XLA Modules:
  0.0 303.3 jit_solution(12038532997132471566)
XLA Ops:
  2.1 7.4 %all-to-all-start = ((bf16[16,128,256]{2,1,0:T(8,128)(2,1)}), bf16[16,128,256]{2,1,0:T(8,128)(2,1)S(1)}, u32[]{:S(2)}, u32[]{:S(2)}) async-start(bf16[16,128,256]{2,1,0:T(8,128)(2,1)} %broadcast_in_dim.27), calls=%async_computation | async-start | bytes 2097152 | tf_op jit(solution)/shard_map/all_to_all | solution.py:23
  11.0 5.8 %collective-permute-start.1 = (bf16[128,512]{1,0:T(8,128)(2,1)}, bf16[128,512]{1,0:T(8,128)(2,1)}, u32[]{:S(2)}, u32[]{:S(2)}) collective-permute-start(bf16[128,512]{1,0:T(8,128)(2,1)} %get-tuple-element.10), channel_id=1, source_target_pairs={{0,7},{1,0},{2,1},{3,2},{4,3},{5,4},{6,5},{7,6},{8,15},{9,8},{10,9... | collective-permute-start | bytes 393224 | tf_op jit(solution)/shard_map/ppermute | solution.py:126
  18.7 5.0 %collective-permute-start.4 = (bf16[128,512]{1,0:T(8,128)(2,1)}, bf16[128,512]{1,0:T(8,128)(2,1)}, u32[]{:S(2)}, u32[]{:S(2)}) collective-permute-start(bf16[128,512]{1,0:T(8,128)(2,1)} %get-tuple-element.7), channel_id=1, source_target_pairs={{0,4},{1,5},{2,6},{3,7},{4,0},{5,1},{6,2},{7,3},{8,12},{9,13},{10,... | collective-permute-start | bytes 393224 | tf_op jit(solution)/shard_map/ppermute | solution.py:126
  23.9 2.5 collective-permute-start.6
  31.3 7.8 %collective-permute-done.3 = bf16[128,512]{1,0:T(8,128)(2,1)} collective-permute-done((bf16[128,512]{1,0:T(8,128)(2,1)}, bf16[128,512]{1,0:T(8,128)(2,1)}, u32[]{:S(2)}, u32[]{:S(2)}) %collective-permute-start.3) | collective-permute-done | bytes 131104 | tf_op jit(solution)/shard_map/ppermute | solution.py:126
  50.7 5.2 %all-to-all-start.1 = ((bf16[8,128,256]{2,1,0:T(8,128)(2,1)}), bf16[8,128,256]{2,1,0:T(8,128)(2,1)S(1)}, u32[]{:S(2)}, u32[]{:S(2)}) async-start(bf16[8,128,256]{2,1,0:T(8,128)(2,1)} %broadcast_in_dim.28), calls=%async_computation.1 | async-start | bytes 1048576 | tf_op jit(solution)/shard_map/all_to_all | solution.py:23
  57.0 16.6 %all-to-all-done.1 = bf16[8,128,256]{2,1,0:T(8,128)(2,1)S(1)} async-done(((bf16[8,128,256]{2,1,0:T(8,128)(2,1)}), bf16[8,128,256]{2,1,0:T(8,128)(2,1)S(1)}, u32[]{:S(2)}, u32[]{:S(2)}) %all-to-all-start.1) | async-done | bytes 524320 | tf_op jit(solution)/shard_map/all_to_all | solution.py:23
  76.4 3.7 %all-to-all-start.2 = ((bf16[8,128,512]{2,1,0:T(8,128)(2,1)}), bf16[8,128,512]{2,1,0:T(8,128)(2,1)S(1)}, u32[]{:S(2)}, u32[]{:S(2)}) async-start(bf16[8,128,512]{2,1,0:T(8,128)(2,1)} %broadcast_in_dim.34), calls=%async_computation.2 | async-start | bytes 2097152 | tf_op jit(solution)/shard_map/all_to_all | solution.py:23
  80.7 26.5 %all-to-all-done.2 = bf16[8,128,512]{2,1,0:T(8,128)(2,1)S(1)} async-done(((bf16[8,128,512]{2,1,0:T(8,128)(2,1)}), bf16[8,128,512]{2,1,0:T(8,128)(2,1)S(1)}, u32[]{:S(2)}, u32[]{:S(2)}) %all-to-all-start.2) | async-done | bytes 1048608 | tf_op jit(solution)/shard_map/all_to_all | solution.py:23
  109.1 3.3 %convolution_convert_fusion = bf16[16,32,4096]{2,1,0:T(8,128)(2,1)} fusion(bf16[16,32,128]{2,1,0:T(8,128)(2,1)S(1)} %bitcast.102, bf16[128,4096,1]{0,1,2:T(8,128)(2,1)S(1)} %bitcast.100), kind=kOutput, calls=%fused_computation | convolution fusion | flops 538968064 | bytes 5373952 | tf_op jit(solution)/shard_map/jct,td->jcd/dot_general | solution.py:178
  112.4 7.5 %all-to-all-start.3 = ((bf16[16,32,4096]{2,1,0:T(8,128)(2,1)}), bf16[16,32,4096]{2,1,0:T(8,128)(2,1)}, u32[]{:S(2)}, u32[]{:S(2)}) async-start(bf16[16,32,4096]{2,1,0:T(8,128)(2,1)} %convolution_convert_fusion), calls=%async_computation.3 | async-start | bytes 8388608 | tf_op jit(solution)/shard_map/all_to_all | solution.py:181
  120.5 5.3 %collective-permute-done.10.up_b = bf16[4096,384]{1,0:T(8,128)(2,1)S(1)} collective-permute-done((bf16[4096,384]{1,0:T(8,128)(2,1)}, bf16[4096,384]{1,0:T(8,128)(2,1)S(1)}, u32[]{:S(2)}, u32[]{:S(2)}) %collective-permute-start.10) | collective-permute-done | bytes 3145760 | tf_op jit(solution)/shard_map/ppermute | solution.py:18
  127.5 7.3 %collective-permute-done.11.down_b = bf16[384,4096]{1,0:T(8,128)(2,1)S(1)} collective-permute-done((bf16[384,4096]{1,0:T(8,128)(2,1)}, bf16[384,4096]{1,0:T(8,128)(2,1)S(1)}, u32[]{:S(2)}, u32[]{:S(2)}) %collective-permute-start.11) | collective-permute-done | bytes 3145760 | tf_op jit(solution)/shard_map/ppermute | solution.py:18
  138.1 47.5 %all-to-all-done.3 = bf16[16,32,4096]{2,1,0:T(8,128)(2,1)} async-done(((bf16[16,32,4096]{2,1,0:T(8,128)(2,1)}), bf16[16,32,4096]{2,1,0:T(8,128)(2,1)}, u32[]{:S(2)}, u32[]{:S(2)}) %all-to-all-start.3) | async-done | bytes 4194336 | tf_op jit(solution)/shard_map/all_to_all | solution.py:181
  185.6 1.9 copy-done.3
  187.5 1.9 copy-done.4
  189.4 1.9 copy-done.6
  191.2 1.9 copy-done.8
  195.0 16.1 %expert_partial.1 = bf16[512,4096]{1,0:T(8,128)(2,1)S(1)} custom-call(bf16[512,4096]{1,0:T(8,128)(2,1)} %bitcast.30.rows, bf16[4096,384]{1,0:T(8,128)(2,1)S(1)} %bitcast.92, bf16[4096,384]{1,0:T(8,128)(2,1)S(1)} %bitcast.94, bf16[384,4096]{1,0:T(8,128)(2,1)S(1)} %bitcast.96, bf16[4096,384]{1,0:T(8,128)(2,1)S(1)} %copy-done.10, ...), custom_call_target="tpu_custom_call" | custom-call | flops 9663676416 | bytes 27262976 | tf_op jit(solution)/shard_map/expert_partial/pallas_call | solution.py:52
  211.1 2.0 copy-done.1
  213.1 8.7 %all-to-all-start.4 = ((bf16[16,32,4096]{2,1,0:T(8,128)(2,1)}), bf16[16,32,4096]{2,1,0:T(8,128)(2,1)}, u32[]{:S(2)}, u32[]{:S(2)}) async-start(bf16[16,32,4096]{2,1,0:T(8,128)(2,1)} %bitcast.90), calls=%async_computation.4 | async-start | bytes 8388608 | tf_op jit(solution)/shard_map/all_to_all | solution.py:187
  222.0 51.0 %all-to-all-done.4 = bf16[16,32,4096]{2,1,0:T(8,128)(2,1)} async-done(((bf16[16,32,4096]{2,1,0:T(8,128)(2,1)}), bf16[16,32,4096]{2,1,0:T(8,128)(2,1)}, u32[]{:S(2)}, u32[]{:S(2)}) %all-to-all-start.4) | async-done | bytes 4194336 | tf_op jit(solution)/shard_map/all_to_all | solution.py:187
  273.0 2.9 fusion.1
  276.0 26.3 %all_to_all.30 = bf16[8,128,512]{2,1,0:T(8,128)(2,1)S(1)} all-to-all(bf16[8,128,512]{2,1,0:T(8,128)(2,1)S(1)} %bitcast.99), channel_id=1, replica_groups=mesh['x'=4,'y'=4,'c'=2,'z'=8] {'z'}, dimensions={0} | all-to-all | bytes 2097152 | tf_op jit(solution)/shard_map/all_to_all | solution.py:193
  (98 shorter events, 37.0 us)
Async XLA Ops:
  0.0 47.3 %copy-start = (bf16[128,256]{1,0:T(8,128)(2,1)S(1)}, bf16[128,256]{1,0:T(8,128)(2,1)}, u32[]{:S(2)}) copy-start(bf16[128,256]{1,0:T(8,128)(2,1)} %param.14) | copy-start | bytes 196612
  2.1 37.0 %all-to-all-start = ((bf16[16,128,256]{2,1,0:T(8,128)(2,1)}), bf16[16,128,256]{2,1,0:T(8,128)(2,1)S(1)}, u32[]{:S(2)}, u32[]{:S(2)}) async-start(bf16[16,128,256]{2,1,0:T(8,128)(2,1)} %broadcast_in_dim.27), calls=%async_computation | async-start | bytes 2097152 | tf_op jit(solution)/shard_map/all_to_all | solution.py:23
  11.0 12.9 %collective-permute-start.1 = (bf16[128,512]{1,0:T(8,128)(2,1)}, bf16[128,512]{1,0:T(8,128)(2,1)}, u32[]{:S(2)}, u32[]{:S(2)}) collective-permute-start(bf16[128,512]{1,0:T(8,128)(2,1)} %get-tuple-element.10), channel_id=1, source_target_pairs={{0,7},{1,0},{2,1},{3,2},{4,3},{5,4},{6,5},{7,6},{8,15},{9,8},{10,9... | collective-permute-start | bytes 393224 | tf_op jit(solution)/shard_map/ppermute | solution.py:126
  16.8 12.4 %collective-permute-start.2 = (bf16[128,512]{1,0:T(8,128)(2,1)}, bf16[128,512]{1,0:T(8,128)(2,1)}, u32[]{:S(2)}, u32[]{:S(2)}) collective-permute-start(bf16[128,512]{1,0:T(8,128)(2,1)} %get-tuple-element.9), channel_id=1, source_target_pairs={{0,6},{1,7},{2,0},{3,1},{4,2},{5,3},{6,4},{7,5},{8,14},{9,15},{10,... | collective-permute-start | bytes 393224 | tf_op jit(solution)/shard_map/ppermute | solution.py:126
  18.3 20.8 %collective-permute-start.3 = (bf16[128,512]{1,0:T(8,128)(2,1)}, bf16[128,512]{1,0:T(8,128)(2,1)}, u32[]{:S(2)}, u32[]{:S(2)}) collective-permute-start(bf16[128,512]{1,0:T(8,128)(2,1)} %get-tuple-element.8), channel_id=1, source_target_pairs={{0,5},{1,6},{2,7},{3,0},{4,1},{5,2},{6,3},{7,4},{8,13},{9,14},{10,... | collective-permute-start | bytes 393224 | tf_op jit(solution)/shard_map/ppermute | solution.py:126
  18.7 21.9 %collective-permute-start.4 = (bf16[128,512]{1,0:T(8,128)(2,1)}, bf16[128,512]{1,0:T(8,128)(2,1)}, u32[]{:S(2)}, u32[]{:S(2)}) collective-permute-start(bf16[128,512]{1,0:T(8,128)(2,1)} %get-tuple-element.7), channel_id=1, source_target_pairs={{0,4},{1,5},{2,6},{3,7},{4,0},{5,1},{6,2},{7,3},{8,12},{9,13},{10,... | collective-permute-start | bytes 393224 | tf_op jit(solution)/shard_map/ppermute | solution.py:126
  23.8 18.7 %collective-permute-start.5 = (bf16[128,512]{1,0:T(8,128)(2,1)}, bf16[128,512]{1,0:T(8,128)(2,1)}, u32[]{:S(2)}, u32[]{:S(2)}) collective-permute-start(bf16[128,512]{1,0:T(8,128)(2,1)} %get-tuple-element.6), channel_id=1, source_target_pairs={{0,3},{1,4},{2,5},{3,6},{4,7},{5,0},{6,1},{7,2},{8,11},{9,12},{10,... | collective-permute-start | bytes 393224 | tf_op jit(solution)/shard_map/ppermute | solution.py:126
  23.9 21.4 %collective-permute-start.6 = (bf16[128,512]{1,0:T(8,128)(2,1)S(1)}, bf16[128,512]{1,0:T(8,128)(2,1)S(1)}, u32[]{:S(2)}, u32[]{:S(2)}) collective-permute-start(bf16[128,512]{1,0:T(8,128)(2,1)S(1)} %get-tuple-element.11), channel_id=1, source_target_pairs={{0,2},{1,3},{2,4},{3,5},{4,6},{5,7},{6,0},{7,1},{8,10},{9,11},{10,... | collective-permute-start | bytes 393224 | tf_op jit(solution)/shard_map/ppermute | solution.py:126
  29.2 17.2 %collective-permute-start.7 = (bf16[128,512]{1,0:T(8,128)(2,1)S(1)}, bf16[128,512]{1,0:T(8,128)(2,1)S(1)}, u32[]{:S(2)}, u32[]{:S(2)}) collective-permute-start(bf16[128,512]{1,0:T(8,128)(2,1)S(1)} %get-tuple-element.5), channel_id=1, source_target_pairs={{0,1},{1,2},{2,3},{3,4},{4,5},{5,6},{6,7},{7,0},{8,9},{9,10},{10,1... | collective-permute-start | bytes 393224 | tf_op jit(solution)/shard_map/ppermute | solution.py:126
  39.0 8.1 %collective-permute-start = (bf16[16,128,256]{2,1,0:T(8,128)(2,1)S(1)}, bf16[16,128,256]{2,1,0:T(8,128)(2,1)S(1)}, u32[]{:S(2)}, u32[]{:S(2)}) collective-permute-start(bf16[16,128,256]{2,1,0:T(8,128)(2,1)S(1)} %all-to-all-done), channel_id=1, source_target_pairs={{0,8},{8,0},{1,9},{9,1},{2,10},{10,2},{3,11},{11,3},{4,12},{12,4},... | collective-permute-start | bytes 3145736 | tf_op jit(solution)/shard_map/ppermute | solution.py:18
  47.1 8.8 %collective-permute-start.8 = (bf16[8,128,512]{2,1,0:T(8,128)(2,1)}, bf16[8,128,512]{2,1,0:T(8,128)(2,1)S(1)}, u32[]{:S(2)}, u32[]{:S(2)}) collective-permute-start(bf16[8,128,512]{2,1,0:T(8,128)(2,1)} %bitcast_dynamic-update-slice_fusion), channel_id=1, source_target_pairs={{0,8},{8,0},{1,9},{9,1},{2,10},{10,2},{3,11},{11,3},{4,12},{12,4},... | collective-permute-start | bytes 3145736 | tf_op jit(solution)/shard_map/ppermute | solution.py:18
  48.8 24.8 %copy-start.14 = (bf16[8,128,512]{2,1,0:T(8,128)(2,1)S(1)}, bf16[8,128,512]{2,1,0:T(8,128)(2,1)}, u32[]{:S(2)}) copy-start(bf16[8,128,512]{2,1,0:T(8,128)(2,1)} %bitcast_dynamic-update-slice_fusion) | copy-start | bytes 3145732
  48.8 24.8 %copy-start.19 = (bf16[128,512]{1,0:T(8,128)(2,1)S(1)}, bf16[128,512]{1,0:T(8,128)(2,1)}, u32[]{:S(2)}) copy-start(bf16[128,512]{1,0:T(8,128)(2,1)} %param.13) | copy-start | bytes 393220
  50.7 22.9 %all-to-all-start.1 = ((bf16[8,128,256]{2,1,0:T(8,128)(2,1)}), bf16[8,128,256]{2,1,0:T(8,128)(2,1)S(1)}, u32[]{:S(2)}, u32[]{:S(2)}) async-start(bf16[8,128,256]{2,1,0:T(8,128)(2,1)} %broadcast_in_dim.28), calls=%async_computation.1 | async-start | bytes 1048576 | tf_op jit(solution)/shard_map/all_to_all | solution.py:23
  55.9 24.2 %copy-start.15 = (f32[4096]{0:T(1024)S(1)}, f32[4096]{0:T(1024)}, u32[]{:S(2)}) copy-start(f32[4096]{0:T(1024)} %param.18) | copy-start | bytes 49156
  55.9 24.3 %copy-start.16 = (s32[128,8]{0,1:T(8,128)S(1)}, s32[128,8]{0,1:T(8,128)}, u32[]{:S(2)}) copy-start(s32[128,8]{0,1:T(8,128)} %param.19) | copy-start | bytes 12292
  55.9 24.3 %copy-start.20 = (s32[128]{0:T(128)S(1)}, s32[128]{0:T(128)}, u32[]{:S(2)}) copy-start(s32[128]{0:T(128)} %param.21) | copy-start | bytes 1540
  76.4 30.7 %all-to-all-start.2 = ((bf16[8,128,512]{2,1,0:T(8,128)(2,1)}), bf16[8,128,512]{2,1,0:T(8,128)(2,1)S(1)}, u32[]{:S(2)}, u32[]{:S(2)}) async-start(bf16[8,128,512]{2,1,0:T(8,128)(2,1)} %broadcast_in_dim.34), calls=%async_computation.2 | async-start | bytes 2097152 | tf_op jit(solution)/shard_map/all_to_all | solution.py:23
  112.4 73.2 %all-to-all-start.3 = ((bf16[16,32,4096]{2,1,0:T(8,128)(2,1)}), bf16[16,32,4096]{2,1,0:T(8,128)(2,1)}, u32[]{:S(2)}, u32[]{:S(2)}) async-start(bf16[16,32,4096]{2,1,0:T(8,128)(2,1)} %convolution_convert_fusion), calls=%async_computation.3 | async-start | bytes 8388608 | tf_op jit(solution)/shard_map/all_to_all | solution.py:181
  119.9 5.9 %collective-permute-start.10 = (bf16[4096,384]{1,0:T(8,128)(2,1)}, bf16[4096,384]{1,0:T(8,128)(2,1)S(1)}, u32[]{:S(2)}, u32[]{:S(2)}) collective-permute-start(bf16[4096,384]{1,0:T(8,128)(2,1)} %bitcast.93), channel_id=1, source_target_pairs={{0,8},{8,0},{1,9},{9,1},{2,10},{10,2},{3,11},{11,3},{4,12},{12,4},... | collective-permute-start | bytes 9437192 | tf_op jit(solution)/shard_map/ppermute | solution.py:18
  119.9 14.9 %collective-permute-start.11 = (bf16[384,4096]{1,0:T(8,128)(2,1)}, bf16[384,4096]{1,0:T(8,128)(2,1)S(1)}, u32[]{:S(2)}, u32[]{:S(2)}) collective-permute-start(bf16[384,4096]{1,0:T(8,128)(2,1)} %bitcast.95), channel_id=1, source_target_pairs={{0,8},{8,0},{1,9},{9,1},{2,10},{10,2},{3,11},{11,3},{4,12},{12,4},... | collective-permute-start | bytes 9437192 | tf_op jit(solution)/shard_map/ppermute | solution.py:18
  120.4 16.0 %collective-permute-start.9 = (bf16[4096,384]{1,0:T(8,128)(2,1)S(1)}, bf16[4096,384]{1,0:T(8,128)(2,1)S(1)}, u32[]{:S(2)}, u32[]{:S(2)}) collective-permute-start(bf16[4096,384]{1,0:T(8,128)(2,1)S(1)} %bitcast.91), channel_id=1, source_target_pairs={{0,8},{8,0},{1,9},{9,1},{2,10},{10,2},{3,11},{11,3},{4,12},{12,4},... | collective-permute-start | bytes 9437192 | tf_op jit(solution)/shard_map/ppermute | solution.py:18
  213.1 59.8 %all-to-all-start.4 = ((bf16[16,32,4096]{2,1,0:T(8,128)(2,1)}), bf16[16,32,4096]{2,1,0:T(8,128)(2,1)}, u32[]{:S(2)}, u32[]{:S(2)}) async-start(bf16[16,32,4096]{2,1,0:T(8,128)(2,1)} %bitcast.90), calls=%async_computation.4 | async-start | bytes 8388608 | tf_op jit(solution)/shard_map/all_to_all | solution.py:187
  275.9 26.6 %copy-start.12 = (bf16[128,512]{1,0:T(8,128)(2,1)S(1)}, bf16[128,512]{1,0:T(8,128)(2,1)}, u32[]{:S(2)}) copy-start(bf16[128,512]{1,0:T(8,128)(2,1)} %param.22) | copy-start | bytes 393220
  (14 other events, 44.8 us)

commit v3 on v2

--- a/solution.py
+++ b/solution.py
@@ -10,7 +10,6 @@
 EXP_GROUP = 8
 BF = jnp.bfloat16
 F32 = jnp.float32
-STEPS = 4
 PIECES = 4
 
 
@@ -23,23 +22,22 @@
     return lax.all_to_all(spread, axes, split_axis=0, concat_axis=0, tiled=True)
 
 
+def sum_slices(array, depth):
+    tokens, width = array.shape
+    slices = array.reshape(tokens, depth, width // depth).transpose(1, 0, 2)
+    shares = lax.all_to_all(slices, "z", split_axis=0, concat_axis=0, tiled=True)
+    return jnp.sum(shares.astype(F32), axis=0)
+
+
 def expert_kernel(
-    rows, gate_a, up_a, down_a, gate_b, up_b, down_b, out, totals, hidden
+    rows, gate_a, up_a, down_a, gate_b, up_b, down_b, out, gate_out, hidden
 ):
-    part = gate_a.shape[1]
-    deep = gate_a.shape[0] // STEPS
     width = down_a.shape[1] // PIECES
-    for which, (gate, up) in enumerate(((gate_a, up_a), (gate_b, up_b))):
-        for step in range(STEPS):
-            here = pl.ds(step * deep, deep)
-            weights = jnp.concatenate([gate[here], up[here]], axis=1)
-            product = jnp.dot(rows[:, here], weights, preferred_element_type=F32)
-            if step:
-                product += totals[...]
-            if step < STEPS - 1:
-                totals[...] = product
-        gate_out, up_out = product[:, :part], product[:, part:]
-        hidden[:, pl.ds(which * part, part)] = (jax.nn.silu(gate_out) * up_out).astype(BF)
+    gates = jnp.concatenate([gate_a[...], gate_b[...]], axis=1)
+    gate_out[...] = jnp.dot(rows[...], gates, preferred_element_type=F32)
+    ups = jnp.concatenate([up_a[...], up_b[...]], axis=1)
+    up_out = jnp.dot(rows[...], ups, preferred_element_type=F32)
+    hidden[...] = (jax.nn.silu(gate_out[...]) * up_out).astype(BF)
     for piece in range(PIECES):
         columns = pl.ds(piece * width, width)
         down = jnp.concatenate([down_a[:, columns], down_b[:, columns]], axis=0)
@@ -106,30 +104,13 @@
     plane = lax.axis_size("x") * lax.axis_size("y")
     depth = lax.axis_size("z")
     group_index = lax.axis_index("z")
-    core = lax.axis_index("c")
     tokens = queries.shape[0]
-    slice_width = residual_in.shape[1]
 
     own_kv = gather_by_exchange(
         jnp.concatenate([key_heads, value_heads], axis=1), ("x", "y"), plane
     )
     all_kv = jnp.concatenate([own_kv, swap_cores(own_kv)], axis=0)
     all_kv = all_kv.reshape(-1, all_kv.shape[-1])
-
-    half_rows = out_proj.shape[0] // 2
-    out_half = lax.dynamic_slice_in_dim(out_proj, core * half_rows, half_rows, 0)
-    out_own = []
-    for step in range(depth):
-        target = lax.rem(group_index + depth - step, depth)
-        piece = lax.dynamic_slice_in_dim(out_half, target * slice_width, slice_width, 1)
-        if step:
-            piece = lax.ppermute(
-                piece, "z", [(i, (i + depth - step) % depth) for i in range(depth)]
-            )
-        out_own.append(piece)
-    out_own = jnp.stack(out_own)
-    out_cols = jnp.concatenate([out_own, swap_cores(out_own)], axis=1)
-    out_cols = out_cols.reshape(-1, slice_width)
 
     gate_other, up_other, down_other = (
         swap_cores(gate_proj[0]),
@@ -138,18 +119,8 @@
     )
 
     attended = attention(queries, all_kv, key_heads.shape[1] // HD)
-    first, second = attended[:, :half_rows], attended[:, half_rows:]
-    attended = jnp.where(
-        core == 0,
-        attended,
-        jnp.concatenate([second, first], axis=1),
-    )
-    attended_all = gather_by_exchange(attended, "z", depth)
-    attended_all = lax.dynamic_slice_in_dim(
-        jnp.concatenate([attended_all, attended_all], axis=0), group_index, depth, 0
-    )
-    attended_all = attended_all.transpose(1, 0, 2).reshape(tokens, -1)
-    attn_share = jnp.dot(attended_all, out_cols, preferred_element_type=F32)
+    partial_attn = jnp.dot(attended, out_proj, preferred_element_type=F32).astype(BF)
+    attn_share = sum_slices(partial_attn, depth)
     mixed_local = (residual_in.astype(F32) + attn_share).astype(BF)
 
     mixed_full = gather_by_exchange(mixed_local, "z", depth)
@@ -178,6 +149,9 @@
     outgoing = jnp.einsum(
         "jct,td->jcd", selector, normed, preferred_element_type=F32
     ).astype(BF)
+    outgoing, gate_other, up_other, down_other, weighted_select = lax.optimization_barrier(
+        (outgoing, gate_other, up_other, down_other, weighted_select)
+    )
     arrived = lax.all_to_all(outgoing, ("x", "y"), split_axis=0, concat_axis=0, tiled=True)
     rows = arrived.reshape(-1, arrived.shape[-1])
 
@@ -190,11 +164,7 @@
     combined = jnp.einsum(
         "jct,jcd->td", weighted_select, returned, preferred_element_type=F32
     ).astype(BF)
-    shares = lax.all_to_all(
-        combined.reshape(tokens, depth, slice_width).transpose(1, 0, 2),
-        "z", split_axis=0, concat_axis=0, tiled=True,
-    )
-    moe_share = jnp.sum(shares.astype(F32), axis=0)
+    moe_share = sum_slices(combined, depth)
     moe_value = jnp.where(changed[:, None] == 1, moe_share, cached_moe.astype(F32))
     return (mixed_local.astype(F32) + moe_value).astype(BF)
 

time: 308 us -> 261 us (0.85); the launches traced: 303 us -> 260 us
  blocking collectives: 26.3 us -> 160 us
  waiting for transfers between devices: 166 us -> 59.6 us
  starting transfers between devices: 48.7 us -> 13.6 us
  local copies, waits for them, and re-layouts: 32.1 us -> 4.18 us
  matrix products: 9.68 us -> 4.24 us
    all_to_all x1 -> x4, blocking collectives: 26.3 us -> 160 us  [the longest x1 55.2 us: shards(): lax.all_to_all(outgoing, ('x', 'y'), split_axis=0, concat_axis=0, tiled=T...]
    all_to_all x2 -> x1, waiting for transfers between devices: 98.5 us -> 28.4 us  [sum_slices(): lax.all_to_all(slices, 'z', split_axis=0, concat_axis=0, tiled=True)]
    unnamed x49 -> x22, local copies, waits for them, and re-layouts: 25.9 us -> 0.06 us
    ppermute x7 -> x0, starting transfers between devices: 15.5 us -> none  [shards(): lax.ppermute(piece, 'z', [(i, (i + depth - step) % depth) for i in range(...]
    all_to_all x3 -> x1, waiting for transfers between devices: 43.1 us -> 28.6 us  [gather_by_exchange(): return lax.all_to_all(spread, axes, split_axis=0, concat_axis=0, tiled=True)]
    all_to_all x3 -> x1, starting transfers between devices: 16.4 us -> 4.24 us  [gather_by_exchange(): return lax.all_to_all(spread, axes, split_axis=0, concat_axis=0, tiled=True)]
    ppermute x7 -> x0, waiting for transfers between devices: 11.7 us -> none  [shards(): lax.ppermute(piece, 'z', [(i, (i + depth - step) % depth) for i in range(...]
    ppermute x5 -> x4, waiting for transfers between devices: 12.5 us -> 2.67 us  [swap_cores(): return lax.ppermute(array, 'c', [(0, 1), (1, 0)])]
  transfers between devices with their start and end apart: 17 -> 6, of which waited for: 11 -> 3; matrix products, arithmetic and copies ran while one was open for 4% -> 2% of each run, Pallas kernels for 0% -> 0%
where the time goes in v3:
time: 261 us; the launch traced here: 260 us
  blocking collectives  160 us (61%)
  waiting for transfers between devices  59.6 us (23%)
  Pallas kernels  13.7 us (5%)
  starting transfers between devices  13.6 us (5%)
  other arithmetic  4.47 us (2%)
  matrix products  4.24 us (2%)
  local copies, waits for them, and re-layouts  4.18 us (2%)
    all_to_all x1, blocking collectives, shards(): lax.all_to_all(outgoing, ('x', 'y'), split_axis=0, concat_axis=0, tiled=T...  55.2 us
    all_to_all x1, blocking collectives, shards(): lax.all_to_all(partial_out.reshape(arrived.shape), ('x', 'y'), split_axis...  53.1 us
    all_to_all x1, blocking collectives, sum_slices(): lax.all_to_all(slices, 'z', split_axis=0, concat_axis=0, tiled=True)  29.3 us
    all_to_all x1, waiting for transfers between devices, gather_by_exchange(): return lax.all_to_all(spread, axes, split_axis=0, concat_axis=0, tiled=True)  28.6 us
    all_to_all x1, waiting for transfers between devices, sum_slices(): lax.all_to_all(slices, 'z', split_axis=0, concat_axis=0, tiled=True)  28.4 us
    all_to_all x1, blocking collectives, gather_by_exchange(): return lax.all_to_all(spread, axes, split_axis=0, concat_axis=0, tiled=True)  22.5 us
    pallas_call x1, Pallas kernels, expert_partial(): pl.pallas_call(expert_kernel, out_shape=jax.ShapeDtypeStruct((count, dept...  13.7 us
    all_to_all x1, starting transfers between devices, sum_slices(): lax.all_to_all(slices, 'z', split_axis=0, concat_axis=0, tiled=True)  8.61 us
  transfers between devices with their start and end apart: 6, of which 3 were waited for; matrix products, arithmetic and copies ran while one was open for 2% of the time, Pallas kernels for 0%

profile of v3, /device:TPU:6, one launch (start us, length us, event | category | flops | bytes accessed | tf_op | source)
XLA Modules:
  0.0 260.1 jit_solution(603133385321372395)
XLA Ops:
  0.0 0.9 pad_maximum_fusion.1
  1.0 22.5 %all_to_all.30 = bf16[16,128,256]{2,1,0:T(8,128)(2,1)S(1)} all-to-all(bf16[16,128,256]{2,1,0:T(8,128)(2,1)S(1)} %broadcast_in_dim.25), channel_id=1, replica_groups=mesh['x'=4,'y'=4,'c'=2,'z'=8] {'x','y'}, dimensions={0} | all-to-all | bytes 2097152 | tf_op jit(solution)/shard_map/all_to_all | solution.py:22
  23.6 2.7 %collective-permute-done = bf16[16,128,256]{2,1,0:T(8,128)(2,1)S(1)} collective-permute-done((bf16[16,128,256]{2,1,0:T(8,128)(2,1)S(1)}, bf16[16,128,256]{2,1,0:T(8,128)(2,1)S(1)}, u32[]{:S(2)}, u32[]{:S(2)}) %collective-permute-start) | collective-permute-done | bytes 1048608 | tf_op jit(solution)/shard_map/ppermute | solution.py:17
  26.4 0.8 fusion.17
  27.3 0.6 fusion.2
  27.8 0.9 fusion.8
  28.8 0.5 convolution_convert_fusion.1
  29.3 1.1 copy.67
  30.4 8.6 %all-to-all-start.1 = ((bf16[8,128,512]{2,1,0:T(8,128)(2,1)}), bf16[8,128,512]{2,1,0:T(8,128)(2,1)S(1)}, u32[]{:S(2)}, u32[]{:S(2)}) async-start(bf16[8,128,512]{2,1,0:T(8,128)(2,1)} %bitcast.84), calls=%async_computation.1 | async-start | bytes 2097152 | tf_op jit(solution)/shard_map/all_to_all | solution.py:28
  39.1 0.5 collective-permute-start.2
  39.7 28.4 %all-to-all-done.1 = bf16[8,128,512]{2,1,0:T(8,128)(2,1)S(1)} async-done(((bf16[8,128,512]{2,1,0:T(8,128)(2,1)}), bf16[8,128,512]{2,1,0:T(8,128)(2,1)S(1)}, u32[]{:S(2)}, u32[]{:S(2)}) %all-to-all-start.1) | async-done | bytes 1048608 | tf_op jit(solution)/shard_map/all_to_all | solution.py:28
  68.2 1.1 broadcast_in_dim.28
  69.3 4.2 %all-to-all-start.2 = ((bf16[8,128,512]{2,1,0:T(8,128)(2,1)}), bf16[8,128,512]{2,1,0:T(8,128)(2,1)}, u32[]{:S(2)}, u32[]{:S(2)}) async-start(bf16[8,128,512]{2,1,0:T(8,128)(2,1)} %broadcast_in_dim.28), calls=%async_computation.2 | async-start | bytes 2097152 | tf_op jit(solution)/shard_map/all_to_all | solution.py:22
  74.2 28.6 %all-to-all-done.2 = bf16[8,128,512]{2,1,0:T(8,128)(2,1)} async-done(((bf16[8,128,512]{2,1,0:T(8,128)(2,1)}), bf16[8,128,512]{2,1,0:T(8,128)(2,1)}, u32[]{:S(2)}, u32[]{:S(2)}) %all-to-all-start.2) | async-done | bytes 1048608 | tf_op jit(solution)/shard_map/all_to_all | solution.py:22
  102.8 1.6 copy.47
  104.4 0.6 fusion.3
  105.0 0.7 fusion.5
  105.7 1.3 convolution_convert_fusion
  107.1 55.2 %all_to_all.31 = bf16[16,32,4096]{2,1,0:T(8,128)(2,1)S(1)} all-to-all(bf16[16,32,4096]{2,1,0:T(8,128)(2,1)S(1)} %convolution_convert_fusion), channel_id=1, replica_groups=mesh['x'=4,'y'=4,'c'=2,'z'=8] {'x','y'}, dimensions={0} | all-to-all | bytes 8388608 | tf_op jit(solution)/shard_map/all_to_all | solution.py:155
  162.3 13.7 %expert_partial.1 = bf16[512,4096]{1,0:T(8,128)(2,1)S(1)} custom-call(bf16[512,4096]{1,0:T(8,128)(2,1)S(1)} %bitcast.73, bf16[4096,384]{1,0:T(8,128)(2,1)S(1)} %bitcast.76, bf16[4096,384]{1,0:T(8,128)(2,1)S(1)} %bitcast.78, bf16[384,4096]{1,0:T(8,128)(2,1)S(1)} %bitcast.80, bf16[4096,384]{1,0:T(8,128)(2,1)} %collective-permute-done.1.gate_b, ...), custom_call_target="tpu_custom_call" | custom-call | flops 9663676416 | bytes 27262976 | tf_op jit(solution)/shard_map/expert_partial/pallas_call | solution.py:50
  175.9 53.1 %all_to_all.32 = bf16[16,32,4096]{2,1,0:T(8,128)(2,1)S(1)} all-to-all(bf16[16,32,4096]{2,1,0:T(8,128)(2,1)S(1)} %bitcast.74), channel_id=1, replica_groups=mesh['x'=4,'y'=4,'c'=2,'z'=8] {'x','y'}, dimensions={0} | all-to-all | bytes 8388608 | tf_op jit(solution)/shard_map/all_to_all | solution.py:161
  229.1 0.7 fusion.1
  229.9 29.3 %all_to_all.33 = bf16[8,128,512]{2,1,0:T(8,128)(2,1)S(1)} all-to-all(bf16[8,128,512]{2,1,0:T(8,128)(2,1)S(1)} %bitcast.85), channel_id=1, replica_groups=mesh['x'=4,'y'=4,'c'=2,'z'=8] {'z'}, dimensions={0} | all-to-all | bytes 2097152 | tf_op jit(solution)/shard_map/all_to_all | solution.py:28
  259.4 0.8 add_convert_fusion
  (49 shorter events, 1.6 us)
Async XLA Ops:
  0.0 28.8 %copy-start = (bf16[256,4096]{1,0:T(8,128)(2,1)S(1)}, bf16[256,4096]{1,0:T(8,128)(2,1)}, u32[]{:S(2)}) copy-start(bf16[256,4096]{1,0:T(8,128)(2,1)} %param.17) | copy-start | bytes 6291460
  1.0 25.4 %copy-start.6 = (bf16[128,256]{1,0:T(8,128)(2,1)S(1)}, bf16[128,256]{1,0:T(8,128)(2,1)}, u32[]{:S(2)}) copy-start(bf16[128,256]{1,0:T(8,128)(2,1)} %param.14) | copy-start | bytes 196612
  23.6 2.7 %collective-permute-start = (bf16[16,128,256]{2,1,0:T(8,128)(2,1)S(1)}, bf16[16,128,256]{2,1,0:T(8,128)(2,1)S(1)}, u32[]{:S(2)}, u32[]{:S(2)}) collective-permute-start(bf16[16,128,256]{2,1,0:T(8,128)(2,1)S(1)} %all_to_all.30), channel_id=1, source_target_pairs={{0,8},{8,0},{1,9},{9,1},{2,10},{10,2},{3,11},{11,3},{4,12},{12,4},... | collective-permute-start | bytes 3145736 | tf_op jit(solution)/shard_map/ppermute | solution.py:17
  29.3 38.9 %copy-start.4 = (bf16[128,512]{1,0:T(8,128)(2,1)S(1)}, bf16[128,512]{1,0:T(8,128)(2,1)}, u32[]{:S(2)}) copy-start(bf16[128,512]{1,0:T(8,128)(2,1)} %param.13) | copy-start | bytes 393220
  30.4 43.2 %copy-start.7 = (f32[4096]{0:T(1024)S(1)}, f32[4096]{0:T(1024)}, u32[]{:S(2)}) copy-start(f32[4096]{0:T(1024)} %param.18) | copy-start | bytes 49156
  30.4 43.2 %copy-start.8 = (s32[128,8]{0,1:T(8,128)S(1)}, s32[128,8]{0,1:T(8,128)}, u32[]{:S(2)}) copy-start(s32[128,8]{0,1:T(8,128)} %param.19) | copy-start | bytes 12292
  30.4 43.3 %copy-start.10 = (s32[128]{0:T(128)S(1)}, s32[128]{0:T(128)}, u32[]{:S(2)}) copy-start(s32[128]{0:T(128)} %param.21) | copy-start | bytes 1540
  30.4 37.7 %all-to-all-start.1 = ((bf16[8,128,512]{2,1,0:T(8,128)(2,1)}), bf16[8,128,512]{2,1,0:T(8,128)(2,1)S(1)}, u32[]{:S(2)}, u32[]{:S(2)}) async-start(bf16[8,128,512]{2,1,0:T(8,128)(2,1)} %bitcast.84), calls=%async_computation.1 | async-start | bytes 2097152 | tf_op jit(solution)/shard_map/all_to_all | solution.py:28
  39.0 35.1 %copy-start.9 = (bf16[128,8]{0,1:T(8,128)(2,1)S(1)}, bf16[128,8]{0,1:T(8,128)(2,1)}, u32[]{:S(2)}) copy-start(bf16[128,8]{0,1:T(8,128)(2,1)} %param.20) | copy-start | bytes 6148
  39.0 68.0 %collective-permute-start.1 = (bf16[4096,384]{1,0:T(8,128)(2,1)}, bf16[4096,384]{1,0:T(8,128)(2,1)}, u32[]{:S(2)}, u32[]{:S(2)}) collective-permute-start(bf16[4096,384]{1,0:T(8,128)(2,1)} %bitcast.75), channel_id=1, source_target_pairs={{0,8},{8,0},{1,9},{9,1},{2,10},{10,2},{3,11},{11,3},{4,12},{12,4},... | collective-permute-start | bytes 9437192 | tf_op jit(solution)/shard_map/ppermute | solution.py:17
  39.1 67.9 %collective-permute-start.2 = (bf16[4096,384]{1,0:T(8,128)(2,1)}, bf16[4096,384]{1,0:T(8,128)(2,1)}, u32[]{:S(2)}, u32[]{:S(2)}) collective-permute-start(bf16[4096,384]{1,0:T(8,128)(2,1)} %bitcast.77), channel_id=1, source_target_pairs={{0,8},{8,0},{1,9},{9,1},{2,10},{10,2},{3,11},{11,3},{4,12},{12,4},... | collective-permute-start | bytes 9437192 | tf_op jit(solution)/shard_map/ppermute | solution.py:17
  39.6 67.4 %collective-permute-start.3 = (bf16[384,4096]{1,0:T(8,128)(2,1)}, bf16[384,4096]{1,0:T(8,128)(2,1)}, u32[]{:S(2)}, u32[]{:S(2)}) collective-permute-start(bf16[384,4096]{1,0:T(8,128)(2,1)} %bitcast.79), channel_id=1, source_target_pairs={{0,8},{8,0},{1,9},{9,1},{2,10},{10,2},{3,11},{11,3},{4,12},{12,4},... | collective-permute-start | bytes 9437192 | tf_op jit(solution)/shard_map/ppermute | solution.py:17
  69.3 33.5 %all-to-all-start.2 = ((bf16[8,128,512]{2,1,0:T(8,128)(2,1)}), bf16[8,128,512]{2,1,0:T(8,128)(2,1)}, u32[]{:S(2)}, u32[]{:S(2)}) async-start(bf16[8,128,512]{2,1,0:T(8,128)(2,1)} %broadcast_in_dim.28), calls=%async_computation.2 | async-start | bytes 2097152 | tf_op jit(solution)/shard_map/all_to_all | solution.py:22
  105.7 56.5 %copy-start.3 = (bf16[1,384,4096]{2,1,0:T(8,128)(2,1)S(1)}, bf16[1,384,4096]{2,1,0:T(8,128)(2,1)}, u32[]{:S(2)}) copy-start(bf16[1,384,4096]{2,1,0:T(8,128)(2,1)} %param.25) | copy-start | bytes 9437188
  107.0 55.2 %copy-start.1 = (bf16[1,4096,384]{2,1,0:T(8,128)(2,1)S(1)}, bf16[1,4096,384]{2,1,0:T(8,128)(2,1)}, u32[]{:S(2)}) copy-start(bf16[1,4096,384]{2,1,0:T(8,128)(2,1)} %param.23) | copy-start | bytes 9437188
  107.0 55.2 %copy-start.2 = (bf16[1,4096,384]{2,1,0:T(8,128)(2,1)S(1)}, bf16[1,4096,384]{2,1,0:T(8,128)(2,1)}, u32[]{:S(2)}) copy-start(bf16[1,4096,384]{2,1,0:T(8,128)(2,1)} %param.24) | copy-start | bytes 9437188
  229.8 29.6 %copy-start.5 = (bf16[128,512]{1,0:T(8,128)(2,1)S(1)}, bf16[128,512]{1,0:T(8,128)(2,1)}, u32[]{:S(2)}) copy-start(bf16[128,512]{1,0:T(8,128)(2,1)} %param.22) | copy-start | bytes 393220

commit v4 on v3

--- a/solution.py
+++ b/solution.py
@@ -20,6 +20,26 @@
 def gather_by_exchange(array, axes, count):
     spread = jnp.broadcast_to(array[None], (count,) + array.shape)
     return lax.all_to_all(spread, axes, split_axis=0, concat_axis=0, tiled=True)
+
+
+def gather_ring(array, depth):
+    ahead = [(i, (i + 1) % depth) for i in range(depth)]
+    behind = [(i, (i + depth - 1) % depth) for i in range(depth)]
+    half = array.shape[0] // 2
+    from_behind, from_ahead = [array], [array]
+    for step in range(1, depth // 2):
+        from_behind.append(lax.ppermute(from_behind[-1], "z", ahead))
+        from_ahead.append(lax.ppermute(from_ahead[-1], "z", behind))
+    far = jnp.concatenate(
+        [
+            lax.ppermute(from_behind[-1][:half], "z", ahead),
+            lax.ppermute(from_ahead[-1][half:], "z", behind),
+        ],
+        axis=0,
+    )
+    pieces = from_ahead + [far] + from_behind[:0:-1]
+    twice = jnp.stack(pieces + pieces)
+    return lax.dynamic_slice_in_dim(twice, depth - lax.axis_index("z"), depth, 0)
 
 
 def sum_slices(array, depth):
@@ -123,7 +143,7 @@
     attn_share = sum_slices(partial_attn, depth)
     mixed_local = (residual_in.astype(F32) + attn_share).astype(BF)
 
-    mixed_full = gather_by_exchange(mixed_local, "z", depth)
+    mixed_full = gather_ring(mixed_local, depth)
     mixed_full = mixed_full.transpose(1, 0, 2).reshape(tokens, -1)
     mixed_float = mixed_full.astype(F32)
     mean_square = jnp.mean(mixed_float * mixed_float, axis=-1, keepdims=True)

time: 261 us -> 241 us (0.923)
  waiting for transfers between devices: 59.6 us -> 41.7 us
  blocking collectives: 160 us -> 150 us
  starting transfers between devices: 13.6 us -> 22.5 us
    all_to_all x1 -> x0, waiting for transfers between devices: 28.6 us -> none  [gather_by_exchange(): return lax.all_to_all(spread, axes, split_axis=0, concat_axis=0, tiled=True)]
    ppermute x0 -> x8, starting transfers between devices: none -> 13.3 us  [the longest x3 9.14 us: gather_ring(): from_ahead.append(lax.ppermute(from_ahead[-1], 'z', behind))]
    ppermute x0 -> x8, waiting for transfers between devices: none -> 11.2 us  [the longest x3 9.21 us: gather_ring(): from_behind.append(lax.ppermute(from_behind[-1], 'z', ahead))]
    all_to_all x1, blocking collectives: 55.2 us -> 50.7 us  [shards(): lax.all_to_all(outgoing, ('x', 'y'), split_axis=0, concat_axis=0, tiled=T...]
    all_to_all x1 -> x0, starting transfers between devices: 4.24 us -> none  [gather_by_exchange(): return lax.all_to_all(spread, axes, split_axis=0, concat_axis=0, tiled=True)]
    all_to_all x1, blocking collectives: 29.3 us -> 26.4 us  [sum_slices(): lax.all_to_all(slices, 'z', split_axis=0, concat_axis=0, tiled=True)]
    all_to_all x1, blocking collectives: 53.1 us -> 50.5 us  [shards(): lax.all_to_all(partial_out.reshape(arrived.shape), ('x', 'y'), split_axis...]
  transfers between devices with their start and end apart: 6 -> 13, of which waited for: 3 -> 6; matrix products, arithmetic and copies ran while one was open for 2% -> 2% of each run, Pallas kernels for 0% -> 0%
where the time goes in v4:
time: 241 us
  blocking collectives  150 us (62%)
  waiting for transfers between devices  41.7 us (17%)
  starting transfers between devices  22.5 us (9%)
  Pallas kernels  13.7 us (6%)
  matrix products  5.63 us (2%)
  other arithmetic  3.87 us (2%)
  local copies, waits for them, and re-layouts  2.92 us (1%)
    all_to_all x1, blocking collectives, shards(): lax.all_to_all(outgoing, ('x', 'y'), split_axis=0, concat_axis=0, tiled=T...  50.7 us
    all_to_all x1, blocking collectives, shards(): lax.all_to_all(partial_out.reshape(arrived.shape), ('x', 'y'), split_axis...  50.5 us
    all_to_all x1, waiting for transfers between devices, sum_slices(): lax.all_to_all(slices, 'z', split_axis=0, concat_axis=0, tiled=True)  27.9 us
    all_to_all x1, blocking collectives, sum_slices(): lax.all_to_all(slices, 'z', split_axis=0, concat_axis=0, tiled=True)  26.4 us
    all_to_all x1, blocking collectives, gather_by_exchange(): return lax.all_to_all(spread, axes, split_axis=0, concat_axis=0, tiled=True)  22.4 us
    pallas_call x1, Pallas kernels, expert_partial(): pl.pallas_call(expert_kernel, out_shape=jax.ShapeDtypeStruct((count, dept...  13.7 us
    ppermute x3, waiting for transfers between devices, gather_ring(): from_behind.append(lax.ppermute(from_behind[-1], 'z', ahead))  9.21 us
    ppermute x3, starting transfers between devices, gather_ring(): from_ahead.append(lax.ppermute(from_ahead[-1], 'z', behind))  9.14 us
  transfers between devices with their start and end apart: 13, of which 6 were waited for; matrix products, arithmetic and copies ran while one was open for 2% of the time, Pallas kernels for 0%

profile of v4, /device:TPU:6, one launch (start us, length us, event | category | flops | bytes accessed | tf_op | source)
XLA Modules:
  0.0 240.7 jit_solution(14070269564035262553)
XLA Ops:
  0.0 0.9 pad_maximum_fusion.1
  1.0 22.4 %all_to_all.25 = bf16[16,128,256]{2,1,0:T(8,128)(2,1)S(1)} all-to-all(bf16[16,128,256]{2,1,0:T(8,128)(2,1)S(1)} %broadcast_in_dim.23), channel_id=1, replica_groups=mesh['x'=4,'y'=4,'c'=2,'z'=8] {'x','y'}, dimensions={0} | all-to-all | bytes 2097152 | tf_op jit(solution)/shard_map/all_to_all | solution.py:22
  23.4 2.7 %collective-permute-done = bf16[16,128,256]{2,1,0:T(8,128)(2,1)S(1)} collective-permute-done((bf16[16,128,256]{2,1,0:T(8,128)(2,1)S(1)}, bf16[16,128,256]{2,1,0:T(8,128)(2,1)S(1)}, u32[]{:S(2)}, u32[]{:S(2)}) %collective-permute-start) | collective-permute-done | bytes 1048608 | tf_op jit(solution)/shard_map/ppermute | solution.py:17
  26.3 0.9 fusion.20
  27.7 0.9 fusion.8
  29.2 1.1 copy.75
  30.2 8.6 %all-to-all-start.1 = ((bf16[8,128,512]{2,1,0:T(8,128)(2,1)}), bf16[8,128,512]{2,1,0:T(8,128)(2,1)S(1)}, u32[]{:S(2)}, u32[]{:S(2)}) async-start(bf16[8,128,512]{2,1,0:T(8,128)(2,1)} %bitcast.111), calls=%async_computation.1 | async-start | bytes 2097152 | tf_op jit(solution)/shard_map/all_to_all | solution.py:48
  40.0 27.9 %all-to-all-done.1 = bf16[8,128,512]{2,1,0:T(8,128)(2,1)S(1)} async-done(((bf16[8,128,512]{2,1,0:T(8,128)(2,1)}), bf16[8,128,512]{2,1,0:T(8,128)(2,1)S(1)}, u32[]{:S(2)}, u32[]{:S(2)}) %all-to-all-start.1) | async-done | bytes 1048608 | tf_op jit(solution)/shard_map/all_to_all | solution.py:48
  68.7 2.7 %collective-permute-start.1 = (bf16[128,512]{1,0:T(8,128)(2,1)S(1)}, bf16[128,512]{1,0:T(8,128)(2,1)S(1)}, u32[]{:S(2)}, u32[]{:S(2)}) collective-permute-start(bf16[128,512]{1,0:T(8,128)(2,1)S(1)} %get-tuple-element.16), channel_id=1, source_target_pairs={{0,7},{1,0},{2,1},{3,2},{4,3},{5,4},{6,5},{7,6},{8,15},{9,8},{10,9... | collective-permute-start | bytes 393224 | tf_op jit(solution)/shard_map/ppermute | solution.py:32
  71.5 3.4 %collective-permute-done.4 = bf16[128,512]{1,0:T(8,128)(2,1)S(1)} collective-permute-done((bf16[128,512]{1,0:T(8,128)(2,1)S(1)}, bf16[128,512]{1,0:T(8,128)(2,1)S(1)}, u32[]{:S(2)}, u32[]{:S(2)}) %collective-permute-start.4) | collective-permute-done | bytes 131104 | tf_op jit(solution)/shard_map/ppermute | solution.py:31
  74.8 3.2 %collective-permute-start.2 = (bf16[128,512]{1,0:T(8,128)(2,1)S(1)}, bf16[128,512]{1,0:T(8,128)(2,1)S(1)}, u32[]{:S(2)}, u32[]{:S(2)}) collective-permute-start(bf16[128,512]{1,0:T(8,128)(2,1)S(1)} %collective-permute-done.1), channel_id=1, source_target_pairs={{0,7},{1,0},{2,1},{3,2},{4,3},{5,4},{6,5},{7,6},{8,15},{9,8},{10,9... | collective-permute-start | bytes 393224 | tf_op jit(solution)/shard_map/ppermute | solution.py:32
  78.1 2.9 %collective-permute-done.5 = bf16[128,512]{1,0:T(8,128)(2,1)S(1)} collective-permute-done((bf16[128,512]{1,0:T(8,128)(2,1)S(1)}, bf16[128,512]{1,0:T(8,128)(2,1)S(1)}, u32[]{:S(2)}, u32[]{:S(2)}) %collective-permute-start.5) | collective-permute-done | bytes 131104 | tf_op jit(solution)/shard_map/ppermute | solution.py:31
  81.0 3.2 %collective-permute-start.3 = (bf16[128,512]{1,0:T(8,128)(2,1)S(1)}, bf16[128,512]{1,0:T(8,128)(2,1)S(1)}, u32[]{:S(2)}, u32[]{:S(2)}) collective-permute-start(bf16[128,512]{1,0:T(8,128)(2,1)S(1)} %collective-permute-done.2), channel_id=1, source_target_pairs={{0,7},{1,0},{2,1},{3,2},{4,3},{5,4},{6,5},{7,6},{8,15},{9,8},{10,9... | collective-permute-start | bytes 393224 | tf_op jit(solution)/shard_map/ppermute | solution.py:32
  84.2 2.9 %collective-permute-done.6 = bf16[128,512]{1,0:T(8,128)(2,1)S(1)} collective-permute-done((bf16[128,512]{1,0:T(8,128)(2,1)S(1)}, bf16[128,512]{1,0:T(8,128)(2,1)S(1)}, u32[]{:S(2)}, u32[]{:S(2)}) %collective-permute-start.6) | collective-permute-done | bytes 131104 | tf_op jit(solution)/shard_map/ppermute | solution.py:31
  87.2 3.5 %collective-permute-start.8 = (bf16[64,512]{1,0:T(8,128)(2,1)S(1)}, bf16[64,512]{1,0:T(8,128)(2,1)S(1)}, u32[]{:S(2)}, u32[]{:S(2)}) collective-permute-start(bf16[64,512]{1,0:T(8,128)(2,1)S(1)} %slice.19), channel_id=1, source_target_pairs={{0,7},{1,0},{2,1},{3,2},{4,3},{5,4},{6,5},{7,6},{8,15},{9,8},{10,9... | collective-permute-start | bytes 196616 | tf_op jit(solution)/shard_map/ppermute | solution.py:36
  90.7 2.0 collective-permute-done.7
  93.5 1.3 copy.52
  94.9 2.6 %convolution_convert_fusion = bf16[16,32,4096]{2,1,0:T(8,128)(2,1)S(1)} fusion(bf16[16,32,128]{2,1,0:T(8,128)(2,1)S(1)} %bitcast.116, bf16[128,4096,1]{0,1,2:T(8,128)(2,1)} %bitcast.113), kind=kOutput, calls=%fused_computation | convolution fusion | flops 538968064 | bytes 5373952 | tf_op jit(solution)/shard_map/jct,td->jcd/dot_general | solution.py:169
  97.6 50.7 %all_to_all.26 = bf16[16,32,4096]{2,1,0:T(8,128)(2,1)S(1)} all-to-all(bf16[16,32,4096]{2,1,0:T(8,128)(2,1)S(1)} %convolution_convert_fusion), channel_id=1, replica_groups=mesh['x'=4,'y'=4,'c'=2,'z'=8] {'x','y'}, dimensions={0} | all-to-all | bytes 8388608 | tf_op jit(solution)/shard_map/all_to_all | solution.py:175
  148.3 13.7 %expert_partial.1 = bf16[512,4096]{1,0:T(8,128)(2,1)S(1)} custom-call(bf16[512,4096]{1,0:T(8,128)(2,1)S(1)} %bitcast.100, bf16[4096,384]{1,0:T(8,128)(2,1)S(1)} %bitcast.103, bf16[4096,384]{1,0:T(8,128)(2,1)S(1)} %bitcast.105, bf16[384,4096]{1,0:T(8,128)(2,1)S(1)} %bitcast.107, bf16[4096,384]{1,0:T(8,128)(2,1)} %collective-permute-done.9.gate_b, ...), custom_call_target="tpu_custom_call" | custom-call | flops 9663676416 | bytes 27262976 | tf_op jit(solution)/shard_map/expert_partial/pallas_call | solution.py:70
  162.0 50.5 %all_to_all.27 = bf16[16,32,4096]{2,1,0:T(8,128)(2,1)S(1)} all-to-all(bf16[16,32,4096]{2,1,0:T(8,128)(2,1)S(1)} %bitcast.101), channel_id=1, replica_groups=mesh['x'=4,'y'=4,'c'=2,'z'=8] {'x','y'}, dimensions={0} | all-to-all | bytes 8388608 | tf_op jit(solution)/shard_map/all_to_all | solution.py:181
  212.5 0.7 fusion.1
  213.3 26.4 %all_to_all.28 = bf16[8,128,512]{2,1,0:T(8,128)(2,1)S(1)} all-to-all(bf16[8,128,512]{2,1,0:T(8,128)(2,1)S(1)} %bitcast.112), channel_id=1, replica_groups=mesh['x'=4,'y'=4,'c'=2,'z'=8] {'z'}, dimensions={0} | all-to-all | bytes 2097152 | tf_op jit(solution)/shard_map/all_to_all | solution.py:48
  239.9 0.8 add_convert_fusion
  (79 shorter events, 4.5 us)
Async XLA Ops:
  0.0 28.6 %copy-start = (bf16[256,4096]{1,0:T(8,128)(2,1)S(1)}, bf16[256,4096]{1,0:T(8,128)(2,1)}, u32[]{:S(2)}) copy-start(bf16[256,4096]{1,0:T(8,128)(2,1)} %param.17) | copy-start | bytes 6291460
  23.4 2.9 %copy-start.6 = (bf16[128,256]{1,0:T(8,128)(2,1)S(1)}, bf16[128,256]{1,0:T(8,128)(2,1)}, u32[]{:S(2)}) copy-start(bf16[128,256]{1,0:T(8,128)(2,1)} %param.14) | copy-start | bytes 196612
  23.4 2.7 %collective-permute-start = (bf16[16,128,256]{2,1,0:T(8,128)(2,1)S(1)}, bf16[16,128,256]{2,1,0:T(8,128)(2,1)S(1)}, u32[]{:S(2)}, u32[]{:S(2)}) collective-permute-start(bf16[16,128,256]{2,1,0:T(8,128)(2,1)S(1)} %all_to_all.25), channel_id=1, source_target_pairs={{0,8},{8,0},{1,9},{9,1},{2,10},{10,2},{3,11},{11,3},{4,12},{12,4},... | collective-permute-start | bytes 3145736 | tf_op jit(solution)/shard_map/ppermute | solution.py:17
  29.1 10.3 %copy-start.7 = (f32[4096]{0:T(1024)S(1)}, f32[4096]{0:T(1024)}, u32[]{:S(2)}) copy-start(f32[4096]{0:T(1024)} %param.18) | copy-start | bytes 49156
  29.1 10.3 %copy-start.8 = (s32[128,8]{0,1:T(8,128)S(1)}, s32[128,8]{0,1:T(8,128)}, u32[]{:S(2)}) copy-start(s32[128,8]{0,1:T(8,128)} %param.19) | copy-start | bytes 12292
  29.2 10.4 %copy-start.10 = (s32[128]{0:T(128)S(1)}, s32[128]{0:T(128)}, u32[]{:S(2)}) copy-start(s32[128]{0:T(128)} %param.21) | copy-start | bytes 1540
  29.2 10.7 %copy-start.9 = (bf16[128,8]{0,1:T(8,128)(2,1)S(1)}, bf16[128,8]{0,1:T(8,128)(2,1)}, u32[]{:S(2)}) copy-start(bf16[128,8]{0,1:T(8,128)(2,1)} %param.20) | copy-start | bytes 6148
  30.2 37.8 %copy-start.4 = (bf16[128,512]{1,0:T(8,128)(2,1)S(1)}, bf16[128,512]{1,0:T(8,128)(2,1)}, u32[]{:S(2)}) copy-start(bf16[128,512]{1,0:T(8,128)(2,1)} %param.13) | copy-start | bytes 393220
  30.2 37.7 %all-to-all-start.1 = ((bf16[8,128,512]{2,1,0:T(8,128)(2,1)}), bf16[8,128,512]{2,1,0:T(8,128)(2,1)S(1)}, u32[]{:S(2)}, u32[]{:S(2)}) async-start(bf16[8,128,512]{2,1,0:T(8,128)(2,1)} %bitcast.111), calls=%async_computation.1 | async-start | bytes 2097152 | tf_op jit(solution)/shard_map/all_to_all | solution.py:48
  38.8 58.7 %collective-permute-start.9 = (bf16[4096,384]{1,0:T(8,128)(2,1)}, bf16[4096,384]{1,0:T(8,128)(2,1)}, u32[]{:S(2)}, u32[]{:S(2)}) collective-permute-start(bf16[4096,384]{1,0:T(8,128)(2,1)} %bitcast.102), channel_id=1, source_target_pairs={{0,8},{8,0},{1,9},{9,1},{2,10},{10,2},{3,11},{11,3},{4,12},{12,4},... | collective-permute-start | bytes 9437192 | tf_op jit(solution)/shard_map/ppermute | solution.py:17
  38.9 58.7 %collective-permute-start.10 = (bf16[4096,384]{1,0:T(8,128)(2,1)}, bf16[4096,384]{1,0:T(8,128)(2,1)}, u32[]{:S(2)}, u32[]{:S(2)}) collective-permute-start(bf16[4096,384]{1,0:T(8,128)(2,1)} %bitcast.104), channel_id=1, source_target_pairs={{0,8},{8,0},{1,9},{9,1},{2,10},{10,2},{3,11},{11,3},{4,12},{12,4},... | collective-permute-start | bytes 9437192 | tf_op jit(solution)/shard_map/ppermute | solution.py:17
  39.4 58.2 %collective-permute-start.11 = (bf16[384,4096]{1,0:T(8,128)(2,1)}, bf16[384,4096]{1,0:T(8,128)(2,1)}, u32[]{:S(2)}, u32[]{:S(2)}) collective-permute-start(bf16[384,4096]{1,0:T(8,128)(2,1)} %bitcast.106), channel_id=1, source_target_pairs={{0,8},{8,0},{1,9},{9,1},{2,10},{10,2},{3,11},{11,3},{4,12},{12,4},... | collective-permute-start | bytes 9437192 | tf_op jit(solution)/shard_map/ppermute | solution.py:17
  68.1 6.7 %collective-permute-start.4 = (bf16[128,512]{1,0:T(8,128)(2,1)S(1)}, bf16[128,512]{1,0:T(8,128)(2,1)S(1)}, u32[]{:S(2)}, u32[]{:S(2)}) collective-permute-start(bf16[128,512]{1,0:T(8,128)(2,1)S(1)} %get-tuple-element.16), channel_id=1, source_target_pairs={{0,1},{1,2},{2,3},{3,4},{4,5},{5,6},{6,7},{7,0},{8,9},{9,10},{10,1... | collective-permute-start | bytes 393224 | tf_op jit(solution)/shard_map/ppermute | solution.py:31
  68.7 6.1 %collective-permute-start.1 = (bf16[128,512]{1,0:T(8,128)(2,1)S(1)}, bf16[128,512]{1,0:T(8,128)(2,1)S(1)}, u32[]{:S(2)}, u32[]{:S(2)}) collective-permute-start(bf16[128,512]{1,0:T(8,128)(2,1)S(1)} %get-tuple-element.16), channel_id=1, source_target_pairs={{0,7},{1,0},{2,1},{3,2},{4,3},{5,4},{6,5},{7,6},{8,15},{9,8},{10,9... | collective-permute-start | bytes 393224 | tf_op jit(solution)/shard_map/ppermute | solution.py:32
  74.8 6.2 %collective-permute-start.5 = (bf16[128,512]{1,0:T(8,128)(2,1)S(1)}, bf16[128,512]{1,0:T(8,128)(2,1)S(1)}, u32[]{:S(2)}, u32[]{:S(2)}) collective-permute-start(bf16[128,512]{1,0:T(8,128)(2,1)S(1)} %collective-permute-done.4), channel_id=1, source_target_pairs={{0,1},{1,2},{2,3},{3,4},{4,5},{5,6},{6,7},{7,0},{8,9},{9,10},{10,1... | collective-permute-start | bytes 393224 | tf_op jit(solution)/shard_map/ppermute | solution.py:31
  74.8 6.2 %collective-permute-start.2 = (bf16[128,512]{1,0:T(8,128)(2,1)S(1)}, bf16[128,512]{1,0:T(8,128)(2,1)S(1)}, u32[]{:S(2)}, u32[]{:S(2)}) collective-permute-start(bf16[128,512]{1,0:T(8,128)(2,1)S(1)} %collective-permute-done.1), channel_id=1, source_target_pairs={{0,7},{1,0},{2,1},{3,2},{4,3},{5,4},{6,5},{7,6},{8,15},{9,8},{10,9... | collective-permute-start | bytes 393224 | tf_op jit(solution)/shard_map/ppermute | solution.py:32
  81.0 6.2 %collective-permute-start.6 = (bf16[128,512]{1,0:T(8,128)(2,1)S(1)}, bf16[128,512]{1,0:T(8,128)(2,1)S(1)}, u32[]{:S(2)}, u32[]{:S(2)}) collective-permute-start(bf16[128,512]{1,0:T(8,128)(2,1)S(1)} %collective-permute-done.5), channel_id=1, source_target_pairs={{0,1},{1,2},{2,3},{3,4},{4,5},{5,6},{6,7},{7,0},{8,9},{9,10},{10,1... | collective-permute-start | bytes 393224 | tf_op jit(solution)/shard_map/ppermute | solution.py:31
  81.0 6.2 %collective-permute-start.3 = (bf16[128,512]{1,0:T(8,128)(2,1)S(1)}, bf16[128,512]{1,0:T(8,128)(2,1)S(1)}, u32[]{:S(2)}, u32[]{:S(2)}) collective-permute-start(bf16[128,512]{1,0:T(8,128)(2,1)S(1)} %collective-permute-done.2), channel_id=1, source_target_pairs={{0,7},{1,0},{2,1},{3,2},{4,3},{5,4},{6,5},{7,6},{8,15},{9,8},{10,9... | collective-permute-start | bytes 393224 | tf_op jit(solution)/shard_map/ppermute | solution.py:32
  87.2 5.5 %collective-permute-start.7 = (bf16[64,512]{1,0:T(8,128)(2,1)S(1)}, bf16[64,512]{1,0:T(8,128)(2,1)S(1)}, u32[]{:S(2)}, u32[]{:S(2)}) collective-permute-start(bf16[64,512]{1,0:T(8,128)(2,1)S(1)} %slice.18), channel_id=1, source_target_pairs={{0,1},{1,2},{2,3},{3,4},{4,5},{5,6},{6,7},{7,0},{8,9},{9,10},{10,1... | collective-permute-start | bytes 196616 | tf_op jit(solution)/shard_map/ppermute | solution.py:35
  87.2 5.4 %collective-permute-start.8 = (bf16[64,512]{1,0:T(8,128)(2,1)S(1)}, bf16[64,512]{1,0:T(8,128)(2,1)S(1)}, u32[]{:S(2)}, u32[]{:S(2)}) collective-permute-start(bf16[64,512]{1,0:T(8,128)(2,1)S(1)} %slice.19), channel_id=1, source_target_pairs={{0,7},{1,0},{2,1},{3,2},{4,3},{5,4},{6,5},{7,6},{8,15},{9,8},{10,9... | collective-permute-start | bytes 196616 | tf_op jit(solution)/shard_map/ppermute | solution.py:36
  94.8 53.5 %copy-start.3 = (bf16[1,384,4096]{2,1,0:T(8,128)(2,1)S(1)}, bf16[1,384,4096]{2,1,0:T(8,128)(2,1)}, u32[]{:S(2)}) copy-start(bf16[1,384,4096]{2,1,0:T(8,128)(2,1)} %param.25) | copy-start | bytes 9437188
  97.6 50.8 %copy-start.1 = (bf16[1,4096,384]{2,1,0:T(8,128)(2,1)S(1)}, bf16[1,4096,384]{2,1,0:T(8,128)(2,1)}, u32[]{:S(2)}) copy-start(bf16[1,4096,384]{2,1,0:T(8,128)(2,1)} %param.23) | copy-start | bytes 9437188
  97.6 50.8 %copy-start.2 = (bf16[1,4096,384]{2,1,0:T(8,128)(2,1)S(1)}, bf16[1,4096,384]{2,1,0:T(8,128)(2,1)}, u32[]{:S(2)}) copy-start(bf16[1,4096,384]{2,1,0:T(8,128)(2,1)} %param.24) | copy-start | bytes 9437188
  213.3 26.6 %copy-start.5 = (bf16[128,512]{1,0:T(8,128)(2,1)S(1)}, bf16[128,512]{1,0:T(8,128)(2,1)}, u32[]{:S(2)}) copy-start(bf16[128,512]{1,0:T(8,128)(2,1)} %param.22) | copy-start | bytes 393220

commit v5 on v4

--- a/solution.py
+++ b/solution.py
@@ -11,6 +11,8 @@
 BF = jnp.bfloat16
 F32 = jnp.float32
 PIECES = 4
+AHEAD = 2
+EIGHTHS = (0, 2, 4, 6, 8)
 
 
 def swap_cores(array):
@@ -42,51 +44,117 @@
     return lax.dynamic_slice_in_dim(twice, depth - lax.axis_index("z"), depth, 0)
 
 
-def sum_slices(array, depth):
+def sum_ring(array, depth):
     tokens, width = array.shape
-    slices = array.reshape(tokens, depth, width // depth).transpose(1, 0, 2)
-    shares = lax.all_to_all(slices, "z", split_axis=0, concat_axis=0, tiled=True)
-    return jnp.sum(shares.astype(F32), axis=0)
+    width //= depth
+    half = tokens // 2
+    here = lax.axis_index("z")
+    ahead = [(i, (i + 1) % depth) for i in range(depth)]
+    behind = [(i, (i + depth - 1) % depth) for i in range(depth)]
+
+    def own(offset):
+        start = lax.rem(here + offset, depth) * width
+        return lax.dynamic_slice_in_dim(array, start, width, 1)
+
+    def add(mine, arrived):
+        return (mine.astype(F32) + arrived.astype(F32)).astype(BF)
+
+    far = own(depth // 2)
+    forward = lax.ppermute(far[:half], "z", ahead)
+    backward = lax.ppermute(far[half:], "z", behind)
+    for offset in range(depth // 2 - 1, 0, -1):
+        mine, other = own(offset), own(depth - offset)
+        if offset == depth // 2 - 1:
+            forward = jnp.concatenate([add(mine[:half], forward), mine[half:]], axis=0)
+            backward = jnp.concatenate([other[:half], add(other[half:], backward)], axis=0)
+        else:
+            forward, backward = add(mine, forward), add(other, backward)
+        forward = lax.ppermute(forward, "z", ahead)
+        backward = lax.ppermute(backward, "z", behind)
+    return own(0).astype(F32) + forward.astype(F32) + backward.astype(F32)
 
 
 def expert_kernel(
-    rows, gate_a, up_a, down_a, gate_b, up_b, down_b, out, gate_out, hidden
+    rows, gate_a, up_a, down_a, gate_b, up_b, down_b, out,
+    gates, ups, downs, totals, hidden, in_sem, down_sem,
 ):
-    width = down_a.shape[1] // PIECES
-    gates = jnp.concatenate([gate_a[...], gate_b[...]], axis=1)
-    gate_out[...] = jnp.dot(rows[...], gates, preferred_element_type=F32)
-    ups = jnp.concatenate([up_a[...], up_b[...]], axis=1)
-    up_out = jnp.dot(rows[...], ups, preferred_element_type=F32)
-    hidden[...] = (jax.nn.silu(gate_out[...]) * up_out).astype(BF)
+    part = gate_a.shape[1]
+    depth = gate_a.shape[0]
+    width = depth // PIECES
+    bounds = [depth * eighth // 8 for eighth in EIGHTHS]
+    steps = len(bounds) - 1
+
+    def in_copies(step):
+        here = pl.ds(bounds[step], bounds[step + 1] - bounds[step])
+        return [
+            pltpu.make_async_copy(part_ref.at[here], store.at[which, here], in_sem.at[2 * which + kind, step])
+            for which, pair in enumerate(((gate_a, up_a), (gate_b, up_b)))
+            for kind, (part_ref, store) in enumerate(zip(pair, (gates, ups)))
+        ]
+
+    def down_copies():
+        return [
+            pltpu.make_async_copy(down, downs.at[pl.ds(which * part, part)], down_sem.at[which])
+            for which, down in enumerate((down_a, down_b))
+        ]
+
+    def start(step):
+        copies = in_copies(step) if step < steps else down_copies() if step == steps else []
+        for copy in copies:
+            copy.start()
+
+    for step in range(AHEAD):
+        start(step)
+    for step in range(steps):
+        start(step + AHEAD)
+        for copy in in_copies(step):
+            copy.wait()
+        here = pl.ds(bounds[step], bounds[step + 1] - bounds[step])
+        weights = jnp.concatenate(
+            [gates[0, here], gates[1, here], ups[0, here], ups[1, here]], axis=1
+        )
+        product = jnp.dot(rows[:, here], weights, preferred_element_type=F32)
+        if step:
+            product += totals[...]
+        if step < steps - 1:
+            totals[...] = product
+    gate_out, up_out = product[:, : 2 * part], product[:, 2 * part :]
+    hidden[...] = (jax.nn.silu(gate_out) * up_out).astype(BF)
+    for copy in down_copies():
+        copy.wait()
     for piece in range(PIECES):
         columns = pl.ds(piece * width, width)
-        down = jnp.concatenate([down_a[:, columns], down_b[:, columns]], axis=0)
-        out[:, columns] = jnp.dot(hidden[...], down, preferred_element_type=F32).astype(BF)
-
-
-def expert_partial(rows, gate_a, up_a, down_a, gate_b, up_b, down_b):
+        out[:, columns] = jnp.dot(
+            hidden[...], downs[:, columns], preferred_element_type=F32
+        ).astype(BF)
+
+
+def expert_partial(rows, *parts):
     count, depth = rows.shape
-    part = gate_a.shape[1]
+    part = parts[0].shape[1]
     return pl.pallas_call(
         expert_kernel,
         out_shape=jax.ShapeDtypeStruct((count, depth), BF),
-        in_specs=[pl.BlockSpec(memory_space=pltpu.VMEM)] * 7,
+        in_specs=[pl.BlockSpec(memory_space=pltpu.VMEM)]
+        + [pl.BlockSpec(memory_space=pl.ANY)] * len(parts),
         out_specs=pl.BlockSpec(memory_space=pltpu.VMEM),
         scratch_shapes=[
-            pltpu.VMEM((count, 2 * part), F32),
+            pltpu.VMEM((2, depth, part), BF),
+            pltpu.VMEM((2, depth, part), BF),
+            pltpu.VMEM((2 * part, depth), BF),
+            pltpu.VMEM((count, 4 * part), F32),
             pltpu.VMEM((count, 2 * part), BF),
+            pltpu.SemaphoreType.DMA((4, len(EIGHTHS) - 1)),
+            pltpu.SemaphoreType.DMA((2,)),
         ],
-        compiler_params=pltpu.CompilerParams(vmem_limit_bytes=16 * 2**20),
+        compiler_params=pltpu.CompilerParams(vmem_limit_bytes=40 * 2**20),
         cost_estimate=pl.CostEstimate(
             flops=12 * count * depth * part,
             bytes_accessed=12 * depth * part + 4 * count * depth,
             transcendentals=2 * count * part,
         ),
         name="expert_partial",
-    )(*[
-        pltpu.with_memory_space_constraint(operand, pltpu.VMEM)
-        for operand in (rows, gate_a, up_a, down_a, gate_b, up_b, down_b)
-    ])
+    )(pltpu.with_memory_space_constraint(rows, pltpu.VMEM), *parts)
 
 
 def attention(queries, all_kv, kv_local):
@@ -132,15 +200,11 @@
     all_kv = jnp.concatenate([own_kv, swap_cores(own_kv)], axis=0)
     all_kv = all_kv.reshape(-1, all_kv.shape[-1])
 
-    gate_other, up_other, down_other = (
-        swap_cores(gate_proj[0]),
-        swap_cores(up_proj[0]),
-        swap_cores(down_proj[0]),
-    )
+    other_parts = tuple(swap_cores(part[0]) for part in (gate_proj, up_proj, down_proj))
 
     attended = attention(queries, all_kv, key_heads.shape[1] // HD)
     partial_attn = jnp.dot(attended, out_proj, preferred_element_type=F32).astype(BF)
-    attn_share = sum_slices(partial_attn, depth)
+    attn_share = sum_ring(partial_attn, depth)
     mixed_local = (residual_in.astype(F32) + attn_share).astype(BF)
 
     mixed_full = gather_ring(mixed_local, depth)
@@ -169,22 +233,21 @@
     outgoing = jnp.einsum(
         "jct,td->jcd", selector, normed, preferred_element_type=F32
     ).astype(BF)
-    outgoing, gate_other, up_other, down_other, weighted_select = lax.optimization_barrier(
-        (outgoing, gate_other, up_other, down_other, weighted_select)
+    own_parts = (gate_proj[0], up_proj[0], down_proj[0])
+    outgoing, own_parts, other_parts, weighted_select = lax.optimization_barrier(
+        (outgoing, own_parts, other_parts, weighted_select)
     )
     arrived = lax.all_to_all(outgoing, ("x", "y"), split_axis=0, concat_axis=0, tiled=True)
     rows = arrived.reshape(-1, arrived.shape[-1])
 
-    partial_out = expert_partial(
-        rows, gate_proj[0], up_proj[0], down_proj[0], gate_other, up_other, down_other
-    )
+    partial_out = expert_partial(rows, *own_parts, *other_parts)
     returned = lax.all_to_all(
         partial_out.reshape(arrived.shape), ("x", "y"), split_axis=0, concat_axis=0, tiled=True
     )
     combined = jnp.einsum(
         "jct,jcd->td", weighted_select, returned, preferred_element_type=F32
     ).astype(BF)
-    moe_share = sum_slices(combined, depth)
+    moe_share = sum_ring(combined, depth)
     moe_value = jnp.where(changed[:, None] == 1, moe_share, cached_moe.astype(F32))
     return (mixed_local.astype(F32) + moe_value).astype(BF)
 

time: 241 us -> 230 us (0.954)
  blocking collectives: 150 us -> 108 us
  starting transfers between devices: 22.5 us -> 38.8 us
  other arithmetic: 3.87 us -> 11 us
  waiting for transfers between devices: 41.7 us -> 46.2 us
    ppermute x0 -> x16, waiting for transfers between devices: none -> 32.9 us  [the longest x6 16.6 us: sum_ring(): forward = lax.ppermute(forward, 'z', ahead)]
    all_to_all x1 -> x0, waiting for transfers between devices: 27.9 us -> none  [sum_slices(): lax.all_to_all(slices, 'z', split_axis=0, concat_axis=0, tiled=True)]
    all_to_all x1 -> x0, blocking collectives: 26.4 us -> none  [sum_slices(): lax.all_to_all(slices, 'z', split_axis=0, concat_axis=0, tiled=True)]
    ppermute x0 -> x16, starting transfers between devices: none -> 24.6 us  [the longest x6 9.11 us: sum_ring(): backward = lax.ppermute(backward, 'z', behind)]
    all_to_all x1 -> x0, starting transfers between devices: 8.6 us -> none  [sum_slices(): lax.all_to_all(slices, 'z', split_axis=0, concat_axis=0, tiled=True)]
    all_to_all x1, blocking collectives: 50.5 us -> 42.8 us  [shards(): lax.all_to_all(partial_out.reshape(arrived.shape), ('x', 'y'), split_axis...]
    all_to_all x1, blocking collectives: 50.7 us -> 43.2 us  [shards(): lax.all_to_all(outgoing, ('x', 'y'), split_axis=0, concat_axis=0, tiled=T...]
  transfers between devices with their start and end apart: 13 -> 28, of which waited for: 6 -> 16; matrix products, arithmetic and copies ran while one was open for 2% -> 7% of each run, Pallas kernels for 0% -> 0%
where the time goes in v5:
time: 230 us; the launch traced here: 228 us
  blocking collectives  108 us (47%)
  waiting for transfers between devices  46.2 us (20%)
  starting transfers between devices  38.8 us (17%)
  Pallas kernels  14.4 us (6%)
  other arithmetic  11 us (5%)
  matrix products  5.49 us (2%)
  local copies, waits for them, and re-layouts  3.17 us (1%)
    all_to_all x1, blocking collectives, shards(): lax.all_to_all(outgoing, ('x', 'y'), split_axis=0, concat_axis=0, tiled=T...  43.2 us
    all_to_all x1, blocking collectives, shards(): lax.all_to_all(partial_out.reshape(arrived.shape), ('x', 'y'), split_axis...  42.8 us
    all_to_all x1, blocking collectives, gather_by_exchange(): return lax.all_to_all(spread, axes, split_axis=0, concat_axis=0, tiled=True)  22.4 us
    ppermute x6, waiting for transfers between devices, sum_ring(): forward = lax.ppermute(forward, 'z', ahead)  16.6 us
    pallas_call x1, Pallas kernels, expert_partial(): pl.pallas_call(expert_kernel, out_shape=jax.ShapeDtypeStruct((count, dept...  14.4 us
    ppermute x6, waiting for transfers between devices, sum_ring(): backward = lax.ppermute(backward, 'z', behind)  11.8 us
    ppermute x3, starting transfers between devices, gather_ring(): from_ahead.append(lax.ppermute(from_ahead[-1], 'z', behind))  9.78 us
    ppermute x6, starting transfers between devices, sum_ring(): backward = lax.ppermute(backward, 'z', behind)  9.11 us
  transfers between devices with their start and end apart: 28, of which 16 were waited for; matrix products, arithmetic and copies ran while one was open for 7% of the time, Pallas kernels for 0%

profile of v5, /device:TPU:6, one launch (start us, length us, event | category | flops | bytes accessed | tf_op | source)
XLA Modules:
  0.0 227.9 jit_solution(18128241490384320166)
XLA Ops:
  1.1 22.4 %all_to_all.15 = bf16[16,128,256]{2,1,0:T(8,128)(2,1)S(1)} all-to-all(bf16[16,128,256]{2,1,0:T(8,128)(2,1)S(1)} %broadcast_in_dim.23), channel_id=1, replica_groups=mesh['x'=4,'y'=4,'c'=2,'z'=8] {'x','y'}, dimensions={0} | all-to-all | bytes 2097152 | tf_op jit(solution)/shard_map/all_to_all | solution.py:24
  24.5 3.2 %collective-permute-done = bf16[16,128,256]{2,1,0:T(8,128)(2,1)} collective-permute-done((bf16[16,128,256]{2,1,0:T(8,128)(2,1)S(1)}, bf16[16,128,256]{2,1,0:T(8,128)(2,1)}, u32[]{:S(2)}, u32[]{:S(2)}) %collective-permute-start) | collective-permute-done | bytes 1048608 | tf_op jit(solution)/shard_map/ppermute | solution.py:19
  34.0 4.0 %collective-permute-start.5 = (bf16[64,512]{1,0:T(8,128)(2,1)S(1)}, bf16[64,512]{1,0:T(8,128)(2,1)S(1)}, u32[]{:S(2)}, u32[]{:S(2)}) collective-permute-start(bf16[64,512]{1,0:T(8,128)(2,1)S(1)} %get-tuple-element.37), channel_id=1, source_target_pairs={{0,7},{1,0},{2,1},{3,2},{4,3},{5,4},{6,5},{7,6},{8,15},{9,8},{10,9... | collective-permute-start | bytes 196616 | tf_op jit(solution)/shard_map/ppermute | solution.py:64
  38.1 2.3 %collective-permute-done.1 = bf16[64,512]{1,0:T(8,128)(2,1)S(1)} collective-permute-done((bf16[64,512]{1,0:T(8,128)(2,1)S(1)}, bf16[64,512]{1,0:T(8,128)(2,1)S(1)}, u32[]{:S(2)}, u32[]{:S(2)}) %collective-permute-start.1) | collective-permute-done | bytes 65568 | tf_op jit(solution)/shard_map/ppermute | solution.py:63
  41.3 3.2 %collective-permute-start.6 = (bf16[128,512]{1,0:T(8,128)(2,1)}, bf16[128,512]{1,0:T(8,128)(2,1)}, u32[]{:S(2)}, u32[]{:S(2)}) collective-permute-start(bf16[128,512]{1,0:T(8,128)(2,1)} %pad_maximum_fusion.2), channel_id=1, source_target_pairs={{0,7},{1,0},{2,1},{3,2},{4,3},{5,4},{6,5},{7,6},{8,15},{9,8},{10,9... | collective-permute-start | bytes 393224 | tf_op jit(solution)/shard_map/ppermute | solution.py:73
  44.5 2.2 collective-permute-done.2
  47.7 5.4 %collective-permute-done.3 = bf16[128,512]{1,0:T(8,128)(2,1)} collective-permute-done((bf16[128,512]{1,0:T(8,128)(2,1)S(1)}, bf16[128,512]{1,0:T(8,128)(2,1)}, u32[]{:S(2)}, u32[]{:S(2)}) %collective-permute-start.3) | collective-permute-done | bytes 131104 | tf_op jit(solution)/shard_map/ppermute | solution.py:72
  63.9 3.8 %collective-permute-done.8 = bf16[128,512]{1,0:T(8,128)(2,1)S(1)} collective-permute-done((bf16[128,512]{1,0:T(8,128)(2,1)S(1)}, bf16[128,512]{1,0:T(8,128)(2,1)S(1)}, u32[]{:S(2)}, u32[]{:S(2)}) %collective-permute-start.8) | collective-permute-done | bytes 131104 | tf_op jit(solution)/shard_map/ppermute | solution.py:73
  68.8 3.2 %collective-permute-start.9 = (bf16[128,512]{1,0:T(8,128)(2,1)S(1)}, bf16[128,512]{1,0:T(8,128)(2,1)S(1)}, u32[]{:S(2)}, u32[]{:S(2)}) collective-permute-start(bf16[128,512]{1,0:T(8,128)(2,1)S(1)} %get-tuple-element.22), channel_id=1, source_target_pairs={{0,7},{1,0},{2,1},{3,2},{4,3},{5,4},{6,5},{7,6},{8,15},{9,8},{10,9... | collective-permute-start | bytes 393224 | tf_op jit(solution)/shard_map/ppermute | solution.py:34
  74.9 3.2 %collective-permute-start.10 = (bf16[128,512]{1,0:T(8,128)(2,1)S(1)}, bf16[128,512]{1,0:T(8,128)(2,1)S(1)}, u32[]{:S(2)}, u32[]{:S(2)}) collective-permute-start(bf16[128,512]{1,0:T(8,128)(2,1)S(1)} %collective-permute-done.9), channel_id=1, source_target_pairs={{0,7},{1,0},{2,1},{3,2},{4,3},{5,4},{6,5},{7,6},{8,15},{9,8},{10,9... | collective-permute-start | bytes 393224 | tf_op jit(solution)/shard_map/ppermute | solution.py:34
  78.2 2.9 %collective-permute-done.13 = bf16[128,512]{1,0:T(8,128)(2,1)S(1)} collective-permute-done((bf16[128,512]{1,0:T(8,128)(2,1)S(1)}, bf16[128,512]{1,0:T(8,128)(2,1)S(1)}, u32[]{:S(2)}, u32[]{:S(2)}) %collective-permute-start.13) | collective-permute-done | bytes 131104 | tf_op jit(solution)/shard_map/ppermute | solution.py:33
  81.1 3.3 %collective-permute-start.11 = (bf16[128,512]{1,0:T(8,128)(2,1)S(1)}, bf16[128,512]{1,0:T(8,128)(2,1)S(1)}, u32[]{:S(2)}, u32[]{:S(2)}) collective-permute-start(bf16[128,512]{1,0:T(8,128)(2,1)S(1)} %collective-permute-done.10), channel_id=1, source_target_pairs={{0,7},{1,0},{2,1},{3,2},{4,3},{5,4},{6,5},{7,6},{8,15},{9,8},{10,9... | collective-permute-start | bytes 393224 | tf_op jit(solution)/shard_map/ppermute | solution.py:34
  84.5 2.8 %collective-permute-done.14 = bf16[128,512]{1,0:T(8,128)(2,1)S(1)} collective-permute-done((bf16[128,512]{1,0:T(8,128)(2,1)S(1)}, bf16[128,512]{1,0:T(8,128)(2,1)S(1)}, u32[]{:S(2)}, u32[]{:S(2)}) %collective-permute-start.14) | collective-permute-done | bytes 131104 | tf_op jit(solution)/shard_map/ppermute | solution.py:33
  87.3 3.3 %collective-permute-start.16 = (bf16[64,512]{1,0:T(8,128)(2,1)S(1)}, bf16[64,512]{1,0:T(8,128)(2,1)S(1)}, u32[]{:S(2)}, u32[]{:S(2)}) collective-permute-start(bf16[64,512]{1,0:T(8,128)(2,1)S(1)} %slice.67), channel_id=1, source_target_pairs={{0,7},{1,0},{2,1},{3,2},{4,3},{5,4},{6,5},{7,6},{8,15},{9,8},{10,9... | collective-permute-start | bytes 196616 | tf_op jit(solution)/shard_map/ppermute | solution.py:38
  95.0 2.5 %convolution_convert_fusion = bf16[16,32,4096]{2,1,0:T(8,128)(2,1)S(1)} fusion(bf16[16,32,128]{2,1,0:T(8,128)(2,1)S(1)} %bitcast.92, bf16[128,4096,1]{0,1,2:T(8,128)(2,1)} %bitcast.90), kind=kOutput, calls=%fused_computation | convolution fusion | flops 538968064 | bytes 5373952 | tf_op jit(solution)/shard_map/jct,td->jcd/dot_general | solution.py:233
  97.5 43.2 %all_to_all.16 = bf16[16,32,4096]{2,1,0:T(8,128)(2,1)S(1)} all-to-all(bf16[16,32,4096]{2,1,0:T(8,128)(2,1)S(1)} %convolution_convert_fusion), channel_id=1, replica_groups=mesh['x'=4,'y'=4,'c'=2,'z'=8] {'x','y'}, dimensions={0} | all-to-all | bytes 8388608 | tf_op jit(solution)/shard_map/all_to_all | solution.py:240
  140.8 14.4 %expert_partial.1 = bf16[512,4096]{1,0:T(8,128)(2,1)} custom-call(bf16[512,4096]{1,0:T(8,128)(2,1)S(1)} %bitcast.86, bf16[4096,384]{1,0:T(8,128)(2,1)} %bitcast.24.gate_a, bf16[4096,384]{1,0:T(8,128)(2,1)} %bitcast.25.up_a, bf16[384,4096]{1,0:T(8,128)(2,1)} %bitcast.26.down_a, bf16[4096,384]{1,0:T(8,128)(2,1)} %collective-permute-done.17.gate_b, ...), custom_call_target="tpu_custom_call" | custom-call | flops 9663676416 | bytes 27262976 | tf_op jit(solution)/shard_map/expert_partial/pallas_call | solution.py:135
  155.1 42.8 %all_to_all.17 = bf16[16,32,4096]{2,1,0:T(8,128)(2,1)S(1)} all-to-all(bf16[16,32,4096]{2,1,0:T(8,128)(2,1)} %bitcast.89), channel_id=1, replica_groups=mesh['x'=4,'y'=4,'c'=2,'z'=8] {'x','y'}, dimensions={0} | all-to-all | bytes 8388608 | tf_op jit(solution)/shard_map/all_to_all | solution.py:244
  198.8 3.2 %collective-permute-start.24 = (bf16[64,512]{1,0:T(8,128)(2,1)S(1)}, bf16[64,512]{1,0:T(8,128)(2,1)S(1)}, u32[]{:S(2)}, u32[]{:S(2)}) collective-permute-start(bf16[64,512]{1,0:T(8,128)(2,1)S(1)} %get-tuple-element.29), channel_id=1, source_target_pairs={{0,7},{1,0},{2,1},{3,2},{4,3},{5,4},{6,5},{7,6},{8,15},{9,8},{10,9... | collective-permute-start | bytes 196616 | tf_op jit(solution)/shard_map/ppermute | solution.py:64
  204.4 2.3 %collective-permute-start.21 = (bf16[128,512]{1,0:T(8,128)(2,1)S(1)}, bf16[128,512]{1,0:T(8,128)(2,1)S(1)}, u32[]{:S(2)}, u32[]{:S(2)}) collective-permute-start(bf16[128,512]{1,0:T(8,128)(2,1)S(1)} %pad_maximum_fusion.3), channel_id=1, source_target_pairs={{0,1},{1,2},{2,3},{3,4},{4,5},{5,6},{6,7},{7,0},{8,9},{9,10},{10,1... | collective-permute-start | bytes 393224 | tf_op jit(solution)/shard_map/ppermute | solution.py:72
  207.8 2.8 %collective-permute-done.21 = bf16[128,512]{1,0:T(8,128)(2,1)S(1)} collective-permute-done((bf16[128,512]{1,0:T(8,128)(2,1)S(1)}, bf16[128,512]{1,0:T(8,128)(2,1)S(1)}, u32[]{:S(2)}, u32[]{:S(2)}) %collective-permute-start.21) | collective-permute-done | bytes 131104 | tf_op jit(solution)/shard_map/ppermute | solution.py:72
  211.8 5.2 %collective-permute-done.22 = bf16[128,512]{1,0:T(8,128)(2,1)S(1)} collective-permute-done((bf16[128,512]{1,0:T(8,128)(2,1)S(1)}, bf16[128,512]{1,0:T(8,128)(2,1)S(1)}, u32[]{:S(2)}, u32[]{:S(2)}) %collective-permute-start.22) | collective-permute-done | bytes 131104 | tf_op jit(solution)/shard_map/ppermute | solution.py:72
  219.1 2.9 %collective-permute-done.26 = bf16[128,512]{1,0:T(8,128)(2,1)S(1)} collective-permute-done((bf16[128,512]{1,0:T(8,128)(2,1)S(1)}, bf16[128,512]{1,0:T(8,128)(2,1)S(1)}, u32[]{:S(2)}, u32[]{:S(2)}) %collective-permute-start.26) | collective-permute-done | bytes 131104 | tf_op jit(solution)/shard_map/ppermute | solution.py:73
  224.2 3.0 %collective-permute-done.27 = bf16[128,512]{1,0:T(8,128)(2,1)S(1)} collective-permute-done((bf16[128,512]{1,0:T(8,128)(2,1)S(1)}, bf16[128,512]{1,0:T(8,128)(2,1)S(1)}, u32[]{:S(2)}, u32[]{:S(2)}) %collective-permute-start.27) | collective-permute-done | bytes 131104 | tf_op jit(solution)/shard_map/ppermute | solution.py:73
  (112 shorter events, 39.8 us)
Async XLA Ops:
  23.4 74.1 %collective-permute-start.17 = (bf16[4096,384]{1,0:T(8,128)(2,1)}, bf16[4096,384]{1,0:T(8,128)(2,1)}, u32[]{:S(2)}, u32[]{:S(2)}) collective-permute-start(bf16[4096,384]{1,0:T(8,128)(2,1)} %bitcast.24.gate_a), channel_id=1, source_target_pairs={{0,8},{8,0},{1,9},{9,1},{2,10},{10,2},{3,11},{11,3},{4,12},{12,4},... | collective-permute-start | bytes 9437192 | tf_op jit(solution)/shard_map/ppermute | solution.py:19
  23.9 73.6 %collective-permute-start.18 = (bf16[4096,384]{1,0:T(8,128)(2,1)}, bf16[4096,384]{1,0:T(8,128)(2,1)}, u32[]{:S(2)}, u32[]{:S(2)}) collective-permute-start(bf16[4096,384]{1,0:T(8,128)(2,1)} %bitcast.25.up_a), channel_id=1, source_target_pairs={{0,8},{8,0},{1,9},{9,1},{2,10},{10,2},{3,11},{11,3},{4,12},{12,4},... | collective-permute-start | bytes 9437192 | tf_op jit(solution)/shard_map/ppermute | solution.py:19
  24.0 73.6 %collective-permute-start.19 = (bf16[384,4096]{1,0:T(8,128)(2,1)}, bf16[384,4096]{1,0:T(8,128)(2,1)}, u32[]{:S(2)}, u32[]{:S(2)}) collective-permute-start(bf16[384,4096]{1,0:T(8,128)(2,1)} %bitcast.26.down_a), channel_id=1, source_target_pairs={{0,8},{8,0},{1,9},{9,1},{2,10},{10,2},{3,11},{11,3},{4,12},{12,4},... | collective-permute-start | bytes 9437192 | tf_op jit(solution)/shard_map/ppermute | solution.py:19
  32.0 8.3 %collective-permute-start.1 = (bf16[64,512]{1,0:T(8,128)(2,1)S(1)}, bf16[64,512]{1,0:T(8,128)(2,1)S(1)}, u32[]{:S(2)}, u32[]{:S(2)}) collective-permute-start(bf16[64,512]{1,0:T(8,128)(2,1)S(1)} %get-tuple-element.35), channel_id=1, source_target_pairs={{0,1},{1,2},{2,3},{3,4},{4,5},{5,6},{6,7},{7,0},{8,9},{9,10},{10,1... | collective-permute-start | bytes 196616 | tf_op jit(solution)/shard_map/ppermute | solution.py:63
  34.0 6.3 %collective-permute-start.5 = (bf16[64,512]{1,0:T(8,128)(2,1)S(1)}, bf16[64,512]{1,0:T(8,128)(2,1)S(1)}, u32[]{:S(2)}, u32[]{:S(2)}) collective-permute-start(bf16[64,512]{1,0:T(8,128)(2,1)S(1)} %get-tuple-element.37), channel_id=1, source_target_pairs={{0,7},{1,0},{2,1},{3,2},{4,3},{5,4},{6,5},{7,6},{8,15},{9,8},{10,9... | collective-permute-start | bytes 196616 | tf_op jit(solution)/shard_map/ppermute | solution.py:64
  40.4 6.3 %collective-permute-start.2 = (bf16[128,512]{1,0:T(8,128)(2,1)S(1)}, bf16[128,512]{1,0:T(8,128)(2,1)S(1)}, u32[]{:S(2)}, u32[]{:S(2)}) collective-permute-start(bf16[128,512]{1,0:T(8,128)(2,1)S(1)} %pad_maximum_fusion.1), channel_id=1, source_target_pairs={{0,1},{1,2},{2,3},{3,4},{4,5},{5,6},{6,7},{7,0},{8,9},{9,10},{10,1... | collective-permute-start | bytes 393224 | tf_op jit(solution)/shard_map/ppermute | solution.py:72
  41.3 6.4 %collective-permute-start.6 = (bf16[128,512]{1,0:T(8,128)(2,1)}, bf16[128,512]{1,0:T(8,128)(2,1)}, u32[]{:S(2)}, u32[]{:S(2)}) collective-permute-start(bf16[128,512]{1,0:T(8,128)(2,1)} %pad_maximum_fusion.2), channel_id=1, source_target_pairs={{0,7},{1,0},{2,1},{3,2},{4,3},{5,4},{6,5},{7,6},{8,15},{9,8},{10,9... | collective-permute-start | bytes 393224 | tf_op jit(solution)/shard_map/ppermute | solution.py:73
  46.8 6.4 %collective-permute-start.3 = (bf16[128,512]{1,0:T(8,128)(2,1)S(1)}, bf16[128,512]{1,0:T(8,128)(2,1)}, u32[]{:S(2)}, u32[]{:S(2)}) collective-permute-start(bf16[128,512]{1,0:T(8,128)(2,1)S(1)} %add_convert_fusion.9), channel_id=1, source_target_pairs={{0,1},{1,2},{2,3},{3,4},{4,5},{5,6},{6,7},{7,0},{8,9},{9,10},{10,1... | collective-permute-start | bytes 393224 | tf_op jit(solution)/shard_map/ppermute | solution.py:72
  54.8 6.2 %collective-permute-start.7 = (bf16[128,512]{1,0:T(8,128)(2,1)}, bf16[128,512]{1,0:T(8,128)(2,1)S(1)}, u32[]{:S(2)}, u32[]{:S(2)}) collective-permute-start(bf16[128,512]{1,0:T(8,128)(2,1)} %get-tuple-element.32), channel_id=1, source_target_pairs={{0,7},{1,0},{2,1},{3,2},{4,3},{5,4},{6,5},{7,6},{8,15},{9,8},{10,9... | collective-permute-start | bytes 393224 | tf_op jit(solution)/shard_map/ppermute | solution.py:73
  57.7 6.2 %collective-permute-start.4 = (bf16[128,512]{1,0:T(8,128)(2,1)S(1)}, bf16[128,512]{1,0:T(8,128)(2,1)S(1)}, u32[]{:S(2)}, u32[]{:S(2)}) collective-permute-start(bf16[128,512]{1,0:T(8,128)(2,1)S(1)} %get-tuple-element.31), channel_id=1, source_target_pairs={{0,1},{1,2},{2,3},{3,4},{4,5},{5,6},{6,7},{7,0},{8,9},{9,10},{10,1... | collective-permute-start | bytes 393224 | tf_op jit(solution)/shard_map/ppermute | solution.py:72
  61.1 6.6 %collective-permute-start.8 = (bf16[128,512]{1,0:T(8,128)(2,1)S(1)}, bf16[128,512]{1,0:T(8,128)(2,1)S(1)}, u32[]{:S(2)}, u32[]{:S(2)}) collective-permute-start(bf16[128,512]{1,0:T(8,128)(2,1)S(1)} %add_convert_fusion.6), channel_id=1, source_target_pairs={{0,7},{1,0},{2,1},{3,2},{4,3},{5,4},{6,5},{7,6},{8,15},{9,8},{10,9... | collective-permute-start | bytes 393224 | tf_op jit(solution)/shard_map/ppermute | solution.py:73
  68.7 6.3 %collective-permute-start.12 = (bf16[128,512]{1,0:T(8,128)(2,1)S(1)}, bf16[128,512]{1,0:T(8,128)(2,1)S(1)}, u32[]{:S(2)}, u32[]{:S(2)}) collective-permute-start(bf16[128,512]{1,0:T(8,128)(2,1)S(1)} %get-tuple-element.22), channel_id=1, source_target_pairs={{0,1},{1,2},{2,3},{3,4},{4,5},{5,6},{6,7},{7,0},{8,9},{9,10},{10,1... | collective-permute-start | bytes 393224 | tf_op jit(solution)/shard_map/ppermute | solution.py:33
  68.8 6.2 %collective-permute-start.9 = (bf16[128,512]{1,0:T(8,128)(2,1)S(1)}, bf16[128,512]{1,0:T(8,128)(2,1)S(1)}, u32[]{:S(2)}, u32[]{:S(2)}) collective-permute-start(bf16[128,512]{1,0:T(8,128)(2,1)S(1)} %get-tuple-element.22), channel_id=1, source_target_pairs={{0,7},{1,0},{2,1},{3,2},{4,3},{5,4},{6,5},{7,6},{8,15},{9,8},{10,9... | collective-permute-start | bytes 393224 | tf_op jit(solution)/shard_map/ppermute | solution.py:34
  74.9 6.2 %collective-permute-start.13 = (bf16[128,512]{1,0:T(8,128)(2,1)S(1)}, bf16[128,512]{1,0:T(8,128)(2,1)S(1)}, u32[]{:S(2)}, u32[]{:S(2)}) collective-permute-start(bf16[128,512]{1,0:T(8,128)(2,1)S(1)} %collective-permute-done.12), channel_id=1, source_target_pairs={{0,1},{1,2},{2,3},{3,4},{4,5},{5,6},{6,7},{7,0},{8,9},{9,10},{10,1... | collective-permute-start | bytes 393224 | tf_op jit(solution)/shard_map/ppermute | solution.py:33
  74.9 6.2 %collective-permute-start.10 = (bf16[128,512]{1,0:T(8,128)(2,1)S(1)}, bf16[128,512]{1,0:T(8,128)(2,1)S(1)}, u32[]{:S(2)}, u32[]{:S(2)}) collective-permute-start(bf16[128,512]{1,0:T(8,128)(2,1)S(1)} %collective-permute-done.9), channel_id=1, source_target_pairs={{0,7},{1,0},{2,1},{3,2},{4,3},{5,4},{6,5},{7,6},{8,15},{9,8},{10,9... | collective-permute-start | bytes 393224 | tf_op jit(solution)/shard_map/ppermute | solution.py:34
  81.1 6.2 %collective-permute-start.14 = (bf16[128,512]{1,0:T(8,128)(2,1)S(1)}, bf16[128,512]{1,0:T(8,128)(2,1)S(1)}, u32[]{:S(2)}, u32[]{:S(2)}) collective-permute-start(bf16[128,512]{1,0:T(8,128)(2,1)S(1)} %collective-permute-done.13), channel_id=1, source_target_pairs={{0,1},{1,2},{2,3},{3,4},{4,5},{5,6},{6,7},{7,0},{8,9},{9,10},{10,1... | collective-permute-start | bytes 393224 | tf_op jit(solution)/shard_map/ppermute | solution.py:33
  81.1 6.2 %collective-permute-start.11 = (bf16[128,512]{1,0:T(8,128)(2,1)S(1)}, bf16[128,512]{1,0:T(8,128)(2,1)S(1)}, u32[]{:S(2)}, u32[]{:S(2)}) collective-permute-start(bf16[128,512]{1,0:T(8,128)(2,1)S(1)} %collective-permute-done.10), channel_id=1, source_target_pairs={{0,7},{1,0},{2,1},{3,2},{4,3},{5,4},{6,5},{7,6},{8,15},{9,8},{10,9... | collective-permute-start | bytes 393224 | tf_op jit(solution)/shard_map/ppermute | solution.py:34
  87.3 5.5 %collective-permute-start.15 = (bf16[64,512]{1,0:T(8,128)(2,1)S(1)}, bf16[64,512]{1,0:T(8,128)(2,1)S(1)}, u32[]{:S(2)}, u32[]{:S(2)}) collective-permute-start(bf16[64,512]{1,0:T(8,128)(2,1)S(1)} %slice.66), channel_id=1, source_target_pairs={{0,1},{1,2},{2,3},{3,4},{4,5},{5,6},{6,7},{7,0},{8,9},{9,10},{10,1... | collective-permute-start | bytes 196616 | tf_op jit(solution)/shard_map/ppermute | solution.py:37
  87.3 5.4 %collective-permute-start.16 = (bf16[64,512]{1,0:T(8,128)(2,1)S(1)}, bf16[64,512]{1,0:T(8,128)(2,1)S(1)}, u32[]{:S(2)}, u32[]{:S(2)}) collective-permute-start(bf16[64,512]{1,0:T(8,128)(2,1)S(1)} %slice.67), channel_id=1, source_target_pairs={{0,7},{1,0},{2,1},{3,2},{4,3},{5,4},{6,5},{7,6},{8,15},{9,8},{10,9... | collective-permute-start | bytes 196616 | tf_op jit(solution)/shard_map/ppermute | solution.py:38
  198.8 5.6 %collective-permute-start.20 = (bf16[64,512]{1,0:T(8,128)(2,1)S(1)}, bf16[64,512]{1,0:T(8,128)(2,1)S(1)}, u32[]{:S(2)}, u32[]{:S(2)}) collective-permute-start(bf16[64,512]{1,0:T(8,128)(2,1)S(1)} %get-tuple-element.27), channel_id=1, source_target_pairs={{0,1},{1,2},{2,3},{3,4},{4,5},{5,6},{6,7},{7,0},{8,9},{9,10},{10,1... | collective-permute-start | bytes 196616 | tf_op jit(solution)/shard_map/ppermute | solution.py:63
  198.8 5.5 %collective-permute-start.24 = (bf16[64,512]{1,0:T(8,128)(2,1)S(1)}, bf16[64,512]{1,0:T(8,128)(2,1)S(1)}, u32[]{:S(2)}, u32[]{:S(2)}) collective-permute-start(bf16[64,512]{1,0:T(8,128)(2,1)S(1)} %get-tuple-element.29), channel_id=1, source_target_pairs={{0,7},{1,0},{2,1},{3,2},{4,3},{5,4},{6,5},{7,6},{8,15},{9,8},{10,9... | collective-permute-start | bytes 196616 | tf_op jit(solution)/shard_map/ppermute | solution.py:64
  204.4 6.3 %collective-permute-start.21 = (bf16[128,512]{1,0:T(8,128)(2,1)S(1)}, bf16[128,512]{1,0:T(8,128)(2,1)S(1)}, u32[]{:S(2)}, u32[]{:S(2)}) collective-permute-start(bf16[128,512]{1,0:T(8,128)(2,1)S(1)} %pad_maximum_fusion.3), channel_id=1, source_target_pairs={{0,1},{1,2},{2,3},{3,4},{4,5},{5,6},{6,7},{7,0},{8,9},{9,10},{10,1... | collective-permute-start | bytes 393224 | tf_op jit(solution)/shard_map/ppermute | solution.py:72
  210.7 6.3 %collective-permute-start.22 = (bf16[128,512]{1,0:T(8,128)(2,1)S(1)}, bf16[128,512]{1,0:T(8,128)(2,1)S(1)}, u32[]{:S(2)}, u32[]{:S(2)}) collective-permute-start(bf16[128,512]{1,0:T(8,128)(2,1)S(1)} %add_convert_fusion.4), channel_id=1, source_target_pairs={{0,1},{1,2},{2,3},{3,4},{4,5},{5,6},{6,7},{7,0},{8,9},{9,10},{10,1... | collective-permute-start | bytes 393224 | tf_op jit(solution)/shard_map/ppermute | solution.py:72
  217.9 6.3 %collective-permute-start.23 = (bf16[128,512]{1,0:T(8,128)(2,1)S(1)}, bf16[128,512]{1,0:T(8,128)(2,1)S(1)}, u32[]{:S(2)}, u32[]{:S(2)}) collective-permute-start(bf16[128,512]{1,0:T(8,128)(2,1)S(1)} %get-tuple-element.23), channel_id=1, source_target_pairs={{0,1},{1,2},{2,3},{3,4},{4,5},{5,6},{6,7},{7,0},{8,9},{9,10},{10,1... | collective-permute-start | bytes 393224 | tf_op jit(solution)/shard_map/ppermute | solution.py:72
  (12 other events, 170.8 us)

commit v6 on v5

--- a/solution.py
+++ b/solution.py
@@ -8,6 +8,7 @@
 HD = 128
 TOP = 8
 EXP_GROUP = 8
+SLICE = 512
 BF = jnp.bfloat16
 F32 = jnp.float32
 PIECES = 4
@@ -24,54 +25,182 @@
     return lax.all_to_all(spread, axes, split_axis=0, concat_axis=0, tiled=True)
 
 
-def gather_ring(array, depth):
+def gather_ring(piece, depth):
     ahead = [(i, (i + 1) % depth) for i in range(depth)]
     behind = [(i, (i + depth - 1) % depth) for i in range(depth)]
-    half = array.shape[0] // 2
-    from_behind, from_ahead = [array], [array]
-    for step in range(1, depth // 2):
+    half = piece.shape[0] // 2
+    from_behind, from_ahead = [piece], [piece]
+    for _ in range(1, depth // 2):
         from_behind.append(lax.ppermute(from_behind[-1], "z", ahead))
         from_ahead.append(lax.ppermute(from_ahead[-1], "z", behind))
-    far = jnp.concatenate(
-        [
-            lax.ppermute(from_behind[-1][:half], "z", ahead),
-            lax.ppermute(from_ahead[-1][half:], "z", behind),
-        ],
-        axis=0,
-    )
-    pieces = from_ahead + [far] + from_behind[:0:-1]
-    twice = jnp.stack(pieces + pieces)
-    return lax.dynamic_slice_in_dim(twice, depth - lax.axis_index("z"), depth, 0)
-
-
-def sum_ring(array, depth):
-    tokens, width = array.shape
-    width //= depth
-    half = tokens // 2
-    here = lax.axis_index("z")
+    far = (
+        lax.ppermute(from_behind[-1][:half], "z", ahead),
+        lax.ppermute(from_ahead[-1][half:], "z", behind),
+    )
+    return from_ahead + [far] + from_behind[:0:-1]
+
+
+def sum_ring(slices, depth):
     ahead = [(i, (i + 1) % depth) for i in range(depth)]
     behind = [(i, (i + depth - 1) % depth) for i in range(depth)]
 
-    def own(offset):
-        start = lax.rem(here + offset, depth) * width
-        return lax.dynamic_slice_in_dim(array, start, width, 1)
-
     def add(mine, arrived):
         return (mine.astype(F32) + arrived.astype(F32)).astype(BF)
 
-    far = own(depth // 2)
-    forward = lax.ppermute(far[:half], "z", ahead)
-    backward = lax.ppermute(far[half:], "z", behind)
-    for offset in range(depth // 2 - 1, 0, -1):
-        mine, other = own(offset), own(depth - offset)
-        if offset == depth // 2 - 1:
+    far = depth // 2
+    first, second = slices[far]
+    half = first.shape[0]
+    forward = lax.ppermute(first, "z", ahead)
+    backward = lax.ppermute(second, "z", behind)
+    for offset in range(far - 1, 0, -1):
+        mine, other = slices[offset], slices[depth - offset]
+        if offset == far - 1:
             forward = jnp.concatenate([add(mine[:half], forward), mine[half:]], axis=0)
             backward = jnp.concatenate([other[:half], add(other[half:], backward)], axis=0)
         else:
             forward, backward = add(mine, forward), add(other, backward)
         forward = lax.ppermute(forward, "z", ahead)
         backward = lax.ppermute(backward, "z", behind)
-    return own(0).astype(F32) + forward.astype(F32) + backward.astype(F32)
+    return slices[0].astype(F32) + forward.astype(F32) + backward.astype(F32)
+
+
+def in_vmem(*operands):
+    return [pltpu.with_memory_space_constraint(operand, pltpu.VMEM) for operand in operands]
+
+
+def slice_shapes(depth, rows, width):
+    shapes = [jax.ShapeDtypeStruct((rows, width), BF)] * (depth + 1)
+    shapes[depth // 2] = shapes[depth // 2 + 1] = jax.ShapeDtypeStruct((rows // 2, width), BF)
+    return shapes
+
+
+def pair_far(slices):
+    far = (len(slices) - 1) // 2
+    return slices[:far] + [(slices[far], slices[far + 1])] + slices[far + 2 :]
+
+
+def store_slices(group, outs, product_of):
+    depth = len(outs) - 1
+    far = depth // 2
+    half, width = outs[far].shape
+    for offset in range(depth):
+        start = pl.multiple_of(lax.rem(group + offset, depth) * width, width)
+        product = product_of(pl.ds(start, width)).astype(BF)
+        if offset < far:
+            outs[offset][...] = product
+        elif offset > far:
+            outs[offset + 1][...] = product
+        else:
+            outs[far][...] = product[:half]
+            outs[far + 1][...] = product[half:]
+
+
+def attention_kernel(group, queries, own_kv, other_kv, out_proj, out):
+    tokens, width = queries.shape
+    heads = width // HD
+    stacked = jnp.concatenate(
+        [queries[:, head * HD : (head + 1) * HD] for head in range(heads)], axis=0
+    )
+    contract = (((1,), (1,)), ((), ()))
+    scores = [
+        lax.dot_general(stacked, kv[:, :HD], contract, preferred_element_type=F32)
+        for kv in (own_kv, other_kv)
+    ]
+    top = jnp.maximum(*[jnp.max(part, axis=1, keepdims=True) for part in scores])
+    weights = [jnp.exp((part - top) * HD ** (-0.5)) for part in scores]
+    total = sum(jnp.sum(part, axis=1, keepdims=True) for part in weights)
+    values = sum(
+        jnp.dot(part.astype(BF), kv[:, HD:], preferred_element_type=F32)
+        for part, kv in zip(weights, (own_kv, other_kv))
+    )
+    attended = (values / total).astype(BF)
+    attended = jnp.concatenate(
+        [attended[head * tokens : (head + 1) * tokens] for head in range(heads)], axis=1
+    )
+    depth = out_proj.shape[1] // SLICE
+    for offset in range(depth):
+        start = pl.multiple_of(lax.rem(group[0] + offset, depth) * SLICE, SLICE)
+        product = jnp.dot(
+            attended, out_proj[:, pl.ds(start, SLICE)], preferred_element_type=F32
+        )
+        out[:, offset * SLICE : (offset + 1) * SLICE] = product.astype(BF)
+
+
+def attention_slices(group, queries, own_kv, other_kv, out_proj, depth):
+    tokens, width = queries.shape
+    total = pl.pallas_call(
+        attention_kernel,
+        out_shape=jax.ShapeDtypeStruct((tokens, out_proj.shape[1]), BF),
+        in_specs=[pl.BlockSpec(memory_space=pltpu.SMEM)]
+        + [pl.BlockSpec(memory_space=pltpu.VMEM)] * 4,
+        out_specs=pl.BlockSpec(memory_space=pltpu.VMEM),
+        compiler_params=pltpu.CompilerParams(vmem_limit_bytes=32 * 2**20),
+        name="attention",
+    )(group, *in_vmem(queries, own_kv, other_kv, out_proj))
+    slices = [total[:, offset * SLICE : (offset + 1) * SLICE] for offset in range(depth)]
+    far = slices[depth // 2]
+    slices[depth // 2] = (far[: tokens // 2], far[tokens // 2 :])
+    return slices
+
+
+def dispatch_kernel(group, selector, gain, *refs):
+    *pieces, out = refs
+    far = (len(pieces) - 1) // 2
+    whole = [piece[...].astype(F32) for piece in pieces]
+    whole[far : far + 2] = [jnp.concatenate(whole[far : far + 2], axis=0)]
+    depth = len(whole)
+    width = whole[0].shape[1]
+    square = sum(jnp.sum(piece * piece, axis=1, keepdims=True) for piece in whole)
+    scale = lax.rsqrt(square / (depth * width) + 1e-06)
+    for offset, piece in enumerate(whole):
+        start = pl.multiple_of(lax.rem(group[0] + offset, depth) * width, width)
+        columns = pl.ds(start, width)
+        normed = (piece * scale * gain[:, columns]).astype(BF)
+        rows = jnp.dot(selector[...], normed, preferred_element_type=F32).astype(BF)
+        rows = rows.reshape(out.shape[0], out.shape[2], width)
+        for copy in range(out.shape[1]):
+            out[:, copy, :, columns] = rows
+
+
+def dispatch_rows(group, selector, gain, pieces, experts, copies):
+    far = len(pieces) // 2
+    flat = pieces[:far] + list(pieces[far]) + pieces[far + 1 :]
+    width = gain.shape[1]
+    return pl.pallas_call(
+        dispatch_kernel,
+        out_shape=jax.ShapeDtypeStruct(
+            (experts, copies, selector.shape[0] // experts, width), BF
+        ),
+        in_specs=[pl.BlockSpec(memory_space=pltpu.SMEM)]
+        + [pl.BlockSpec(memory_space=pltpu.VMEM)] * (2 + len(flat)),
+        out_specs=pl.BlockSpec(memory_space=pltpu.VMEM),
+        compiler_params=pltpu.CompilerParams(vmem_limit_bytes=24 * 2**20),
+        name="dispatch",
+    )(group, *in_vmem(selector, gain, *flat))
+
+
+def combine_kernel(group, weights, returned, *outs):
+    store_slices(
+        group[0],
+        outs,
+        lambda columns: jnp.dot(
+            weights[...], returned[:, columns], preferred_element_type=F32
+        ),
+    )
+
+
+def combine_slices(group, weights, returned, depth):
+    shapes = slice_shapes(depth, weights.shape[0], returned.shape[1] // depth)
+    slices = pl.pallas_call(
+        combine_kernel,
+        out_shape=shapes,
+        in_specs=[pl.BlockSpec(memory_space=pltpu.SMEM)]
+        + [pl.BlockSpec(memory_space=pltpu.VMEM)] * 2,
+        out_specs=[pl.BlockSpec(memory_space=pltpu.VMEM)] * len(shapes),
+        compiler_params=pltpu.CompilerParams(vmem_limit_bytes=16 * 2**20),
+        name="combine",
+    )(group, *in_vmem(weights, returned))
+    return pair_far(list(slices))
 
 
 def expert_kernel(
@@ -157,23 +286,6 @@
     )(pltpu.with_memory_space_constraint(rows, pltpu.VMEM), *parts)
 
 
-def attention(queries, all_kv, kv_local):
-    tokens = queries.shape[0]
-    group_size = queries.shape[1] // HD // kv_local
-    width = kv_local * HD
-    query_split = queries.reshape(tokens, kv_local, group_size, HD)
-    key_split = all_kv[:, :width].reshape(-1, kv_local, HD)
-    value_split = all_kv[:, width:].reshape(-1, kv_local, HD)
-    scores = jnp.einsum(
-        "tkgd,skd->kgts", query_split, key_split, preferred_element_type=F32
-    ) * HD ** (-0.5)
-    attn_probs = jax.nn.softmax(scores, axis=-1).astype(BF)
-    attended = jnp.einsum(
-        "kgts,skd->tkgd", attn_probs, value_split, preferred_element_type=F32
-    ).astype(BF)
-    return attended.reshape(tokens, -1)
-
-
 def shards(
     residual_in,
     queries,
@@ -197,21 +309,17 @@
     own_kv = gather_by_exchange(
         jnp.concatenate([key_heads, value_heads], axis=1), ("x", "y"), plane
     )
-    all_kv = jnp.concatenate([own_kv, swap_cores(own_kv)], axis=0)
-    all_kv = all_kv.reshape(-1, all_kv.shape[-1])
+    own_kv = own_kv.reshape(-1, own_kv.shape[-1])
+    other_kv = swap_cores(own_kv)
 
     other_parts = tuple(swap_cores(part[0]) for part in (gate_proj, up_proj, down_proj))
 
-    attended = attention(queries, all_kv, key_heads.shape[1] // HD)
-    partial_attn = jnp.dot(attended, out_proj, preferred_element_type=F32).astype(BF)
-    attn_share = sum_ring(partial_attn, depth)
+    group = group_index.astype(jnp.int32).reshape(1)
+    attn_share = sum_ring(
+        attention_slices(group, queries, own_kv, other_kv, out_proj, depth), depth
+    )
     mixed_local = (residual_in.astype(F32) + attn_share).astype(BF)
-
-    mixed_full = gather_ring(mixed_local, depth)
-    mixed_full = mixed_full.transpose(1, 0, 2).reshape(tokens, -1)
-    mixed_float = mixed_full.astype(F32)
-    mean_square = jnp.mean(mixed_float * mixed_float, axis=-1, keepdims=True)
-    normed = (mixed_float * lax.rsqrt(mean_square + 1e-06) * norm_gain).astype(BF)
+    mixed_pieces = gather_ring(mixed_local, depth)
 
     capacity = 2 * tokens * TOP // (EXP_GROUP * depth)
     copies = plane // EXP_GROUP
@@ -227,12 +335,17 @@
     select_hit = live_rows.T[:, None, :] & (rank.T[:, None, :] == slot_range[None, :, None])
     selector = select_hit.astype(BF)
     weighted_select = selector * token_weight.T[:, None, :]
-    selector = jnp.repeat(selector, copies, axis=0)
     weighted_select = jnp.repeat(weighted_select, copies, axis=0)
-
-    outgoing = jnp.einsum(
-        "jct,td->jcd", selector, normed, preferred_element_type=F32
-    ).astype(BF)
+    weighted_select = weighted_select.reshape(-1, tokens).T
+    outgoing = dispatch_rows(
+        group,
+        selector.reshape(-1, tokens),
+        norm_gain.reshape(1, -1),
+        mixed_pieces,
+        EXP_GROUP,
+        copies,
+    )
+    outgoing = outgoing.reshape(plane, capacity, -1)
     own_parts = (gate_proj[0], up_proj[0], down_proj[0])
     outgoing, own_parts, other_parts, weighted_select = lax.optimization_barrier(
         (outgoing, own_parts, other_parts, weighted_select)
@@ -244,10 +357,9 @@
     returned = lax.all_to_all(
         partial_out.reshape(arrived.shape), ("x", "y"), split_axis=0, concat_axis=0, tiled=True
     )
-    combined = jnp.einsum(
-        "jct,jcd->td", weighted_select, returned, preferred_element_type=F32
-    ).astype(BF)
-    moe_share = sum_ring(combined, depth)
+    moe_share = sum_ring(
+        combine_slices(group, weighted_select, returned.reshape(rows.shape), depth), depth
+    )
     moe_value = jnp.where(changed[:, None] == 1, moe_share, cached_moe.astype(F32))
     return (mixed_local.astype(F32) + moe_value).astype(BF)
 

time: 230 us -> 222 us (0.965)
  other arithmetic: 11 us -> 2.52 us
  matrix products: 5.49 us -> 0 us
  Pallas kernels: 14.4 us -> 18.6 us
    ppermute x6, starting transfers between devices: 9.11 us -> 16.4 us  [sum_ring(): backward = lax.ppermute(backward, 'z', behind)]
    dot_general x5 -> x0, matrix products: 5.49 us -> none  [the longest x1 2.48 us: shards(): jnp.einsum('jct,td->jcd', selector, normed, preferred_element_type=F32)]
    ppermute x6, starting transfers between devices: 6.14 us -> 1.7 us  [sum_ring(): forward = lax.ppermute(forward, 'z', ahead)]
    ppermute x6, waiting for transfers between devices: 11.8 us -> 16.1 us  [sum_ring(): backward = lax.ppermute(backward, 'z', behind)]
    pallas_call x0 -> x3, Pallas kernels: none -> 4.26 us  [the longest x1 2.49 us: attention_slices(): pl.pallas_call(attention_kernel, out_shape=jax.ShapeDtypeStruct((tokens,...]
    ppermute x6, waiting for transfers between devices: 16.6 us -> 12.9 us  [sum_ring(): forward = lax.ppermute(forward, 'z', ahead)]
  transfers between devices with their start and end apart: 28 -> 28, of which waited for: 16 -> 17; matrix products, arithmetic and copies ran while one was open for 7% -> 1% of each run, Pallas kernels for 0% -> 2%
where the time goes in v6:
time: 222 us; the launch traced here: 221 us
  blocking collectives  109 us (49%)
  waiting for transfers between devices  47.8 us (22%)
  starting transfers between devices  39.9 us (18%)
  Pallas kernels  18.6 us (8%)
  other arithmetic  2.52 us (1%)
    all_to_all x1, blocking collectives, shards(): lax.all_to_all(outgoing, ('x', 'y'), split_axis=0, concat_axis=0, tiled=T...  43.9 us
    all_to_all x1, blocking collectives, shards(): lax.all_to_all(partial_out.reshape(arrived.shape), ('x', 'y'), split_axis...  43 us
    all_to_all x1, blocking collectives, gather_by_exchange(): return lax.all_to_all(spread, axes, split_axis=0, concat_axis=0, tiled=True)  22.4 us
    ppermute x6, starting transfers between devices, sum_ring(): backward = lax.ppermute(backward, 'z', behind)  16.4 us
    ppermute x6, waiting for transfers between devices, sum_ring(): backward = lax.ppermute(backward, 'z', behind)  16.1 us
    pallas_call x1, Pallas kernels, expert_partial(): pl.pallas_call(expert_kernel, out_shape=jax.ShapeDtypeStruct((count, dept...  14.4 us
    ppermute x6, waiting for transfers between devices, sum_ring(): forward = lax.ppermute(forward, 'z', ahead)  12.9 us
    ppermute x3, waiting for transfers between devices, gather_ring(): from_behind.append(lax.ppermute(from_behind[-1], 'z', ahead))  8.31 us
  transfers between devices with their start and end apart: 28, of which 17 were waited for; matrix products, arithmetic and copies ran while one was open for 1% of the time, Pallas kernels for 2%

profile of v6, /device:TPU:6, one launch (start us, length us, event | category | flops | bytes accessed | tf_op | source)
XLA Modules:
  0.0 220.5 jit_solution(13947879597305199910)
XLA Ops:
  0.9 22.4 %all_to_all.15 = bf16[16,128,256]{2,1,0:T(8,128)(2,1)S(1)} all-to-all(bf16[16,128,256]{2,1,0:T(8,128)(2,1)S(1)} %broadcast_in_dim.21), channel_id=1, replica_groups=mesh['x'=4,'y'=4,'c'=2,'z'=8] {'x','y'}, dimensions={0} | all-to-all | bytes 2097152 | tf_op jit(solution)/shard_map/all_to_all | solution.py:25
  24.3 3.1 %collective-permute-done.other_kv = bf16[2048,256]{1,0:T(8,128)(2,1)S(1)} collective-permute-done((bf16[2048,256]{1,0:T(8,128)(2,1)S(1)}, bf16[2048,256]{1,0:T(8,128)(2,1)S(1)}, u32[]{:S(2)}, u32[]{:S(2)}) %collective-permute-start) | collective-permute-done | bytes 1048608 | tf_op jit(solution)/shard_map/ppermute | solution.py:20
  29.0 2.5 %attention.1 = bf16[128,4096]{1,0:T(8,128)(2,1)S(1)} custom-call(s32[1]{0:T(128)} %bitcast.group, bf16[128,256]{1,0:T(8,128)(2,1)S(1)} %copy-done.1, bf16[2048,256]{1,0:T(8,128)(2,1)S(1)} %bitcast.29, bf16[2048,256]{1,0:T(8,128)(2,1)S(1)} %collective-permute-done.other_kv, bf16[256,4096]{1,0:T(8,128)(2,1)S(1)} %copy-done), custom_call_target="tpu_custom_call" | custom-call | tf_op jit(solution)/shard_map/attention/pallas_call | solution.py:131
  33.6 4.0 %collective-permute-start.5 = (bf16[64,512]{1,0:T(8,128)(2,1)S(1)}, bf16[64,512]{1,0:T(8,128)(2,1)S(1)}, u32[]{:S(2)}, u32[]{:S(2)}) collective-permute-start(bf16[64,512]{1,0:T(8,128)(2,1)S(1)} %get-tuple-element.44), channel_id=1, source_target_pairs={{0,7},{1,0},{2,1},{3,2},{4,3},{5,4},{6,5},{7,6},{8,15},{9,8},{10,9... | collective-permute-start | bytes 196616 | tf_op jit(solution)/shard_map/ppermute | solution.py:54
  40.1 3.3 %collective-permute-start.6 = (bf16[128,512]{1,0:T(8,128)(2,1)S(1)}, bf16[128,512]{1,0:T(8,128)(2,1)S(1)}, u32[]{:S(2)}, u32[]{:S(2)}) collective-permute-start(bf16[128,512]{1,0:T(8,128)(2,1)S(1)} %pad_maximum_fusion.1), channel_id=1, source_target_pairs={{0,7},{1,0},{2,1},{3,2},{4,3},{5,4},{6,5},{7,6},{8,15},{9,8},{10,9... | collective-permute-start | bytes 393224 | tf_op jit(solution)/shard_map/ppermute | solution.py:63
  43.4 2.9 %collective-permute-done.2 = bf16[128,512]{1,0:T(8,128)(2,1)S(1)} collective-permute-done((bf16[128,512]{1,0:T(8,128)(2,1)S(1)}, bf16[128,512]{1,0:T(8,128)(2,1)S(1)}, u32[]{:S(2)}, u32[]{:S(2)}) %collective-permute-start.2) | collective-permute-done | bytes 131104 | tf_op jit(solution)/shard_map/ppermute | solution.py:62
  46.4 6.2 %collective-permute-done.3 = bf16[128,512]{1,0:T(8,128)(2,1)S(1)} collective-permute-done((bf16[128,512]{1,0:T(8,128)(2,1)S(1)}, bf16[128,512]{1,0:T(8,128)(2,1)S(1)}, u32[]{:S(2)}, u32[]{:S(2)}) %collective-permute-start.3) | collective-permute-done | bytes 131104 | tf_op jit(solution)/shard_map/ppermute | solution.py:62
  54.8 3.9 %collective-permute-done.7 = bf16[128,512]{1,0:T(8,128)(2,1)S(1)} collective-permute-done((bf16[128,512]{1,0:T(8,128)(2,1)S(1)}, bf16[128,512]{1,0:T(8,128)(2,1)S(1)}, u32[]{:S(2)}, u32[]{:S(2)}) %collective-permute-start.7) | collective-permute-done | bytes 131104 | tf_op jit(solution)/shard_map/ppermute | solution.py:63
  59.9 5.1 %collective-permute-done.8 = bf16[128,512]{1,0:T(8,128)(2,1)S(1)} collective-permute-done((bf16[128,512]{1,0:T(8,128)(2,1)S(1)}, bf16[128,512]{1,0:T(8,128)(2,1)S(1)}, u32[]{:S(2)}, u32[]{:S(2)}) %collective-permute-start.8) | collective-permute-done | bytes 131104 | tf_op jit(solution)/shard_map/ppermute | solution.py:63
  65.3 3.2 %collective-permute-start.9 = (bf16[128,512]{1,0:T(8,128)(2,1)S(1)}, bf16[128,512]{1,0:T(8,128)(2,1)S(1)}, u32[]{:S(2)}, u32[]{:S(2)}) collective-permute-start(bf16[128,512]{1,0:T(8,128)(2,1)S(1)} %add_convert_fusion.5.refs_0_), channel_id=1, source_target_pairs={{0,7},{1,0},{2,1},{3,2},{4,3},{5,4},{6,5},{7,6},{8,15},{9,8},{10,9... | collective-permute-start | bytes 393224 | tf_op jit(solution)/shard_map/ppermute | solution.py:35
  68.6 2.9 %collective-permute-done.12.refs_8_ = bf16[128,512]{1,0:T(8,128)(2,1)S(1)} collective-permute-done((bf16[128,512]{1,0:T(8,128)(2,1)S(1)}, bf16[128,512]{1,0:T(8,128)(2,1)S(1)}, u32[]{:S(2)}, u32[]{:S(2)}) %collective-permute-start.12) | collective-permute-done | bytes 131104 | tf_op jit(solution)/shard_map/ppermute | solution.py:34
  71.6 3.1 %collective-permute-start.10 = (bf16[128,512]{1,0:T(8,128)(2,1)S(1)}, bf16[128,512]{1,0:T(8,128)(2,1)S(1)}, u32[]{:S(2)}, u32[]{:S(2)}) collective-permute-start(bf16[128,512]{1,0:T(8,128)(2,1)S(1)} %collective-permute-done.9.refs_1_), channel_id=1, source_target_pairs={{0,7},{1,0},{2,1},{3,2},{4,3},{5,4},{6,5},{7,6},{8,15},{9,8},{10,9... | collective-permute-start | bytes 393224 | tf_op jit(solution)/shard_map/ppermute | solution.py:35
  75.0 2.7 %collective-permute-done.13.refs_7_ = bf16[128,512]{1,0:T(8,128)(2,1)S(1)} collective-permute-done((bf16[128,512]{1,0:T(8,128)(2,1)S(1)}, bf16[128,512]{1,0:T(8,128)(2,1)S(1)}, u32[]{:S(2)}, u32[]{:S(2)}) %collective-permute-start.13) | collective-permute-done | bytes 131104 | tf_op jit(solution)/shard_map/ppermute | solution.py:34
  81.0 2.8 %collective-permute-done.14.refs_6_ = bf16[128,512]{1,0:T(8,128)(2,1)S(1)} collective-permute-done((bf16[128,512]{1,0:T(8,128)(2,1)S(1)}, bf16[128,512]{1,0:T(8,128)(2,1)S(1)}, u32[]{:S(2)}, u32[]{:S(2)}) %collective-permute-start.14) | collective-permute-done | bytes 131104 | tf_op jit(solution)/shard_map/ppermute | solution.py:34
  84.1 3.1 %collective-permute-start.16 = (bf16[64,512]{1,0:T(8,128)(2,1)S(1)}, bf16[64,512]{1,0:T(8,128)(2,1)S(1)}, u32[]{:S(2)}, u32[]{:S(2)}) collective-permute-start(bf16[64,512]{1,0:T(8,128)(2,1)S(1)} %slice.89), channel_id=1, source_target_pairs={{0,7},{1,0},{2,1},{3,2},{4,3},{5,4},{6,5},{7,6},{8,15},{9,8},{10,9... | collective-permute-start | bytes 196616 | tf_op jit(solution)/shard_map/ppermute | solution.py:38
  90.3 43.9 %all_to_all.16 = bf16[16,32,4096]{2,1,0:T(8,128)(2,1)S(1)} all-to-all(bf16[16,32,4096]{2,1,0:T(8,128)(2,1)S(1)} %bitcast.25), channel_id=1, replica_groups=mesh['x'=4,'y'=4,'c'=2,'z'=8] {'x','y'}, dimensions={0} | all-to-all | bytes 8388608 | tf_op jit(solution)/shard_map/all_to_all | solution.py:353
  134.3 14.4 %expert_partial.1 = bf16[512,4096]{1,0:T(8,128)(2,1)} custom-call(bf16[512,4096]{1,0:T(8,128)(2,1)S(1)} %bitcast.27, bf16[4096,384]{1,0:T(8,128)(2,1)} %bitcast.8.gate_a, bf16[4096,384]{1,0:T(8,128)(2,1)} %bitcast.9.up_a, bf16[384,4096]{1,0:T(8,128)(2,1)} %bitcast.10.down_a, bf16[4096,384]{1,0:T(8,128)(2,1)} %collective-permute-done.17.gate_b, ...), custom_call_target="tpu_custom_call" | custom-call | flops 9663676416 | bytes 27262976 | tf_op jit(solution)/shard_map/expert_partial/pallas_call | solution.py:264
  148.6 43.0 %all_to_all.17 = bf16[16,32,4096]{2,1,0:T(8,128)(2,1)S(1)} all-to-all(bf16[16,32,4096]{2,1,0:T(8,128)(2,1)} %bitcast.32), channel_id=1, replica_groups=mesh['x'=4,'y'=4,'c'=2,'z'=8] {'x','y'}, dimensions={0} | all-to-all | bytes 8388608 | tf_op jit(solution)/shard_map/all_to_all | solution.py:357
  192.4 2.8 %collective-permute-start.24 = (bf16[64,512]{1,0:T(8,128)(2,1)S(1)}, bf16[64,512]{1,0:T(8,128)(2,1)S(1)}, u32[]{:S(2)}, u32[]{:S(2)}) collective-permute-start(bf16[64,512]{1,0:T(8,128)(2,1)S(1)} %get-tuple-element.38), channel_id=1, source_target_pairs={{0,7},{1,0},{2,1},{3,2},{4,3},{5,4},{6,5},{7,6},{8,15},{9,8},{10,9... | collective-permute-start | bytes 196616 | tf_op jit(solution)/shard_map/ppermute | solution.py:54
  197.2 3.6 %collective-permute-start.25 = (bf16[128,512]{1,0:T(8,128)(2,1)S(1)}, bf16[128,512]{1,0:T(8,128)(2,1)S(1)}, u32[]{:S(2)}, u32[]{:S(2)}) collective-permute-start(bf16[128,512]{1,0:T(8,128)(2,1)S(1)} %pad_maximum_fusion.3), channel_id=1, source_target_pairs={{0,7},{1,0},{2,1},{3,2},{4,3},{5,4},{6,5},{7,6},{8,15},{9,8},{10,9... | collective-permute-start | bytes 393224 | tf_op jit(solution)/shard_map/ppermute | solution.py:63
  201.0 2.4 %collective-permute-done.25 = bf16[128,512]{1,0:T(8,128)(2,1)S(1)} collective-permute-done((bf16[128,512]{1,0:T(8,128)(2,1)S(1)}, bf16[128,512]{1,0:T(8,128)(2,1)S(1)}, u32[]{:S(2)}, u32[]{:S(2)}) %collective-permute-start.25) | collective-permute-done | bytes 131104 | tf_op jit(solution)/shard_map/ppermute | solution.py:63
  203.4 3.7 %collective-permute-start.26 = (bf16[128,512]{1,0:T(8,128)(2,1)S(1)}, bf16[128,512]{1,0:T(8,128)(2,1)S(1)}, u32[]{:S(2)}, u32[]{:S(2)}) collective-permute-start(bf16[128,512]{1,0:T(8,128)(2,1)S(1)} %add_convert_fusion.2), channel_id=1, source_target_pairs={{0,7},{1,0},{2,1},{3,2},{4,3},{5,4},{6,5},{7,6},{8,15},{9,8},{10,9... | collective-permute-start | bytes 393224 | tf_op jit(solution)/shard_map/ppermute | solution.py:63
  209.7 3.7 %collective-permute-start.27 = (bf16[128,512]{1,0:T(8,128)(2,1)S(1)}, bf16[128,512]{1,0:T(8,128)(2,1)S(1)}, u32[]{:S(2)}, u32[]{:S(2)}) collective-permute-start(bf16[128,512]{1,0:T(8,128)(2,1)S(1)} %add_convert_fusion.1), channel_id=1, source_target_pairs={{0,7},{1,0},{2,1},{3,2},{4,3},{5,4},{6,5},{7,6},{8,15},{9,8},{10,9... | collective-permute-start | bytes 393224 | tf_op jit(solution)/shard_map/ppermute | solution.py:63
  216.0 3.8 %collective-permute-done.23 = bf16[128,512]{1,0:T(8,128)(2,1)S(1)} collective-permute-done((bf16[128,512]{1,0:T(8,128)(2,1)S(1)}, bf16[128,512]{1,0:T(8,128)(2,1)S(1)}, u32[]{:S(2)}, u32[]{:S(2)}) %collective-permute-start.23) | collective-permute-done | bytes 131104 | tf_op jit(solution)/shard_map/ppermute | solution.py:62
  (93 shorter events, 27.7 us)
Async XLA Ops:
  23.3 67.0 %collective-permute-start.17 = (bf16[4096,384]{1,0:T(8,128)(2,1)}, bf16[4096,384]{1,0:T(8,128)(2,1)}, u32[]{:S(2)}, u32[]{:S(2)}) collective-permute-start(bf16[4096,384]{1,0:T(8,128)(2,1)} %bitcast.8.gate_a), channel_id=1, source_target_pairs={{0,8},{8,0},{1,9},{9,1},{2,10},{10,2},{3,11},{11,3},{4,12},{12,4},... | collective-permute-start | bytes 9437192 | tf_op jit(solution)/shard_map/ppermute | solution.py:20
  23.8 66.5 %collective-permute-start.18 = (bf16[4096,384]{1,0:T(8,128)(2,1)}, bf16[4096,384]{1,0:T(8,128)(2,1)}, u32[]{:S(2)}, u32[]{:S(2)}) collective-permute-start(bf16[4096,384]{1,0:T(8,128)(2,1)} %bitcast.9.up_a), channel_id=1, source_target_pairs={{0,8},{8,0},{1,9},{9,1},{2,10},{10,2},{3,11},{11,3},{4,12},{12,4},... | collective-permute-start | bytes 9437192 | tf_op jit(solution)/shard_map/ppermute | solution.py:20
  23.8 66.5 %collective-permute-start.19 = (bf16[384,4096]{1,0:T(8,128)(2,1)}, bf16[384,4096]{1,0:T(8,128)(2,1)}, u32[]{:S(2)}, u32[]{:S(2)}) collective-permute-start(bf16[384,4096]{1,0:T(8,128)(2,1)} %bitcast.10.down_a), channel_id=1, source_target_pairs={{0,8},{8,0},{1,9},{9,1},{2,10},{10,2},{3,11},{11,3},{4,12},{12,4},... | collective-permute-start | bytes 9437192 | tf_op jit(solution)/shard_map/ppermute | solution.py:20
  31.6 8.3 %collective-permute-start.1 = (bf16[64,512]{1,0:T(8,128)(2,1)S(1)}, bf16[64,512]{1,0:T(8,128)(2,1)S(1)}, u32[]{:S(2)}, u32[]{:S(2)}) collective-permute-start(bf16[64,512]{1,0:T(8,128)(2,1)S(1)} %get-tuple-element.43), channel_id=1, source_target_pairs={{0,1},{1,2},{2,3},{3,4},{4,5},{5,6},{6,7},{7,0},{8,9},{9,10},{10,1... | collective-permute-start | bytes 196616 | tf_op jit(solution)/shard_map/ppermute | solution.py:53
  33.6 6.3 %collective-permute-start.5 = (bf16[64,512]{1,0:T(8,128)(2,1)S(1)}, bf16[64,512]{1,0:T(8,128)(2,1)S(1)}, u32[]{:S(2)}, u32[]{:S(2)}) collective-permute-start(bf16[64,512]{1,0:T(8,128)(2,1)S(1)} %get-tuple-element.44), channel_id=1, source_target_pairs={{0,7},{1,0},{2,1},{3,2},{4,3},{5,4},{6,5},{7,6},{8,15},{9,8},{10,9... | collective-permute-start | bytes 196616 | tf_op jit(solution)/shard_map/ppermute | solution.py:54
  40.0 6.3 %collective-permute-start.2 = (bf16[128,512]{1,0:T(8,128)(2,1)S(1)}, bf16[128,512]{1,0:T(8,128)(2,1)S(1)}, u32[]{:S(2)}, u32[]{:S(2)}) collective-permute-start(bf16[128,512]{1,0:T(8,128)(2,1)S(1)} %pad_maximum_fusion), channel_id=1, source_target_pairs={{0,1},{1,2},{2,3},{3,4},{4,5},{5,6},{6,7},{7,0},{8,9},{9,10},{10,1... | collective-permute-start | bytes 393224 | tf_op jit(solution)/shard_map/ppermute | solution.py:62
  40.1 6.3 %collective-permute-start.6 = (bf16[128,512]{1,0:T(8,128)(2,1)S(1)}, bf16[128,512]{1,0:T(8,128)(2,1)S(1)}, u32[]{:S(2)}, u32[]{:S(2)}) collective-permute-start(bf16[128,512]{1,0:T(8,128)(2,1)S(1)} %pad_maximum_fusion.1), channel_id=1, source_target_pairs={{0,7},{1,0},{2,1},{3,2},{4,3},{5,4},{6,5},{7,6},{8,15},{9,8},{10,9... | collective-permute-start | bytes 393224 | tf_op jit(solution)/shard_map/ppermute | solution.py:63
  46.3 6.3 %collective-permute-start.3 = (bf16[128,512]{1,0:T(8,128)(2,1)S(1)}, bf16[128,512]{1,0:T(8,128)(2,1)S(1)}, u32[]{:S(2)}, u32[]{:S(2)}) collective-permute-start(bf16[128,512]{1,0:T(8,128)(2,1)S(1)} %add_convert_fusion.9), channel_id=1, source_target_pairs={{0,1},{1,2},{2,3},{3,4},{4,5},{5,6},{6,7},{7,0},{8,9},{9,10},{10,1... | collective-permute-start | bytes 393224 | tf_op jit(solution)/shard_map/ppermute | solution.py:62
  52.7 6.0 %collective-permute-start.7 = (bf16[128,512]{1,0:T(8,128)(2,1)S(1)}, bf16[128,512]{1,0:T(8,128)(2,1)S(1)}, u32[]{:S(2)}, u32[]{:S(2)}) collective-permute-start(bf16[128,512]{1,0:T(8,128)(2,1)S(1)} %get-tuple-element.40), channel_id=1, source_target_pairs={{0,7},{1,0},{2,1},{3,2},{4,3},{5,4},{6,5},{7,6},{8,15},{9,8},{10,9... | collective-permute-start | bytes 393224 | tf_op jit(solution)/shard_map/ppermute | solution.py:63
  53.5 6.4 %collective-permute-start.4 = (bf16[128,512]{1,0:T(8,128)(2,1)S(1)}, bf16[128,512]{1,0:T(8,128)(2,1)S(1)}, u32[]{:S(2)}, u32[]{:S(2)}) collective-permute-start(bf16[128,512]{1,0:T(8,128)(2,1)S(1)} %get-tuple-element.39), channel_id=1, source_target_pairs={{0,1},{1,2},{2,3},{3,4},{4,5},{5,6},{6,7},{7,0},{8,9},{9,10},{10,1... | collective-permute-start | bytes 393224 | tf_op jit(solution)/shard_map/ppermute | solution.py:62
  58.7 6.3 %collective-permute-start.8 = (bf16[128,512]{1,0:T(8,128)(2,1)S(1)}, bf16[128,512]{1,0:T(8,128)(2,1)S(1)}, u32[]{:S(2)}, u32[]{:S(2)}) collective-permute-start(bf16[128,512]{1,0:T(8,128)(2,1)S(1)} %add_convert_fusion.6), channel_id=1, source_target_pairs={{0,7},{1,0},{2,1},{3,2},{4,3},{5,4},{6,5},{7,6},{8,15},{9,8},{10,9... | collective-permute-start | bytes 393224 | tf_op jit(solution)/shard_map/ppermute | solution.py:63
  65.0 6.4 %collective-permute-start.12 = (bf16[128,512]{1,0:T(8,128)(2,1)S(1)}, bf16[128,512]{1,0:T(8,128)(2,1)S(1)}, u32[]{:S(2)}, u32[]{:S(2)}) collective-permute-start(bf16[128,512]{1,0:T(8,128)(2,1)S(1)} %add_convert_fusion.5.refs_0_), channel_id=1, source_target_pairs={{0,1},{1,2},{2,3},{3,4},{4,5},{5,6},{6,7},{7,0},{8,9},{9,10},{10,1... | collective-permute-start | bytes 393224 | tf_op jit(solution)/shard_map/ppermute | solution.py:34
  65.3 6.3 %collective-permute-start.9 = (bf16[128,512]{1,0:T(8,128)(2,1)S(1)}, bf16[128,512]{1,0:T(8,128)(2,1)S(1)}, u32[]{:S(2)}, u32[]{:S(2)}) collective-permute-start(bf16[128,512]{1,0:T(8,128)(2,1)S(1)} %add_convert_fusion.5.refs_0_), channel_id=1, source_target_pairs={{0,7},{1,0},{2,1},{3,2},{4,3},{5,4},{6,5},{7,6},{8,15},{9,8},{10,9... | collective-permute-start | bytes 393224 | tf_op jit(solution)/shard_map/ppermute | solution.py:35
  71.5 6.2 %collective-permute-start.13 = (bf16[128,512]{1,0:T(8,128)(2,1)S(1)}, bf16[128,512]{1,0:T(8,128)(2,1)S(1)}, u32[]{:S(2)}, u32[]{:S(2)}) collective-permute-start(bf16[128,512]{1,0:T(8,128)(2,1)S(1)} %collective-permute-done.12.refs_8_), channel_id=1, source_target_pairs={{0,1},{1,2},{2,3},{3,4},{4,5},{5,6},{6,7},{7,0},{8,9},{9,10},{10,1... | collective-permute-start | bytes 393224 | tf_op jit(solution)/shard_map/ppermute | solution.py:34
  71.6 7.5 %collective-permute-start.10 = (bf16[128,512]{1,0:T(8,128)(2,1)S(1)}, bf16[128,512]{1,0:T(8,128)(2,1)S(1)}, u32[]{:S(2)}, u32[]{:S(2)}) collective-permute-start(bf16[128,512]{1,0:T(8,128)(2,1)S(1)} %collective-permute-done.9.refs_1_), channel_id=1, source_target_pairs={{0,7},{1,0},{2,1},{3,2},{4,3},{5,4},{6,5},{7,6},{8,15},{9,8},{10,9... | collective-permute-start | bytes 393224 | tf_op jit(solution)/shard_map/ppermute | solution.py:35
  77.6 6.2 %collective-permute-start.14 = (bf16[128,512]{1,0:T(8,128)(2,1)S(1)}, bf16[128,512]{1,0:T(8,128)(2,1)S(1)}, u32[]{:S(2)}, u32[]{:S(2)}) collective-permute-start(bf16[128,512]{1,0:T(8,128)(2,1)S(1)} %collective-permute-done.13.refs_7_), channel_id=1, source_target_pairs={{0,1},{1,2},{2,3},{3,4},{4,5},{5,6},{6,7},{7,0},{8,9},{9,10},{10,1... | collective-permute-start | bytes 393224 | tf_op jit(solution)/shard_map/ppermute | solution.py:34
  83.8 5.5 %collective-permute-start.15 = (bf16[64,512]{1,0:T(8,128)(2,1)S(1)}, bf16[64,512]{1,0:T(8,128)(2,1)S(1)}, u32[]{:S(2)}, u32[]{:S(2)}) collective-permute-start(bf16[64,512]{1,0:T(8,128)(2,1)S(1)} %slice.88), channel_id=1, source_target_pairs={{0,1},{1,2},{2,3},{3,4},{4,5},{5,6},{6,7},{7,0},{8,9},{9,10},{10,1... | collective-permute-start | bytes 196616 | tf_op jit(solution)/shard_map/ppermute | solution.py:37
  195.3 5.6 %collective-permute-start.20 = (bf16[64,512]{1,0:T(8,128)(2,1)S(1)}, bf16[64,512]{1,0:T(8,128)(2,1)S(1)}, u32[]{:S(2)}, u32[]{:S(2)}) collective-permute-start(bf16[64,512]{1,0:T(8,128)(2,1)S(1)} %get-tuple-element.34), channel_id=1, source_target_pairs={{0,1},{1,2},{2,3},{3,4},{4,5},{5,6},{6,7},{7,0},{8,9},{9,10},{10,1... | collective-permute-start | bytes 196616 | tf_op jit(solution)/shard_map/ppermute | solution.py:53
  197.2 6.2 %collective-permute-start.25 = (bf16[128,512]{1,0:T(8,128)(2,1)S(1)}, bf16[128,512]{1,0:T(8,128)(2,1)S(1)}, u32[]{:S(2)}, u32[]{:S(2)}) collective-permute-start(bf16[128,512]{1,0:T(8,128)(2,1)S(1)} %pad_maximum_fusion.3), channel_id=1, source_target_pairs={{0,7},{1,0},{2,1},{3,2},{4,3},{5,4},{6,5},{7,6},{8,15},{9,8},{10,9... | collective-permute-start | bytes 393224 | tf_op jit(solution)/shard_map/ppermute | solution.py:63
  200.9 6.3 %collective-permute-start.21 = (bf16[128,512]{1,0:T(8,128)(2,1)S(1)}, bf16[128,512]{1,0:T(8,128)(2,1)S(1)}, u32[]{:S(2)}, u32[]{:S(2)}) collective-permute-start(bf16[128,512]{1,0:T(8,128)(2,1)S(1)} %pad_maximum_fusion.2), channel_id=1, source_target_pairs={{0,1},{1,2},{2,3},{3,4},{4,5},{5,6},{6,7},{7,0},{8,9},{9,10},{10,1... | collective-permute-start | bytes 393224 | tf_op jit(solution)/shard_map/ppermute | solution.py:62
  203.4 6.3 %collective-permute-start.26 = (bf16[128,512]{1,0:T(8,128)(2,1)S(1)}, bf16[128,512]{1,0:T(8,128)(2,1)S(1)}, u32[]{:S(2)}, u32[]{:S(2)}) collective-permute-start(bf16[128,512]{1,0:T(8,128)(2,1)S(1)} %add_convert_fusion.2), channel_id=1, source_target_pairs={{0,7},{1,0},{2,1},{3,2},{4,3},{5,4},{6,5},{7,6},{8,15},{9,8},{10,9... | collective-permute-start | bytes 393224 | tf_op jit(solution)/shard_map/ppermute | solution.py:63
  207.2 6.3 %collective-permute-start.22 = (bf16[128,512]{1,0:T(8,128)(2,1)S(1)}, bf16[128,512]{1,0:T(8,128)(2,1)S(1)}, u32[]{:S(2)}, u32[]{:S(2)}) collective-permute-start(bf16[128,512]{1,0:T(8,128)(2,1)S(1)} %add_convert_fusion.4), channel_id=1, source_target_pairs={{0,1},{1,2},{2,3},{3,4},{4,5},{5,6},{6,7},{7,0},{8,9},{9,10},{10,1... | collective-permute-start | bytes 393224 | tf_op jit(solution)/shard_map/ppermute | solution.py:62
  209.7 6.3 %collective-permute-start.27 = (bf16[128,512]{1,0:T(8,128)(2,1)S(1)}, bf16[128,512]{1,0:T(8,128)(2,1)S(1)}, u32[]{:S(2)}, u32[]{:S(2)}) collective-permute-start(bf16[128,512]{1,0:T(8,128)(2,1)S(1)} %add_convert_fusion.1), channel_id=1, source_target_pairs={{0,7},{1,0},{2,1},{3,2},{4,3},{5,4},{6,5},{7,6},{8,15},{9,8},{10,9... | collective-permute-start | bytes 393224 | tf_op jit(solution)/shard_map/ppermute | solution.py:63
  213.5 6.3 %collective-permute-start.23 = (bf16[128,512]{1,0:T(8,128)(2,1)S(1)}, bf16[128,512]{1,0:T(8,128)(2,1)S(1)}, u32[]{:S(2)}, u32[]{:S(2)}) collective-permute-start(bf16[128,512]{1,0:T(8,128)(2,1)S(1)} %add_convert_fusion.3), channel_id=1, source_target_pairs={{0,1},{1,2},{2,3},{3,4},{4,5},{5,6},{6,7},{7,0},{8,9},{9,10},{10,1... | collective-permute-start | bytes 393224 | tf_op jit(solution)/shard_map/ppermute | solution.py:62
  (12 other events, 287.2 us)

commit v7 on v6

--- a/solution.py
+++ b/solution.py
@@ -23,6 +23,11 @@
 def gather_by_exchange(array, axes, count):
     spread = jnp.broadcast_to(array[None], (count,) + array.shape)
     return lax.all_to_all(spread, axes, split_axis=0, concat_axis=0, tiled=True)
+
+
+def shift(array, hops):
+    depth = lax.axis_size("z")
+    return lax.ppermute(array, "z", [(i, (i + hops) % depth) for i in range(depth)])
 
 
 def gather_ring(piece, depth):
@@ -41,6 +46,25 @@
 
 
 def sum_ring(slices, depth):
+    assert depth == 8
+    first, second = slices[4]
+    half = first.shape[0]
+    near = shift(slices[3], 1).astype(F32), shift(slices[5], -1).astype(F32)
+    far = shift(first, 2).astype(F32), shift(second, -2).astype(F32)
+    forward = slices[2].astype(F32) + near[0]
+    backward = slices[6].astype(F32) + near[1]
+    forward = jnp.concatenate([forward[:half] + far[0], forward[half:]], axis=0)
+    backward = jnp.concatenate([backward[:half], backward[half:] + far[1]], axis=0)
+    arrived = [
+        shift(slices[1], 1),
+        shift(slices[7], -1),
+        shift(forward.astype(BF), 2),
+        shift(backward.astype(BF), -2),
+    ]
+    return sum((part.astype(F32) for part in arrived), slices[0].astype(F32))
+
+
+def sum_long_ring(slices, depth):
     ahead = [(i, (i + 1) % depth) for i in range(depth)]
     behind = [(i, (i + depth - 1) % depth) for i in range(depth)]
 
@@ -68,6 +92,10 @@
     return [pltpu.with_memory_space_constraint(operand, pltpu.VMEM) for operand in operands]
 
 
+def in_hbm(operand):
+    return pltpu.with_memory_space_constraint(operand, pltpu.HBM)
+
+
 def slice_shapes(depth, rows, width):
     shapes = [jax.ShapeDtypeStruct((rows, width), BF)] * (depth + 1)
     shapes[depth // 2] = shapes[depth // 2 + 1] = jax.ShapeDtypeStruct((rows // 2, width), BF)
@@ -95,7 +123,11 @@
             outs[far + 1][...] = product[half:]
 
 
-def attention_kernel(group, queries, own_kv, other_kv, out_proj, out):
+def attention_kernel(
+    group, queries, own_kv, other_kv, out_proj_hbm, out, out_proj, proj_sem
+):
+    proj_copy = pltpu.make_async_copy(out_proj_hbm, out_proj, proj_sem)
+    proj_copy.start()
     tokens, width = queries.shape
     heads = width // HD
     stacked = jnp.concatenate(
@@ -117,6 +149,7 @@
     attended = jnp.concatenate(
         [attended[head * tokens : (head + 1) * tokens] for head in range(heads)], axis=1
     )
+    proj_copy.wait()
     depth = out_proj.shape[1] // SLICE
     for offset in range(depth):
         start = pl.multiple_of(lax.rem(group[0] + offset, depth) * SLICE, SLICE)
@@ -132,11 +165,13 @@
         attention_kernel,
         out_shape=jax.ShapeDtypeStruct((tokens, out_proj.shape[1]), BF),
         in_specs=[pl.BlockSpec(memory_space=pltpu.SMEM)]
-        + [pl.BlockSpec(memory_space=pltpu.VMEM)] * 4,
+        + [pl.BlockSpec(memory_space=pltpu.VMEM)] * 3
+        + [pl.BlockSpec(memory_space=pl.ANY)],
         out_specs=pl.BlockSpec(memory_space=pltpu.VMEM),
+        scratch_shapes=[pltpu.VMEM(out_proj.shape, BF), pltpu.SemaphoreType.DMA],
         compiler_params=pltpu.CompilerParams(vmem_limit_bytes=32 * 2**20),
         name="attention",
-    )(group, *in_vmem(queries, own_kv, other_kv, out_proj))
+    )(group, *in_vmem(queries, own_kv, other_kv), in_hbm(out_proj))
     slices = [total[:, offset * SLICE : (offset + 1) * SLICE] for offset in range(depth)]
     far = slices[depth // 2]
     slices[depth // 2] = (far[: tokens // 2], far[tokens // 2 :])
@@ -263,7 +298,7 @@
     part = parts[0].shape[1]
     return pl.pallas_call(
         expert_kernel,
-        out_shape=jax.ShapeDtypeStruct((count, depth), BF),
+        out_shape=pltpu.VMEM((count, depth), BF),
         in_specs=[pl.BlockSpec(memory_space=pltpu.VMEM)]
         + [pl.BlockSpec(memory_space=pl.ANY)] * len(parts),
         out_specs=pl.BlockSpec(memory_space=pltpu.VMEM),
@@ -276,7 +311,7 @@
             pltpu.SemaphoreType.DMA((4, len(EIGHTHS) - 1)),
             pltpu.SemaphoreType.DMA((2,)),
         ],
-        compiler_params=pltpu.CompilerParams(vmem_limit_bytes=40 * 2**20),
+        compiler_params=pltpu.CompilerParams(vmem_limit_bytes=36 * 2**20),
         cost_estimate=pl.CostEstimate(
             flops=12 * count * depth * part,
             bytes_accessed=12 * depth * part + 4 * count * depth,
@@ -315,7 +350,7 @@
     other_parts = tuple(swap_cores(part[0]) for part in (gate_proj, up_proj, down_proj))
 
     group = group_index.astype(jnp.int32).reshape(1)
-    attn_share = sum_ring(
+    attn_share = sum_long_ring(
         attention_slices(group, queries, own_kv, other_kv, out_proj, depth), depth
     )
     mixed_local = (residual_in.astype(F32) + attn_share).astype(BF)

time: 222 us -> 214 us (0.964)
  waiting for transfers between devices: 47.8 us -> 44.4 us
    ppermute x16, waiting for transfers between devices: 33.1 us -> 29.7 us  [the longest x8 9.39 us: shift(): lax.ppermute(array, 'z', [(i, (i + hops) % depth) for i in range(depth)])]
  transfers between devices with their start and end apart: 28 -> 28, of which waited for: 17 -> 15; matrix products, arithmetic and copies ran while one was open for 1% -> 1% of each run, Pallas kernels for 2% -> 2%
where the time goes in v7:
time: 214 us; the launch traced here: 213 us
  blocking collectives  109 us (51%)
  waiting for transfers between devices  44.4 us (21%)
  starting transfers between devices  38 us (18%)
  Pallas kernels  18.1 us (8%)
  other arithmetic  2.46 us (1%)
    all_to_all x1, blocking collectives, shards(): lax.all_to_all(outgoing, ('x', 'y'), split_axis=0, concat_axis=0, tiled=T...  43.9 us
    all_to_all x1, blocking collectives, shards(): lax.all_to_all(partial_out.reshape(arrived.shape), ('x', 'y'), split_axis...  43.1 us
    all_to_all x1, blocking collectives, gather_by_exchange(): return lax.all_to_all(spread, axes, split_axis=0, concat_axis=0, tiled=True)  22.4 us
    ppermute x8, starting transfers between devices, shift(): lax.ppermute(array, 'z', [(i, (i + hops) % depth) for i in range(depth)])  12.4 us
    pallas_call x1, Pallas kernels, expert_partial(): pl.pallas_call(expert_kernel, out_shape=pltpu.VMEM((count, depth), BF), i...  12.4 us
    ppermute x8, waiting for transfers between devices, shift(): lax.ppermute(array, 'z', [(i, (i + hops) % depth) for i in range(depth)])  9.39 us
    ppermute x3, waiting for transfers between devices, sum_long_ring(): forward = lax.ppermute(forward, 'z', ahead)  9.07 us
    ppermute x3, waiting for transfers between devices, sum_long_ring(): backward = lax.ppermute(backward, 'z', behind)  8.97 us
  transfers between devices with their start and end apart: 28, of which 15 were waited for; matrix products, arithmetic and copies ran while one was open for 1% of the time, Pallas kernels for 2%

profile of v7, /device:TPU:6, one launch (start us, length us, event | category | flops | bytes accessed | tf_op | source)
XLA Modules:
  0.0 213.2 jit_solution(15444007179506399606)
XLA Ops:
  0.9 22.4 %all_to_all.15 = bf16[16,128,256]{2,1,0:T(8,128)(2,1)S(1)} all-to-all(bf16[16,128,256]{2,1,0:T(8,128)(2,1)S(1)} %broadcast_in_dim.21), channel_id=1, replica_groups=mesh['x'=4,'y'=4,'c'=2,'z'=8] {'x','y'}, dimensions={0} | all-to-all | bytes 2097152 | tf_op jit(solution)/shard_map/all_to_all | solution.py:25
  24.3 3.1 %collective-permute-done.other_kv = bf16[2048,256]{1,0:T(8,128)(2,1)S(1)} collective-permute-done((bf16[2048,256]{1,0:T(8,128)(2,1)S(1)}, bf16[2048,256]{1,0:T(8,128)(2,1)S(1)}, u32[]{:S(2)}, u32[]{:S(2)}) %collective-permute-start) | collective-permute-done | bytes 1048608 | tf_op jit(solution)/shard_map/ppermute | solution.py:20
  27.4 3.9 %attention.1 = bf16[128,4096]{1,0:T(8,128)(2,1)S(1)} custom-call(s32[1]{0:T(128)} %bitcast.group, bf16[128,256]{1,0:T(8,128)(2,1)S(1)} %copy-done, bf16[2048,256]{1,0:T(8,128)(2,1)S(1)} %bitcast.30, bf16[2048,256]{1,0:T(8,128)(2,1)S(1)} %collective-permute-done.other_kv, bf16[256,4096]{1,0:T(8,128)(2,1)} %out_proj_hbm.1), custom_call_target="tpu_custom_call" | custom-call | tf_op jit(solution)/shard_map/attention/pallas_call | solution.py:164
  33.4 4.0 %collective-permute-start.5 = (bf16[64,512]{1,0:T(8,128)(2,1)S(1)}, bf16[64,512]{1,0:T(8,128)(2,1)S(1)}, u32[]{:S(2)}, u32[]{:S(2)}) collective-permute-start(bf16[64,512]{1,0:T(8,128)(2,1)S(1)} %get-tuple-element.44), channel_id=1, source_target_pairs={{0,7},{1,0},{2,1},{3,2},{4,3},{5,4},{6,5},{7,6},{8,15},{9,8},{10,9... | collective-permute-start | bytes 196616 | tf_op jit(solution)/shard_map/ppermute | solution.py:78
  39.9 3.3 %collective-permute-start.6 = (bf16[128,512]{1,0:T(8,128)(2,1)S(1)}, bf16[128,512]{1,0:T(8,128)(2,1)S(1)}, u32[]{:S(2)}, u32[]{:S(2)}) collective-permute-start(bf16[128,512]{1,0:T(8,128)(2,1)S(1)} %pad_maximum_fusion.1), channel_id=1, source_target_pairs={{0,7},{1,0},{2,1},{3,2},{4,3},{5,4},{6,5},{7,6},{8,15},{9,8},{10,9... | collective-permute-start | bytes 393224 | tf_op jit(solution)/shard_map/ppermute | solution.py:87
  43.2 2.9 %collective-permute-done.2 = bf16[128,512]{1,0:T(8,128)(2,1)S(1)} collective-permute-done((bf16[128,512]{1,0:T(8,128)(2,1)S(1)}, bf16[128,512]{1,0:T(8,128)(2,1)S(1)}, u32[]{:S(2)}, u32[]{:S(2)}) %collective-permute-start.2) | collective-permute-done | bytes 131104 | tf_op jit(solution)/shard_map/ppermute | solution.py:86
  46.3 6.2 %collective-permute-done.3 = bf16[128,512]{1,0:T(8,128)(2,1)S(1)} collective-permute-done((bf16[128,512]{1,0:T(8,128)(2,1)S(1)}, bf16[128,512]{1,0:T(8,128)(2,1)S(1)}, u32[]{:S(2)}, u32[]{:S(2)}) %collective-permute-start.3) | collective-permute-done | bytes 131104 | tf_op jit(solution)/shard_map/ppermute | solution.py:86
  54.6 3.9 %collective-permute-done.7 = bf16[128,512]{1,0:T(8,128)(2,1)S(1)} collective-permute-done((bf16[128,512]{1,0:T(8,128)(2,1)S(1)}, bf16[128,512]{1,0:T(8,128)(2,1)S(1)}, u32[]{:S(2)}, u32[]{:S(2)}) %collective-permute-start.7) | collective-permute-done | bytes 131104 | tf_op jit(solution)/shard_map/ppermute | solution.py:87
  59.7 5.1 %collective-permute-done.8 = bf16[128,512]{1,0:T(8,128)(2,1)S(1)} collective-permute-done((bf16[128,512]{1,0:T(8,128)(2,1)S(1)}, bf16[128,512]{1,0:T(8,128)(2,1)S(1)}, u32[]{:S(2)}, u32[]{:S(2)}) %collective-permute-start.8) | collective-permute-done | bytes 131104 | tf_op jit(solution)/shard_map/ppermute | solution.py:87
  65.1 3.2 %collective-permute-start.9 = (bf16[128,512]{1,0:T(8,128)(2,1)S(1)}, bf16[128,512]{1,0:T(8,128)(2,1)S(1)}, u32[]{:S(2)}, u32[]{:S(2)}) collective-permute-start(bf16[128,512]{1,0:T(8,128)(2,1)S(1)} %add_convert_fusion.1.refs_0_), channel_id=1, source_target_pairs={{0,7},{1,0},{2,1},{3,2},{4,3},{5,4},{6,5},{7,6},{8,15},{9,8},{10,9... | collective-permute-start | bytes 393224 | tf_op jit(solution)/shard_map/ppermute | solution.py:40
  68.4 2.9 %collective-permute-done.12.refs_8_ = bf16[128,512]{1,0:T(8,128)(2,1)S(1)} collective-permute-done((bf16[128,512]{1,0:T(8,128)(2,1)S(1)}, bf16[128,512]{1,0:T(8,128)(2,1)S(1)}, u32[]{:S(2)}, u32[]{:S(2)}) %collective-permute-start.12) | collective-permute-done | bytes 131104 | tf_op jit(solution)/shard_map/ppermute | solution.py:39
  71.4 3.1 %collective-permute-start.10 = (bf16[128,512]{1,0:T(8,128)(2,1)S(1)}, bf16[128,512]{1,0:T(8,128)(2,1)S(1)}, u32[]{:S(2)}, u32[]{:S(2)}) collective-permute-start(bf16[128,512]{1,0:T(8,128)(2,1)S(1)} %collective-permute-done.9.refs_1_), channel_id=1, source_target_pairs={{0,7},{1,0},{2,1},{3,2},{4,3},{5,4},{6,5},{7,6},{8,15},{9,8},{10,9... | collective-permute-start | bytes 393224 | tf_op jit(solution)/shard_map/ppermute | solution.py:40
  74.8 2.7 %collective-permute-done.13.refs_7_ = bf16[128,512]{1,0:T(8,128)(2,1)S(1)} collective-permute-done((bf16[128,512]{1,0:T(8,128)(2,1)S(1)}, bf16[128,512]{1,0:T(8,128)(2,1)S(1)}, u32[]{:S(2)}, u32[]{:S(2)}) %collective-permute-start.13) | collective-permute-done | bytes 131104 | tf_op jit(solution)/shard_map/ppermute | solution.py:39
  80.9 2.8 %collective-permute-done.14.refs_6_ = bf16[128,512]{1,0:T(8,128)(2,1)S(1)} collective-permute-done((bf16[128,512]{1,0:T(8,128)(2,1)S(1)}, bf16[128,512]{1,0:T(8,128)(2,1)S(1)}, u32[]{:S(2)}, u32[]{:S(2)}) %collective-permute-start.14) | collective-permute-done | bytes 131104 | tf_op jit(solution)/shard_map/ppermute | solution.py:39
  83.9 3.1 %collective-permute-start.16 = (bf16[64,512]{1,0:T(8,128)(2,1)S(1)}, bf16[64,512]{1,0:T(8,128)(2,1)S(1)}, u32[]{:S(2)}, u32[]{:S(2)}) collective-permute-start(bf16[64,512]{1,0:T(8,128)(2,1)S(1)} %slice.91), channel_id=1, source_target_pairs={{0,7},{1,0},{2,1},{3,2},{4,3},{5,4},{6,5},{7,6},{8,15},{9,8},{10,9... | collective-permute-start | bytes 196616 | tf_op jit(solution)/shard_map/ppermute | solution.py:43
  90.2 43.9 %all_to_all.16 = bf16[16,32,4096]{2,1,0:T(8,128)(2,1)S(1)} all-to-all(bf16[16,32,4096]{2,1,0:T(8,128)(2,1)S(1)} %bitcast.25), channel_id=1, replica_groups=mesh['x'=4,'y'=4,'c'=2,'z'=8] {'x','y'}, dimensions={0} | all-to-all | bytes 8388608 | tf_op jit(solution)/shard_map/all_to_all | solution.py:388
  134.1 12.4 %expert_partial.1 = bf16[512,4096]{1,0:T(8,128)(2,1)S(1)} custom-call(bf16[512,4096]{1,0:T(8,128)(2,1)S(1)} %bitcast.27, bf16[4096,384]{1,0:T(8,128)(2,1)} %bitcast.8.gate_a, bf16[4096,384]{1,0:T(8,128)(2,1)} %bitcast.9.up_a, bf16[384,4096]{1,0:T(8,128)(2,1)} %bitcast.10.down_a, bf16[4096,384]{1,0:T(8,128)(2,1)} %collective-permute-done.17.gate_b, ...), custom_call_target="tpu_custom_call" | custom-call | flops 9663676416 | bytes 27262976 | tf_op jit(solution)/shard_map/expert_partial/pallas_call | solution.py:299
  146.5 43.1 %all_to_all.17 = bf16[16,32,4096]{2,1,0:T(8,128)(2,1)S(1)} all-to-all(bf16[16,32,4096]{2,1,0:T(8,128)(2,1)S(1)} %bitcast.28), channel_id=1, replica_groups=mesh['x'=4,'y'=4,'c'=2,'z'=8] {'x','y'}, dimensions={0} | all-to-all | bytes 8388608 | tf_op jit(solution)/shard_map/all_to_all | solution.py:392
  190.6 4.5 %collective-permute-start.23 = (bf16[64,512]{1,0:T(8,128)(2,1)S(1)}, bf16[64,512]{1,0:T(8,128)(2,1)S(1)}, u32[]{:S(2)}, u32[]{:S(2)}) collective-permute-start(bf16[64,512]{1,0:T(8,128)(2,1)S(1)} %get-tuple-element.35), channel_id=1, source_target_pairs={{0,2},{1,3},{2,4},{3,5},{4,6},{5,7},{6,0},{7,1},{8,10},{9,11},{10,... | collective-permute-start | bytes 196616 | tf_op jit(solution)/shard_map/ppermute | solution.py:30
  195.1 4.0 %collective-permute-start.20 = (bf16[128,512]{1,0:T(8,128)(2,1)S(1)}, bf16[128,512]{1,0:T(8,128)(2,1)S(1)}, u32[]{:S(2)}, u32[]{:S(2)}) collective-permute-start(bf16[128,512]{1,0:T(8,128)(2,1)S(1)} %get-tuple-element.31), channel_id=1, source_target_pairs={{0,1},{1,2},{2,3},{3,4},{4,5},{5,6},{6,7},{7,0},{8,9},{9,10},{10,1... | collective-permute-start | bytes 393224 | tf_op jit(solution)/shard_map/ppermute | solution.py:30
  199.8 3.0 %collective-permute-start.24 = (bf16[128,512]{1,0:T(8,128)(2,1)S(1)}, bf16[128,512]{1,0:T(8,128)(2,1)S(1)}, u32[]{:S(2)}, u32[]{:S(2)}) collective-permute-start(bf16[128,512]{1,0:T(8,128)(2,1)S(1)} %pad_maximum_fusion.2), channel_id=1, source_target_pairs={{0,2},{1,3},{2,4},{3,5},{4,6},{5,7},{6,0},{7,1},{8,10},{9,11},{10,... | collective-permute-start | bytes 393224 | tf_op jit(solution)/shard_map/ppermute | solution.py:30
  202.8 2.7 %collective-permute-done.25 = bf16[128,512]{1,0:T(8,128)(2,1)S(1)} collective-permute-done((bf16[128,512]{1,0:T(8,128)(2,1)S(1)}, bf16[128,512]{1,0:T(8,128)(2,1)S(1)}, u32[]{:S(2)}, u32[]{:S(2)}) %collective-permute-start.25) | collective-permute-done | bytes 131104 | tf_op jit(solution)/shard_map/ppermute | solution.py:30
  205.8 2.6 %collective-permute-done.24 = bf16[128,512]{1,0:T(8,128)(2,1)S(1)} collective-permute-done((bf16[128,512]{1,0:T(8,128)(2,1)S(1)}, bf16[128,512]{1,0:T(8,128)(2,1)S(1)}, u32[]{:S(2)}, u32[]{:S(2)}) %collective-permute-start.24) | collective-permute-done | bytes 131104 | tf_op jit(solution)/shard_map/ppermute | solution.py:30
  208.4 4.1 %collective-permute-done.27 = bf16[128,512]{1,0:T(8,128)(2,1)S(1)} collective-permute-done((bf16[128,512]{1,0:T(8,128)(2,1)S(1)}, bf16[128,512]{1,0:T(8,128)(2,1)S(1)}, u32[]{:S(2)}, u32[]{:S(2)}) %collective-permute-start.27) | collective-permute-done | bytes 131104 | tf_op jit(solution)/shard_map/ppermute | solution.py:30
  (89 shorter events, 20.0 us)
Async XLA Ops:
  23.3 66.8 %collective-permute-start.17 = (bf16[4096,384]{1,0:T(8,128)(2,1)}, bf16[4096,384]{1,0:T(8,128)(2,1)}, u32[]{:S(2)}, u32[]{:S(2)}) collective-permute-start(bf16[4096,384]{1,0:T(8,128)(2,1)} %bitcast.8.gate_a), channel_id=1, source_target_pairs={{0,8},{8,0},{1,9},{9,1},{2,10},{10,2},{3,11},{11,3},{4,12},{12,4},... | collective-permute-start | bytes 9437192 | tf_op jit(solution)/shard_map/ppermute | solution.py:20
  23.8 66.3 %collective-permute-start.18 = (bf16[4096,384]{1,0:T(8,128)(2,1)}, bf16[4096,384]{1,0:T(8,128)(2,1)}, u32[]{:S(2)}, u32[]{:S(2)}) collective-permute-start(bf16[4096,384]{1,0:T(8,128)(2,1)} %bitcast.9.up_a), channel_id=1, source_target_pairs={{0,8},{8,0},{1,9},{9,1},{2,10},{10,2},{3,11},{11,3},{4,12},{12,4},... | collective-permute-start | bytes 9437192 | tf_op jit(solution)/shard_map/ppermute | solution.py:20
  23.8 66.3 %collective-permute-start.19 = (bf16[384,4096]{1,0:T(8,128)(2,1)}, bf16[384,4096]{1,0:T(8,128)(2,1)}, u32[]{:S(2)}, u32[]{:S(2)}) collective-permute-start(bf16[384,4096]{1,0:T(8,128)(2,1)} %bitcast.10.down_a), channel_id=1, source_target_pairs={{0,8},{8,0},{1,9},{9,1},{2,10},{10,2},{3,11},{11,3},{4,12},{12,4},... | collective-permute-start | bytes 9437192 | tf_op jit(solution)/shard_map/ppermute | solution.py:20
  31.4 8.3 %collective-permute-start.1 = (bf16[64,512]{1,0:T(8,128)(2,1)S(1)}, bf16[64,512]{1,0:T(8,128)(2,1)S(1)}, u32[]{:S(2)}, u32[]{:S(2)}) collective-permute-start(bf16[64,512]{1,0:T(8,128)(2,1)S(1)} %get-tuple-element.43), channel_id=1, source_target_pairs={{0,1},{1,2},{2,3},{3,4},{4,5},{5,6},{6,7},{7,0},{8,9},{9,10},{10,1... | collective-permute-start | bytes 196616 | tf_op jit(solution)/shard_map/ppermute | solution.py:77
  33.4 6.3 %collective-permute-start.5 = (bf16[64,512]{1,0:T(8,128)(2,1)S(1)}, bf16[64,512]{1,0:T(8,128)(2,1)S(1)}, u32[]{:S(2)}, u32[]{:S(2)}) collective-permute-start(bf16[64,512]{1,0:T(8,128)(2,1)S(1)} %get-tuple-element.44), channel_id=1, source_target_pairs={{0,7},{1,0},{2,1},{3,2},{4,3},{5,4},{6,5},{7,6},{8,15},{9,8},{10,9... | collective-permute-start | bytes 196616 | tf_op jit(solution)/shard_map/ppermute | solution.py:78
  39.8 6.3 %collective-permute-start.2 = (bf16[128,512]{1,0:T(8,128)(2,1)S(1)}, bf16[128,512]{1,0:T(8,128)(2,1)S(1)}, u32[]{:S(2)}, u32[]{:S(2)}) collective-permute-start(bf16[128,512]{1,0:T(8,128)(2,1)S(1)} %pad_maximum_fusion), channel_id=1, source_target_pairs={{0,1},{1,2},{2,3},{3,4},{4,5},{5,6},{6,7},{7,0},{8,9},{9,10},{10,1... | collective-permute-start | bytes 393224 | tf_op jit(solution)/shard_map/ppermute | solution.py:86
  39.9 6.3 %collective-permute-start.6 = (bf16[128,512]{1,0:T(8,128)(2,1)S(1)}, bf16[128,512]{1,0:T(8,128)(2,1)S(1)}, u32[]{:S(2)}, u32[]{:S(2)}) collective-permute-start(bf16[128,512]{1,0:T(8,128)(2,1)S(1)} %pad_maximum_fusion.1), channel_id=1, source_target_pairs={{0,7},{1,0},{2,1},{3,2},{4,3},{5,4},{6,5},{7,6},{8,15},{9,8},{10,9... | collective-permute-start | bytes 393224 | tf_op jit(solution)/shard_map/ppermute | solution.py:87
  46.2 6.3 %collective-permute-start.3 = (bf16[128,512]{1,0:T(8,128)(2,1)S(1)}, bf16[128,512]{1,0:T(8,128)(2,1)S(1)}, u32[]{:S(2)}, u32[]{:S(2)}) collective-permute-start(bf16[128,512]{1,0:T(8,128)(2,1)S(1)} %add_convert_fusion.5), channel_id=1, source_target_pairs={{0,1},{1,2},{2,3},{3,4},{4,5},{5,6},{6,7},{7,0},{8,9},{9,10},{10,1... | collective-permute-start | bytes 393224 | tf_op jit(solution)/shard_map/ppermute | solution.py:86
  52.5 6.0 %collective-permute-start.7 = (bf16[128,512]{1,0:T(8,128)(2,1)S(1)}, bf16[128,512]{1,0:T(8,128)(2,1)S(1)}, u32[]{:S(2)}, u32[]{:S(2)}) collective-permute-start(bf16[128,512]{1,0:T(8,128)(2,1)S(1)} %get-tuple-element.40), channel_id=1, source_target_pairs={{0,7},{1,0},{2,1},{3,2},{4,3},{5,4},{6,5},{7,6},{8,15},{9,8},{10,9... | collective-permute-start | bytes 393224 | tf_op jit(solution)/shard_map/ppermute | solution.py:87
  53.3 6.4 %collective-permute-start.4 = (bf16[128,512]{1,0:T(8,128)(2,1)S(1)}, bf16[128,512]{1,0:T(8,128)(2,1)S(1)}, u32[]{:S(2)}, u32[]{:S(2)}) collective-permute-start(bf16[128,512]{1,0:T(8,128)(2,1)S(1)} %get-tuple-element.39), channel_id=1, source_target_pairs={{0,1},{1,2},{2,3},{3,4},{4,5},{5,6},{6,7},{7,0},{8,9},{9,10},{10,1... | collective-permute-start | bytes 393224 | tf_op jit(solution)/shard_map/ppermute | solution.py:86
  58.5 6.3 %collective-permute-start.8 = (bf16[128,512]{1,0:T(8,128)(2,1)S(1)}, bf16[128,512]{1,0:T(8,128)(2,1)S(1)}, u32[]{:S(2)}, u32[]{:S(2)}) collective-permute-start(bf16[128,512]{1,0:T(8,128)(2,1)S(1)} %add_convert_fusion.2), channel_id=1, source_target_pairs={{0,7},{1,0},{2,1},{3,2},{4,3},{5,4},{6,5},{7,6},{8,15},{9,8},{10,9... | collective-permute-start | bytes 393224 | tf_op jit(solution)/shard_map/ppermute | solution.py:87
  64.9 6.4 %collective-permute-start.12 = (bf16[128,512]{1,0:T(8,128)(2,1)S(1)}, bf16[128,512]{1,0:T(8,128)(2,1)S(1)}, u32[]{:S(2)}, u32[]{:S(2)}) collective-permute-start(bf16[128,512]{1,0:T(8,128)(2,1)S(1)} %add_convert_fusion.1.refs_0_), channel_id=1, source_target_pairs={{0,1},{1,2},{2,3},{3,4},{4,5},{5,6},{6,7},{7,0},{8,9},{9,10},{10,1... | collective-permute-start | bytes 393224 | tf_op jit(solution)/shard_map/ppermute | solution.py:39
  65.1 6.3 %collective-permute-start.9 = (bf16[128,512]{1,0:T(8,128)(2,1)S(1)}, bf16[128,512]{1,0:T(8,128)(2,1)S(1)}, u32[]{:S(2)}, u32[]{:S(2)}) collective-permute-start(bf16[128,512]{1,0:T(8,128)(2,1)S(1)} %add_convert_fusion.1.refs_0_), channel_id=1, source_target_pairs={{0,7},{1,0},{2,1},{3,2},{4,3},{5,4},{6,5},{7,6},{8,15},{9,8},{10,9... | collective-permute-start | bytes 393224 | tf_op jit(solution)/shard_map/ppermute | solution.py:40
  71.3 6.2 %collective-permute-start.13 = (bf16[128,512]{1,0:T(8,128)(2,1)S(1)}, bf16[128,512]{1,0:T(8,128)(2,1)S(1)}, u32[]{:S(2)}, u32[]{:S(2)}) collective-permute-start(bf16[128,512]{1,0:T(8,128)(2,1)S(1)} %collective-permute-done.12.refs_8_), channel_id=1, source_target_pairs={{0,1},{1,2},{2,3},{3,4},{4,5},{5,6},{6,7},{7,0},{8,9},{9,10},{10,1... | collective-permute-start | bytes 393224 | tf_op jit(solution)/shard_map/ppermute | solution.py:39
  71.4 7.5 %collective-permute-start.10 = (bf16[128,512]{1,0:T(8,128)(2,1)S(1)}, bf16[128,512]{1,0:T(8,128)(2,1)S(1)}, u32[]{:S(2)}, u32[]{:S(2)}) collective-permute-start(bf16[128,512]{1,0:T(8,128)(2,1)S(1)} %collective-permute-done.9.refs_1_), channel_id=1, source_target_pairs={{0,7},{1,0},{2,1},{3,2},{4,3},{5,4},{6,5},{7,6},{8,15},{9,8},{10,9... | collective-permute-start | bytes 393224 | tf_op jit(solution)/shard_map/ppermute | solution.py:40
  77.5 6.2 %collective-permute-start.14 = (bf16[128,512]{1,0:T(8,128)(2,1)S(1)}, bf16[128,512]{1,0:T(8,128)(2,1)S(1)}, u32[]{:S(2)}, u32[]{:S(2)}) collective-permute-start(bf16[128,512]{1,0:T(8,128)(2,1)S(1)} %collective-permute-done.13.refs_7_), channel_id=1, source_target_pairs={{0,1},{1,2},{2,3},{3,4},{4,5},{5,6},{6,7},{7,0},{8,9},{9,10},{10,1... | collective-permute-start | bytes 393224 | tf_op jit(solution)/shard_map/ppermute | solution.py:39
  190.4 8.8 %collective-permute-start.22 = (bf16[128,512]{1,0:T(8,128)(2,1)S(1)}, bf16[128,512]{1,0:T(8,128)(2,1)S(1)}, u32[]{:S(2)}, u32[]{:S(2)}) collective-permute-start(bf16[128,512]{1,0:T(8,128)(2,1)S(1)} %get-tuple-element.34), channel_id=1, source_target_pairs={{0,1},{1,2},{2,3},{3,4},{4,5},{5,6},{6,7},{7,0},{8,9},{9,10},{10,1... | collective-permute-start | bytes 393224 | tf_op jit(solution)/shard_map/ppermute | solution.py:30
  190.6 9.1 %collective-permute-start.23 = (bf16[64,512]{1,0:T(8,128)(2,1)S(1)}, bf16[64,512]{1,0:T(8,128)(2,1)S(1)}, u32[]{:S(2)}, u32[]{:S(2)}) collective-permute-start(bf16[64,512]{1,0:T(8,128)(2,1)S(1)} %get-tuple-element.35), channel_id=1, source_target_pairs={{0,2},{1,3},{2,4},{3,5},{4,6},{5,7},{6,0},{7,1},{8,10},{9,11},{10,... | collective-permute-start | bytes 196616 | tf_op jit(solution)/shard_map/ppermute | solution.py:30
  195.1 10.4 %collective-permute-start.26 = (bf16[64,512]{1,0:T(8,128)(2,1)S(1)}, bf16[64,512]{1,0:T(8,128)(2,1)S(1)}, u32[]{:S(2)}, u32[]{:S(2)}) collective-permute-start(bf16[64,512]{1,0:T(8,128)(2,1)S(1)} %get-tuple-element.38), channel_id=1, source_target_pairs={{0,6},{1,7},{2,0},{3,1},{4,2},{5,3},{6,4},{7,5},{8,14},{9,15},{10,... | collective-permute-start | bytes 196616 | tf_op jit(solution)/shard_map/ppermute | solution.py:30
  195.1 10.6 %collective-permute-start.20 = (bf16[128,512]{1,0:T(8,128)(2,1)S(1)}, bf16[128,512]{1,0:T(8,128)(2,1)S(1)}, u32[]{:S(2)}, u32[]{:S(2)}) collective-permute-start(bf16[128,512]{1,0:T(8,128)(2,1)S(1)} %get-tuple-element.31), channel_id=1, source_target_pairs={{0,1},{1,2},{2,3},{3,4},{4,5},{5,6},{6,7},{7,0},{8,9},{9,10},{10,1... | collective-permute-start | bytes 393224 | tf_op jit(solution)/shard_map/ppermute | solution.py:30
  199.2 6.6 %collective-permute-start.21 = (bf16[128,512]{1,0:T(8,128)(2,1)S(1)}, bf16[128,512]{1,0:T(8,128)(2,1)S(1)}, u32[]{:S(2)}, u32[]{:S(2)}) collective-permute-start(bf16[128,512]{1,0:T(8,128)(2,1)S(1)} %get-tuple-element.32), channel_id=1, source_target_pairs={{0,7},{1,0},{2,1},{3,2},{4,3},{5,4},{6,5},{7,6},{8,15},{9,8},{10,9... | collective-permute-start | bytes 393224 | tf_op jit(solution)/shard_map/ppermute | solution.py:30
  199.2 6.4 %collective-permute-start.25 = (bf16[128,512]{1,0:T(8,128)(2,1)S(1)}, bf16[128,512]{1,0:T(8,128)(2,1)S(1)}, u32[]{:S(2)}, u32[]{:S(2)}) collective-permute-start(bf16[128,512]{1,0:T(8,128)(2,1)S(1)} %get-tuple-element.37), channel_id=1, source_target_pairs={{0,7},{1,0},{2,1},{3,2},{4,3},{5,4},{6,5},{7,6},{8,15},{9,8},{10,9... | collective-permute-start | bytes 393224 | tf_op jit(solution)/shard_map/ppermute | solution.py:30
  199.8 8.5 %collective-permute-start.24 = (bf16[128,512]{1,0:T(8,128)(2,1)S(1)}, bf16[128,512]{1,0:T(8,128)(2,1)S(1)}, u32[]{:S(2)}, u32[]{:S(2)}) collective-permute-start(bf16[128,512]{1,0:T(8,128)(2,1)S(1)} %pad_maximum_fusion.2), channel_id=1, source_target_pairs={{0,2},{1,3},{2,4},{3,5},{4,6},{5,7},{6,0},{7,1},{8,10},{9,11},{10,... | collective-permute-start | bytes 393224 | tf_op jit(solution)/shard_map/ppermute | solution.py:30
  205.6 6.8 %collective-permute-start.27 = (bf16[128,512]{1,0:T(8,128)(2,1)S(1)}, bf16[128,512]{1,0:T(8,128)(2,1)S(1)}, u32[]{:S(2)}, u32[]{:S(2)}) collective-permute-start(bf16[128,512]{1,0:T(8,128)(2,1)S(1)} %pad_maximum_fusion.3), channel_id=1, source_target_pairs={{0,6},{1,7},{2,0},{3,1},{4,2},{5,3},{6,4},{7,5},{8,14},{9,15},{10,... | collective-permute-start | bytes 393224 | tf_op jit(solution)/shard_map/ppermute | solution.py:30
  (11 other events, 283.9 us)

commit v8 on v7

--- a/solution.py
+++ b/solution.py
@@ -126,8 +126,17 @@
 def attention_kernel(
     group, queries, own_kv, other_kv, out_proj_hbm, out, out_proj, proj_sem
 ):
-    proj_copy = pltpu.make_async_copy(out_proj_hbm, out_proj, proj_sem)
-    proj_copy.start()
+    rows = out_proj.shape[0] // PIECES
+    proj_copies = [
+        pltpu.make_async_copy(
+            out_proj_hbm.at[pl.ds(piece * rows, rows)],
+            out_proj.at[pl.ds(piece * rows, rows)],
+            proj_sem.at[piece],
+        )
+        for piece in range(PIECES)
+    ]
+    for copy in proj_copies:
+        copy.start()
     tokens, width = queries.shape
     heads = width // HD
     stacked = jnp.concatenate(
@@ -149,7 +158,8 @@
     attended = jnp.concatenate(
         [attended[head * tokens : (head + 1) * tokens] for head in range(heads)], axis=1
     )
-    proj_copy.wait()
+    for copy in proj_copies:
+        copy.wait()
     depth = out_proj.shape[1] // SLICE
     for offset in range(depth):
         start = pl.multiple_of(lax.rem(group[0] + offset, depth) * SLICE, SLICE)
@@ -168,7 +178,10 @@
         + [pl.BlockSpec(memory_space=pltpu.VMEM)] * 3
         + [pl.BlockSpec(memory_space=pl.ANY)],
         out_specs=pl.BlockSpec(memory_space=pltpu.VMEM),
-        scratch_shapes=[pltpu.VMEM(out_proj.shape, BF), pltpu.SemaphoreType.DMA],
+        scratch_shapes=[
+            pltpu.VMEM(out_proj.shape, BF),
+            pltpu.SemaphoreType.DMA((PIECES,)),
+        ],
         compiler_params=pltpu.CompilerParams(vmem_limit_bytes=32 * 2**20),
         name="attention",
     )(group, *in_vmem(queries, own_kv, other_kv), in_hbm(out_proj))
@@ -349,13 +362,6 @@
 
     other_parts = tuple(swap_cores(part[0]) for part in (gate_proj, up_proj, down_proj))
 
-    group = group_index.astype(jnp.int32).reshape(1)
-    attn_share = sum_long_ring(
-        attention_slices(group, queries, own_kv, other_kv, out_proj, depth), depth
-    )
-    mixed_local = (residual_in.astype(F32) + attn_share).astype(BF)
-    mixed_pieces = gather_ring(mixed_local, depth)
-
     capacity = 2 * tokens * TOP // (EXP_GROUP * depth)
     copies = plane // EXP_GROUP
     local_experts = jnp.arange(EXP_GROUP, dtype=jnp.int32) + group_index * EXP_GROUP
@@ -372,6 +378,15 @@
     weighted_select = selector * token_weight.T[:, None, :]
     weighted_select = jnp.repeat(weighted_select, copies, axis=0)
     weighted_select = weighted_select.reshape(-1, tokens).T
+    group = group_index.astype(jnp.int32).reshape(1)
+    slices = attention_slices(group, queries, own_kv, other_kv, out_proj, depth)
+    slices, selector, weighted_select = lax.optimization_barrier(
+        (slices, selector, weighted_select)
+    )
+    attn_share = sum_long_ring(slices, depth)
+    mixed_local = (residual_in.astype(F32) + attn_share).astype(BF)
+    mixed_pieces = gather_ring(mixed_local, depth)
+
     outgoing = dispatch_rows(
         group,
         selector.reshape(-1, tokens),

time: 214 us -> 214 us (level)
  blocking collectives: 109 us -> 90.5 us
  starting transfers between devices: 38 us -> 50.3 us
  waiting for transfers between devices: 44.4 us -> 50 us
    all_to_all x1 -> x0, blocking collectives: 22.4 us -> none  [gather_by_exchange(): return lax.all_to_all(spread, axes, split_axis=0, concat_axis=0, tiled=True)]
    all_to_all x0 -> x1, waiting for transfers between devices: none -> 14.6 us  [gather_by_exchange(): return lax.all_to_all(spread, axes, split_axis=0, concat_axis=0, tiled=True)]
    all_to_all x0 -> x1, starting transfers between devices: none -> 7.43 us  [gather_by_exchange(): return lax.all_to_all(spread, axes, split_axis=0, concat_axis=0, tiled=True)]
    ppermute x3, starting transfers between devices: 5.29 us -> 11.1 us  [sum_long_ring(): backward = lax.ppermute(backward, 'z', behind)]
    ppermute x3, waiting for transfers between devices: 9.07 us -> 4.43 us  [sum_long_ring(): forward = lax.ppermute(forward, 'z', ahead)]
    ppermute x1, waiting for transfers between devices: 2.31 us -> 0.01 us  [sum_long_ring(): forward = lax.ppermute(first, 'z', ahead)]
  transfers between devices with their start and end apart: 28 -> 29, of which waited for: 15 -> 15; matrix products, arithmetic and copies ran while one was open for 1% -> 1% of each run, Pallas kernels for 2% -> 2%
where the time goes in v8:
time: 214 us; the launch traced here: 213 us
  blocking collectives  90.5 us (42%)
  starting transfers between devices  50.3 us (24%)
  waiting for transfers between devices  50 us (23%)
  Pallas kernels  17.9 us (8%)
  other arithmetic  2.43 us (1%)
    all_to_all x1, blocking collectives, shards(): lax.all_to_all(outgoing, ('x', 'y'), split_axis=0, concat_axis=0, tiled=T...  45.7 us
    all_to_all x1, blocking collectives, shards(): lax.all_to_all(partial_out.reshape(arrived.shape), ('x', 'y'), split_axis...  44.8 us
    all_to_all x1, waiting for transfers between devices, gather_by_exchange(): return lax.all_to_all(spread, axes, split_axis=0, concat_axis=0, tiled=True)  14.6 us
    pallas_call x1, Pallas kernels, expert_partial(): pl.pallas_call(expert_kernel, out_shape=pltpu.VMEM((count, depth), BF), i...  12.4 us
    ppermute x8, starting transfers between devices, shift(): lax.ppermute(array, 'z', [(i, (i + hops) % depth) for i in range(depth)])  11.7 us
    ppermute x3, starting transfers between devices, sum_long_ring(): backward = lax.ppermute(backward, 'z', behind)  11.1 us
    ppermute x3, starting transfers between devices, gather_ring(): from_ahead.append(lax.ppermute(from_ahead[-1], 'z', behind))  9.69 us
    ppermute x3, waiting for transfers between devices, gather_ring(): from_behind.append(lax.ppermute(from_behind[-1], 'z', ahead))  9.52 us
  transfers between devices with their start and end apart: 29, of which 15 were waited for; matrix products, arithmetic and copies ran while one was open for 1% of the time, Pallas kernels for 2%

profile of v8, /device:TPU:6, one launch (start us, length us, event | category | flops | bytes accessed | tf_op | source)
XLA Modules:
  0.0 213.1 jit_solution(9729833676106868988)
XLA Ops:
  2.0 7.4 %all-to-all-start = ((bf16[16,128,256]{2,1,0:T(8,128)(2,1)}), bf16[16,128,256]{2,1,0:T(8,128)(2,1)S(1)}, u32[]{:S(2)}, u32[]{:S(2)}) async-start(bf16[16,128,256]{2,1,0:T(8,128)(2,1)} %broadcast_in_dim.21), calls=%async_computation | async-start | bytes 2097152 | tf_op jit(solution)/shard_map/all_to_all | solution.py:25
  10.0 14.6 %all-to-all-done = bf16[16,128,256]{2,1,0:T(8,128)(2,1)S(1)} async-done(((bf16[16,128,256]{2,1,0:T(8,128)(2,1)}), bf16[16,128,256]{2,1,0:T(8,128)(2,1)S(1)}, u32[]{:S(2)}, u32[]{:S(2)}) %all-to-all-start) | async-done | bytes 1048608 | tf_op jit(solution)/shard_map/all_to_all | solution.py:25
  27.3 3.9 %attention.1 = bf16[128,4096]{1,0:T(8,128)(2,1)S(1)} custom-call(s32[1]{0:T(128)} %bitcast.group, bf16[128,256]{1,0:T(8,128)(2,1)S(1)} %copy-done, bf16[2048,256]{1,0:T(8,128)(2,1)S(1)} %bitcast.23, bf16[2048,256]{1,0:T(8,128)(2,1)S(1)} %collective-permute-done.other_kv, bf16[256,4096]{1,0:T(8,128)(2,1)} %out_proj_hbm.1), custom_call_target="tpu_custom_call" | custom-call | tf_op jit(solution)/shard_map/attention/pallas_call | solution.py:174
  31.3 5.9 %collective-permute-start.5 = (bf16[64,512]{1,0:T(8,128)(2,1)S(1)}, bf16[64,512]{1,0:T(8,128)(2,1)S(1)}, u32[]{:S(2)}, u32[]{:S(2)}) collective-permute-start(bf16[64,512]{1,0:T(8,128)(2,1)S(1)} %get-tuple-element.41), channel_id=1, source_target_pairs={{0,7},{1,0},{2,1},{3,2},{4,3},{5,4},{6,5},{7,6},{8,15},{9,8},{10,9... | collective-permute-start | bytes 196616 | tf_op jit(solution)/shard_map/ppermute | solution.py:78
  39.1 3.6 %collective-permute-start.6 = (bf16[128,512]{1,0:T(8,128)(2,1)S(1)}, bf16[128,512]{1,0:T(8,128)(2,1)S(1)}, u32[]{:S(2)}, u32[]{:S(2)}) collective-permute-start(bf16[128,512]{1,0:T(8,128)(2,1)S(1)} %pad_maximum_fusion.1), channel_id=1, source_target_pairs={{0,7},{1,0},{2,1},{3,2},{4,3},{5,4},{6,5},{7,6},{8,15},{9,8},{10,9... | collective-permute-start | bytes 393224 | tf_op jit(solution)/shard_map/ppermute | solution.py:87
  42.9 2.4 %collective-permute-done.6 = bf16[128,512]{1,0:T(8,128)(2,1)S(1)} collective-permute-done((bf16[128,512]{1,0:T(8,128)(2,1)S(1)}, bf16[128,512]{1,0:T(8,128)(2,1)S(1)}, u32[]{:S(2)}, u32[]{:S(2)}) %collective-permute-start.6) | collective-permute-done | bytes 131104 | tf_op jit(solution)/shard_map/ppermute | solution.py:87
  45.4 3.7 %collective-permute-start.7 = (bf16[128,512]{1,0:T(8,128)(2,1)S(1)}, bf16[128,512]{1,0:T(8,128)(2,1)S(1)}, u32[]{:S(2)}, u32[]{:S(2)}) collective-permute-start(bf16[128,512]{1,0:T(8,128)(2,1)S(1)} %add_convert_fusion.3), channel_id=1, source_target_pairs={{0,7},{1,0},{2,1},{3,2},{4,3},{5,4},{6,5},{7,6},{8,15},{9,8},{10,9... | collective-permute-start | bytes 393224 | tf_op jit(solution)/shard_map/ppermute | solution.py:87
  49.2 2.4 %collective-permute-done.7 = bf16[128,512]{1,0:T(8,128)(2,1)S(1)} collective-permute-done((bf16[128,512]{1,0:T(8,128)(2,1)S(1)}, bf16[128,512]{1,0:T(8,128)(2,1)S(1)}, u32[]{:S(2)}, u32[]{:S(2)}) %collective-permute-start.7) | collective-permute-done | bytes 131104 | tf_op jit(solution)/shard_map/ppermute | solution.py:87
  51.6 3.7 %collective-permute-start.8 = (bf16[128,512]{1,0:T(8,128)(2,1)S(1)}, bf16[128,512]{1,0:T(8,128)(2,1)S(1)}, u32[]{:S(2)}, u32[]{:S(2)}) collective-permute-start(bf16[128,512]{1,0:T(8,128)(2,1)S(1)} %add_convert_fusion.2), channel_id=1, source_target_pairs={{0,7},{1,0},{2,1},{3,2},{4,3},{5,4},{6,5},{7,6},{8,15},{9,8},{10,9... | collective-permute-start | bytes 393224 | tf_op jit(solution)/shard_map/ppermute | solution.py:87
  57.9 4.4 %collective-permute-done.4 = bf16[128,512]{1,0:T(8,128)(2,1)S(1)} collective-permute-done((bf16[128,512]{1,0:T(8,128)(2,1)S(1)}, bf16[128,512]{1,0:T(8,128)(2,1)S(1)}, u32[]{:S(2)}, u32[]{:S(2)}) %collective-permute-start.4) | collective-permute-done | bytes 131104 | tf_op jit(solution)/shard_map/ppermute | solution.py:86
  62.7 3.2 %collective-permute-start.9 = (bf16[128,512]{1,0:T(8,128)(2,1)S(1)}, bf16[128,512]{1,0:T(8,128)(2,1)S(1)}, u32[]{:S(2)}, u32[]{:S(2)}) collective-permute-start(bf16[128,512]{1,0:T(8,128)(2,1)S(1)} %add_convert_fusion.1.refs_0_), channel_id=1, source_target_pairs={{0,7},{1,0},{2,1},{3,2},{4,3},{5,4},{6,5},{7,6},{8,15},{9,8},{10,9... | collective-permute-start | bytes 393224 | tf_op jit(solution)/shard_map/ppermute | solution.py:40
  65.9 3.6 %collective-permute-done.12.refs_8_ = bf16[128,512]{1,0:T(8,128)(2,1)S(1)} collective-permute-done((bf16[128,512]{1,0:T(8,128)(2,1)S(1)}, bf16[128,512]{1,0:T(8,128)(2,1)S(1)}, u32[]{:S(2)}, u32[]{:S(2)}) %collective-permute-start.12) | collective-permute-done | bytes 131104 | tf_op jit(solution)/shard_map/ppermute | solution.py:39
  69.5 3.2 %collective-permute-start.10 = (bf16[128,512]{1,0:T(8,128)(2,1)S(1)}, bf16[128,512]{1,0:T(8,128)(2,1)S(1)}, u32[]{:S(2)}, u32[]{:S(2)}) collective-permute-start(bf16[128,512]{1,0:T(8,128)(2,1)S(1)} %collective-permute-done.9.refs_1_), channel_id=1, source_target_pairs={{0,7},{1,0},{2,1},{3,2},{4,3},{5,4},{6,5},{7,6},{8,15},{9,8},{10,9... | collective-permute-start | bytes 393224 | tf_op jit(solution)/shard_map/ppermute | solution.py:40
  72.8 2.9 %collective-permute-done.13.refs_7_ = bf16[128,512]{1,0:T(8,128)(2,1)S(1)} collective-permute-done((bf16[128,512]{1,0:T(8,128)(2,1)S(1)}, bf16[128,512]{1,0:T(8,128)(2,1)S(1)}, u32[]{:S(2)}, u32[]{:S(2)}) %collective-permute-start.13) | collective-permute-done | bytes 131104 | tf_op jit(solution)/shard_map/ppermute | solution.py:39
  75.7 3.2 %collective-permute-start.11 = (bf16[128,512]{1,0:T(8,128)(2,1)S(1)}, bf16[128,512]{1,0:T(8,128)(2,1)S(1)}, u32[]{:S(2)}, u32[]{:S(2)}) collective-permute-start(bf16[128,512]{1,0:T(8,128)(2,1)S(1)} %collective-permute-done.10.refs_2_), channel_id=1, source_target_pairs={{0,7},{1,0},{2,1},{3,2},{4,3},{5,4},{6,5},{7,6},{8,15},{9,8},{10,9... | collective-permute-start | bytes 393224 | tf_op jit(solution)/shard_map/ppermute | solution.py:40
  78.9 2.9 %collective-permute-done.14.refs_6_ = bf16[128,512]{1,0:T(8,128)(2,1)S(1)} collective-permute-done((bf16[128,512]{1,0:T(8,128)(2,1)S(1)}, bf16[128,512]{1,0:T(8,128)(2,1)S(1)}, u32[]{:S(2)}, u32[]{:S(2)}) %collective-permute-start.14) | collective-permute-done | bytes 131104 | tf_op jit(solution)/shard_map/ppermute | solution.py:39
  81.9 3.3 %collective-permute-start.16 = (bf16[64,512]{1,0:T(8,128)(2,1)S(1)}, bf16[64,512]{1,0:T(8,128)(2,1)S(1)}, u32[]{:S(2)}, u32[]{:S(2)}) collective-permute-start(bf16[64,512]{1,0:T(8,128)(2,1)S(1)} %slice.91), channel_id=1, source_target_pairs={{0,7},{1,0},{2,1},{3,2},{4,3},{5,4},{6,5},{7,6},{8,15},{9,8},{10,9... | collective-permute-start | bytes 196616 | tf_op jit(solution)/shard_map/ppermute | solution.py:43
  88.4 45.7 %all_to_all.15 = bf16[16,32,4096]{2,1,0:T(8,128)(2,1)S(1)} all-to-all(bf16[16,32,4096]{2,1,0:T(8,128)(2,1)S(1)} %bitcast.18), channel_id=1, replica_groups=mesh['x'=4,'y'=4,'c'=2,'z'=8] {'x','y'}, dimensions={0} | all-to-all | bytes 8388608 | tf_op jit(solution)/shard_map/all_to_all | solution.py:403
  134.1 12.4 %expert_partial.1 = bf16[512,4096]{1,0:T(8,128)(2,1)S(1)} custom-call(bf16[512,4096]{1,0:T(8,128)(2,1)S(1)} %bitcast.20, bf16[4096,384]{1,0:T(8,128)(2,1)S(1)} %bitcast.28, bf16[4096,384]{1,0:T(8,128)(2,1)S(1)} %bitcast.30, bf16[384,4096]{1,0:T(8,128)(2,1)S(1)} %bitcast.32, bf16[4096,384]{1,0:T(8,128)(2,1)} %collective-permute-done.17.gate_b, ...), custom_call_target="tpu_custom_call" | custom-call | flops 9663676416 | bytes 27262976 | tf_op jit(solution)/shard_map/expert_partial/pallas_call | solution.py:312
  146.5 44.8 %all_to_all.16 = bf16[16,32,4096]{2,1,0:T(8,128)(2,1)S(1)} all-to-all(bf16[16,32,4096]{2,1,0:T(8,128)(2,1)S(1)} %bitcast.21), channel_id=1, replica_groups=mesh['x'=4,'y'=4,'c'=2,'z'=8] {'x','y'}, dimensions={0} | all-to-all | bytes 8388608 | tf_op jit(solution)/shard_map/all_to_all | solution.py:407
  192.1 3.9 %collective-permute-start.23 = (bf16[64,512]{1,0:T(8,128)(2,1)S(1)}, bf16[64,512]{1,0:T(8,128)(2,1)S(1)}, u32[]{:S(2)}, u32[]{:S(2)}) collective-permute-start(bf16[64,512]{1,0:T(8,128)(2,1)S(1)} %get-tuple-element.57), channel_id=1, source_target_pairs={{0,2},{1,3},{2,4},{3,5},{4,6},{5,7},{6,0},{7,1},{8,10},{9,11},{10,... | collective-permute-start | bytes 196616 | tf_op jit(solution)/shard_map/ppermute | solution.py:30
  202.0 2.7 %collective-permute-done.25 = bf16[128,512]{1,0:T(8,128)(2,1)S(1)} collective-permute-done((bf16[128,512]{1,0:T(8,128)(2,1)S(1)}, bf16[128,512]{1,0:T(8,128)(2,1)S(1)}, u32[]{:S(2)}, u32[]{:S(2)}) %collective-permute-start.25) | collective-permute-done | bytes 131104 | tf_op jit(solution)/shard_map/ppermute | solution.py:30
  206.7 2.4 %collective-permute-done.24 = bf16[128,512]{1,0:T(8,128)(2,1)S(1)} collective-permute-done((bf16[128,512]{1,0:T(8,128)(2,1)S(1)}, bf16[128,512]{1,0:T(8,128)(2,1)S(1)}, u32[]{:S(2)}, u32[]{:S(2)}) %collective-permute-start.24) | collective-permute-done | bytes 131104 | tf_op jit(solution)/shard_map/ppermute | solution.py:30
  209.1 3.2 %collective-permute-done.27 = bf16[128,512]{1,0:T(8,128)(2,1)S(1)} collective-permute-done((bf16[128,512]{1,0:T(8,128)(2,1)S(1)}, bf16[128,512]{1,0:T(8,128)(2,1)S(1)}, u32[]{:S(2)}, u32[]{:S(2)}) %collective-permute-start.27) | collective-permute-done | bytes 131104 | tf_op jit(solution)/shard_map/ppermute | solution.py:30
  (99 shorter events, 23.1 us)
Async XLA Ops:
  2.0 22.7 %all-to-all-start = ((bf16[16,128,256]{2,1,0:T(8,128)(2,1)}), bf16[16,128,256]{2,1,0:T(8,128)(2,1)S(1)}, u32[]{:S(2)}, u32[]{:S(2)}) async-start(bf16[16,128,256]{2,1,0:T(8,128)(2,1)} %broadcast_in_dim.21), calls=%async_computation | async-start | bytes 2097152 | tf_op jit(solution)/shard_map/all_to_all | solution.py:25
  9.4 79.0 %collective-permute-start.17 = (bf16[4096,384]{1,0:T(8,128)(2,1)}, bf16[4096,384]{1,0:T(8,128)(2,1)}, u32[]{:S(2)}, u32[]{:S(2)}) collective-permute-start(bf16[4096,384]{1,0:T(8,128)(2,1)} %bitcast.27), channel_id=1, source_target_pairs={{0,8},{8,0},{1,9},{9,1},{2,10},{10,2},{3,11},{11,3},{4,12},{12,4},... | collective-permute-start | bytes 9437192 | tf_op jit(solution)/shard_map/ppermute | solution.py:20
  9.4 79.0 %collective-permute-start.18 = (bf16[4096,384]{1,0:T(8,128)(2,1)}, bf16[4096,384]{1,0:T(8,128)(2,1)}, u32[]{:S(2)}, u32[]{:S(2)}) collective-permute-start(bf16[4096,384]{1,0:T(8,128)(2,1)} %bitcast.29), channel_id=1, source_target_pairs={{0,8},{8,0},{1,9},{9,1},{2,10},{10,2},{3,11},{11,3},{4,12},{12,4},... | collective-permute-start | bytes 9437192 | tf_op jit(solution)/shard_map/ppermute | solution.py:20
  9.9 78.5 %collective-permute-start.19 = (bf16[384,4096]{1,0:T(8,128)(2,1)}, bf16[384,4096]{1,0:T(8,128)(2,1)}, u32[]{:S(2)}, u32[]{:S(2)}) collective-permute-start(bf16[384,4096]{1,0:T(8,128)(2,1)} %bitcast.31), channel_id=1, source_target_pairs={{0,8},{8,0},{1,9},{9,1},{2,10},{10,2},{3,11},{11,3},{4,12},{12,4},... | collective-permute-start | bytes 9437192 | tf_op jit(solution)/shard_map/ppermute | solution.py:20
  31.3 7.8 %collective-permute-start.5 = (bf16[64,512]{1,0:T(8,128)(2,1)S(1)}, bf16[64,512]{1,0:T(8,128)(2,1)S(1)}, u32[]{:S(2)}, u32[]{:S(2)}) collective-permute-start(bf16[64,512]{1,0:T(8,128)(2,1)S(1)} %get-tuple-element.41), channel_id=1, source_target_pairs={{0,7},{1,0},{2,1},{3,2},{4,3},{5,4},{6,5},{7,6},{8,15},{9,8},{10,9... | collective-permute-start | bytes 196616 | tf_op jit(solution)/shard_map/ppermute | solution.py:78
  39.1 6.2 %collective-permute-start.6 = (bf16[128,512]{1,0:T(8,128)(2,1)S(1)}, bf16[128,512]{1,0:T(8,128)(2,1)S(1)}, u32[]{:S(2)}, u32[]{:S(2)}) collective-permute-start(bf16[128,512]{1,0:T(8,128)(2,1)S(1)} %pad_maximum_fusion.1), channel_id=1, source_target_pairs={{0,7},{1,0},{2,1},{3,2},{4,3},{5,4},{6,5},{7,6},{8,15},{9,8},{10,9... | collective-permute-start | bytes 393224 | tf_op jit(solution)/shard_map/ppermute | solution.py:87
  42.8 6.3 %collective-permute-start.2 = (bf16[128,512]{1,0:T(8,128)(2,1)S(1)}, bf16[128,512]{1,0:T(8,128)(2,1)S(1)}, u32[]{:S(2)}, u32[]{:S(2)}) collective-permute-start(bf16[128,512]{1,0:T(8,128)(2,1)S(1)} %pad_maximum_fusion), channel_id=1, source_target_pairs={{0,1},{1,2},{2,3},{3,4},{4,5},{5,6},{6,7},{7,0},{8,9},{9,10},{10,1... | collective-permute-start | bytes 393224 | tf_op jit(solution)/shard_map/ppermute | solution.py:86
  45.4 6.3 %collective-permute-start.7 = (bf16[128,512]{1,0:T(8,128)(2,1)S(1)}, bf16[128,512]{1,0:T(8,128)(2,1)S(1)}, u32[]{:S(2)}, u32[]{:S(2)}) collective-permute-start(bf16[128,512]{1,0:T(8,128)(2,1)S(1)} %add_convert_fusion.3), channel_id=1, source_target_pairs={{0,7},{1,0},{2,1},{3,2},{4,3},{5,4},{6,5},{7,6},{8,15},{9,8},{10,9... | collective-permute-start | bytes 393224 | tf_op jit(solution)/shard_map/ppermute | solution.py:87
  49.1 6.3 %collective-permute-start.3 = (bf16[128,512]{1,0:T(8,128)(2,1)S(1)}, bf16[128,512]{1,0:T(8,128)(2,1)S(1)}, u32[]{:S(2)}, u32[]{:S(2)}) collective-permute-start(bf16[128,512]{1,0:T(8,128)(2,1)S(1)} %add_convert_fusion.5), channel_id=1, source_target_pairs={{0,1},{1,2},{2,3},{3,4},{4,5},{5,6},{6,7},{7,0},{8,9},{9,10},{10,1... | collective-permute-start | bytes 393224 | tf_op jit(solution)/shard_map/ppermute | solution.py:86
  51.6 6.3 %collective-permute-start.8 = (bf16[128,512]{1,0:T(8,128)(2,1)S(1)}, bf16[128,512]{1,0:T(8,128)(2,1)S(1)}, u32[]{:S(2)}, u32[]{:S(2)}) collective-permute-start(bf16[128,512]{1,0:T(8,128)(2,1)S(1)} %add_convert_fusion.2), channel_id=1, source_target_pairs={{0,7},{1,0},{2,1},{3,2},{4,3},{5,4},{6,5},{7,6},{8,15},{9,8},{10,9... | collective-permute-start | bytes 393224 | tf_op jit(solution)/shard_map/ppermute | solution.py:87
  55.4 6.9 %collective-permute-start.4 = (bf16[128,512]{1,0:T(8,128)(2,1)S(1)}, bf16[128,512]{1,0:T(8,128)(2,1)S(1)}, u32[]{:S(2)}, u32[]{:S(2)}) collective-permute-start(bf16[128,512]{1,0:T(8,128)(2,1)S(1)} %add_convert_fusion.4), channel_id=1, source_target_pairs={{0,1},{1,2},{2,3},{3,4},{4,5},{5,6},{6,7},{7,0},{8,9},{9,10},{10,1... | collective-permute-start | bytes 393224 | tf_op jit(solution)/shard_map/ppermute | solution.py:86
  62.4 7.1 %collective-permute-start.12 = (bf16[128,512]{1,0:T(8,128)(2,1)S(1)}, bf16[128,512]{1,0:T(8,128)(2,1)S(1)}, u32[]{:S(2)}, u32[]{:S(2)}) collective-permute-start(bf16[128,512]{1,0:T(8,128)(2,1)S(1)} %add_convert_fusion.1.refs_0_), channel_id=1, source_target_pairs={{0,1},{1,2},{2,3},{3,4},{4,5},{5,6},{6,7},{7,0},{8,9},{9,10},{10,1... | collective-permute-start | bytes 393224 | tf_op jit(solution)/shard_map/ppermute | solution.py:39
  62.7 6.9 %collective-permute-start.9 = (bf16[128,512]{1,0:T(8,128)(2,1)S(1)}, bf16[128,512]{1,0:T(8,128)(2,1)S(1)}, u32[]{:S(2)}, u32[]{:S(2)}) collective-permute-start(bf16[128,512]{1,0:T(8,128)(2,1)S(1)} %add_convert_fusion.1.refs_0_), channel_id=1, source_target_pairs={{0,7},{1,0},{2,1},{3,2},{4,3},{5,4},{6,5},{7,6},{8,15},{9,8},{10,9... | collective-permute-start | bytes 393224 | tf_op jit(solution)/shard_map/ppermute | solution.py:40
  69.5 6.2 %collective-permute-start.13 = (bf16[128,512]{1,0:T(8,128)(2,1)S(1)}, bf16[128,512]{1,0:T(8,128)(2,1)S(1)}, u32[]{:S(2)}, u32[]{:S(2)}) collective-permute-start(bf16[128,512]{1,0:T(8,128)(2,1)S(1)} %collective-permute-done.12.refs_8_), channel_id=1, source_target_pairs={{0,1},{1,2},{2,3},{3,4},{4,5},{5,6},{6,7},{7,0},{8,9},{9,10},{10,1... | collective-permute-start | bytes 393224 | tf_op jit(solution)/shard_map/ppermute | solution.py:39
  69.5 6.2 %collective-permute-start.10 = (bf16[128,512]{1,0:T(8,128)(2,1)S(1)}, bf16[128,512]{1,0:T(8,128)(2,1)S(1)}, u32[]{:S(2)}, u32[]{:S(2)}) collective-permute-start(bf16[128,512]{1,0:T(8,128)(2,1)S(1)} %collective-permute-done.9.refs_1_), channel_id=1, source_target_pairs={{0,7},{1,0},{2,1},{3,2},{4,3},{5,4},{6,5},{7,6},{8,15},{9,8},{10,9... | collective-permute-start | bytes 393224 | tf_op jit(solution)/shard_map/ppermute | solution.py:40
  75.7 6.2 %collective-permute-start.14 = (bf16[128,512]{1,0:T(8,128)(2,1)S(1)}, bf16[128,512]{1,0:T(8,128)(2,1)S(1)}, u32[]{:S(2)}, u32[]{:S(2)}) collective-permute-start(bf16[128,512]{1,0:T(8,128)(2,1)S(1)} %collective-permute-done.13.refs_7_), channel_id=1, source_target_pairs={{0,1},{1,2},{2,3},{3,4},{4,5},{5,6},{6,7},{7,0},{8,9},{9,10},{10,1... | collective-permute-start | bytes 393224 | tf_op jit(solution)/shard_map/ppermute | solution.py:39
  75.7 6.2 %collective-permute-start.11 = (bf16[128,512]{1,0:T(8,128)(2,1)S(1)}, bf16[128,512]{1,0:T(8,128)(2,1)S(1)}, u32[]{:S(2)}, u32[]{:S(2)}) collective-permute-start(bf16[128,512]{1,0:T(8,128)(2,1)S(1)} %collective-permute-done.10.refs_2_), channel_id=1, source_target_pairs={{0,7},{1,0},{2,1},{3,2},{4,3},{5,4},{6,5},{7,6},{8,15},{9,8},{10,9... | collective-permute-start | bytes 393224 | tf_op jit(solution)/shard_map/ppermute | solution.py:40
  192.0 7.7 %collective-permute-start.22 = (bf16[128,512]{1,0:T(8,128)(2,1)S(1)}, bf16[128,512]{1,0:T(8,128)(2,1)S(1)}, u32[]{:S(2)}, u32[]{:S(2)}) collective-permute-start(bf16[128,512]{1,0:T(8,128)(2,1)S(1)} %get-tuple-element.56), channel_id=1, source_target_pairs={{0,1},{1,2},{2,3},{3,4},{4,5},{5,6},{6,7},{7,0},{8,9},{9,10},{10,1... | collective-permute-start | bytes 393224 | tf_op jit(solution)/shard_map/ppermute | solution.py:30
  192.1 8.7 %collective-permute-start.23 = (bf16[64,512]{1,0:T(8,128)(2,1)S(1)}, bf16[64,512]{1,0:T(8,128)(2,1)S(1)}, u32[]{:S(2)}, u32[]{:S(2)}) collective-permute-start(bf16[64,512]{1,0:T(8,128)(2,1)S(1)} %get-tuple-element.57), channel_id=1, source_target_pairs={{0,2},{1,3},{2,4},{3,5},{4,6},{5,7},{6,0},{7,1},{8,10},{9,11},{10,... | collective-permute-start | bytes 196616 | tf_op jit(solution)/shard_map/ppermute | solution.py:30
  196.0 8.8 %collective-permute-start.26 = (bf16[64,512]{1,0:T(8,128)(2,1)S(1)}, bf16[64,512]{1,0:T(8,128)(2,1)S(1)}, u32[]{:S(2)}, u32[]{:S(2)}) collective-permute-start(bf16[64,512]{1,0:T(8,128)(2,1)S(1)} %get-tuple-element.60), channel_id=1, source_target_pairs={{0,6},{1,7},{2,0},{3,1},{4,2},{5,3},{6,4},{7,5},{8,14},{9,15},{10,... | collective-permute-start | bytes 196616 | tf_op jit(solution)/shard_map/ppermute | solution.py:30
  196.5 10.2 %collective-permute-start.20 = (bf16[128,512]{1,0:T(8,128)(2,1)S(1)}, bf16[128,512]{1,0:T(8,128)(2,1)S(1)}, u32[]{:S(2)}, u32[]{:S(2)}) collective-permute-start(bf16[128,512]{1,0:T(8,128)(2,1)S(1)} %get-tuple-element.53), channel_id=1, source_target_pairs={{0,1},{1,2},{2,3},{3,4},{4,5},{5,6},{6,7},{7,0},{8,9},{9,10},{10,1... | collective-permute-start | bytes 393224 | tf_op jit(solution)/shard_map/ppermute | solution.py:30
  197.8 8.9 %collective-permute-start.21 = (bf16[128,512]{1,0:T(8,128)(2,1)S(1)}, bf16[128,512]{1,0:T(8,128)(2,1)S(1)}, u32[]{:S(2)}, u32[]{:S(2)}) collective-permute-start(bf16[128,512]{1,0:T(8,128)(2,1)S(1)} %get-tuple-element.54), channel_id=1, source_target_pairs={{0,7},{1,0},{2,1},{3,2},{4,3},{5,4},{6,5},{7,6},{8,15},{9,8},{10,9... | collective-permute-start | bytes 393224 | tf_op jit(solution)/shard_map/ppermute | solution.py:30
  200.9 8.2 %collective-permute-start.24 = (bf16[128,512]{1,0:T(8,128)(2,1)S(1)}, bf16[128,512]{1,0:T(8,128)(2,1)S(1)}, u32[]{:S(2)}, u32[]{:S(2)}) collective-permute-start(bf16[128,512]{1,0:T(8,128)(2,1)S(1)} %pad_maximum_fusion.2), channel_id=1, source_target_pairs={{0,2},{1,3},{2,4},{3,5},{4,6},{5,7},{6,0},{7,1},{8,10},{9,11},{10,... | collective-permute-start | bytes 393224 | tf_op jit(solution)/shard_map/ppermute | solution.py:30
  204.8 7.4 %collective-permute-start.27 = (bf16[128,512]{1,0:T(8,128)(2,1)S(1)}, bf16[128,512]{1,0:T(8,128)(2,1)S(1)}, u32[]{:S(2)}, u32[]{:S(2)}) collective-permute-start(bf16[128,512]{1,0:T(8,128)(2,1)S(1)} %pad_maximum_fusion.3), channel_id=1, source_target_pairs={{0,6},{1,7},{2,0},{3,1},{4,2},{5,3},{6,4},{7,5},{8,14},{9,15},{10,... | collective-permute-start | bytes 393224 | tf_op jit(solution)/shard_map/ppermute | solution.py:30
  (15 other events, 357.7 us)
